TPU v7x, 256 devices: a whole 4x4x8 slice. The times are simulated.
256 devices in a mesh: grp: 2 (over z_lo), dp: 32 (over z_hi, y, core), mp: 4 (over x).
Axes of the slice: x: 4, y: 4, z: 8 (z_hi: 4, z_lo: 2; z = z_hi * 2 + z_lo), core: 2. Of those that a mesh axis runs over, the one named last changes fastest.
Arguments:
- states: bfloat16 [2, 16384, 1024], P('grp', 'dp')
- w_in: bfloat16 [1024, 4096], P(('grp', 'dp'), 'mp'), may hold values from -0.1875 to 0.1875
- b_in: float32 [4096], P('mp'), may hold values from -3 to 3
- w_out: bfloat16 [4096, 1024], P('mp', ('grp', 'dp')), may hold values from -0.09375 to 0.09375
- b_out: float32 [1024], replicated, may hold values from -3 to 3
- ln_gain: float32 [1024], replicated, may hold values from 0.25 to 1.75
- ln_bias: float32 [1024], replicated, may hold values from -2 to 2
- lengths: int32 [4096], P('dp'), may hold values from 128 to 512, as said below
- neg_ids: int32 [256, 32], P('dp'), may hold values from 0 to 4095, as said below
- neg_count: int32 [256], P('dp'), may hold values from 8 to 32
- pos_ids: int32 [256], P('dp'), may hold values from 0 to 4095
Outputs:
- encoded: bfloat16 [2, 16384, 1024], P('grp', 'dp', 'mp')
- question_direction_derivative: float32 [256, 1024], P('dp', 'mp')
- query_loss: float32 [256], P('dp')
Inputs may be any that keep to these rules, and one draw needn't show every extreme that they name: `lengths`: each is 128, 256 or 512. `neg_ids`: for each query its 32 entries and its positive are distinct passage numbers; entries at or after the query's neg_count are ignored.
All inputs are finite; a program needn't handle non-finite values.
Results may differ from a plain program's by a relative error of at most 0.0054.
Values may be sent and summed in bfloat16 or wider, within the bound.
No kernel may reach another device: no remote copies, remote signals or barrier semaphores. Data moves between devices by JAX's collectives and lax.ppermute only.
A program may use at most 64 MiB of HBM per device.

v0:
```python
import jax
import jax.numpy as jnp
from jax import lax
from jax.sharding import PartitionSpec as P

WIN = 4
QLEN = 64


sharpness_divisor = 0.05
window_tokens = 128
eps_norm = 1e-05
eps_unit = 1e-06


def shifted(block, axis, distance):
    devices = range(lax.axis_size(axis))
    route = [(i - distance, i) for i in devices if i - distance in devices]
    return lax.ppermute(block, axis, route)


def body(states, w_in, b_in, w_out, b_out, ln_gain, ln_bias, lengths, neg_ids, neg_count, pos_ids):
    tokens = states[0]
    row_count, gathered_width = tokens.shape
    part_width = gathered_width // lax.axis_size("mp")
    feature_start = lax.axis_index("mp") * part_width
    gain_part = lax.dynamic_slice_in_dim(ln_gain, feature_start, part_width, 0)
    bias_part = lax.dynamic_slice_in_dim(ln_bias, feature_start, part_width, 0)
    pre = jnp.dot(
        tokens,
        lax.all_gather(w_in, ("grp", "dp"), axis=0, tiled=True),
        preferred_element_type=jnp.float32,
    )
    hidden = jax.nn.gelu(pre + b_in, approximate=False).astype(jnp.bfloat16)
    partial_terms = jnp.dot(
        hidden,
        lax.all_gather(w_out, ("grp", "dp"), axis=1, tiled=True),
        preferred_element_type=jnp.float32,
    )
    mixed_sum = lax.psum(partial_terms, "mp")
    summed = tokens.astype(jnp.float32) + mixed_sum + b_out
    center = jnp.mean(summed, axis=1, keepdims=True)
    spread = jnp.mean(jnp.square(summed - center), axis=1, keepdims=True)
    normed = (summed - center) * lax.rsqrt(spread + eps_norm)
    normed_part = lax.dynamic_slice_in_dim(normed, feature_start, part_width, 1)
    encoded_part = (normed_part * gain_part + bias_part).astype(jnp.bfloat16)
    encoded_f = encoded_part.astype(jnp.float32)
    pass_count = lengths.shape[0]
    windows = encoded_f.reshape(pass_count, WIN, part_width)
    live_mask = (jnp.arange(WIN)[None, :] * window_tokens < lengths[:, None]).astype(jnp.float32)
    passage_emb = (
        jnp.sum(windows * live_mask[:, :, None], axis=1) / jnp.sum(live_mask, axis=1, keepdims=True)
    ).astype(jnp.bfloat16)
    own_count = row_count // QLEN
    query_own = jnp.mean(encoded_f.reshape(own_count, QLEN, part_width), axis=1).astype(
        jnp.bfloat16
    )
    refresh_side = lax.axis_index("grp") == 1
    query_all, ids_all, count_all, pos_all = (
        lax.all_gather(query_own, "dp", axis=0, tiled=True),
        lax.all_gather(neg_ids, "dp", axis=0, tiled=True),
        lax.all_gather(neg_count, "dp", axis=0, tiled=True),
        lax.all_gather(pos_ids, "dp", axis=0, tiled=True),
    )
    arrived = shifted(query_all, "grp", 1)
    query_all = jnp.where(refresh_side, arrived, query_all)
    angle_similarity_scores = lax.dot_general(
        query_all, passage_emb, (((1,), (1,)), ((), ())), preferred_element_type=jnp.float32
    )
    query_sq = jnp.sum(jnp.square(query_all.astype(jnp.float32)), axis=1)
    passage_sq = jnp.sum(jnp.square(passage_emb.astype(jnp.float32)), axis=1)
    angle_similarity_scores, query_sq, passage_sq = lax.psum(
        (angle_similarity_scores, query_sq, passage_sq), "mp"
    )
    question_reciprocal_length = jnp.sqrt(query_sq / gathered_width + eps_unit)
    document_reciprocal_length = jnp.sqrt(passage_sq / gathered_width + eps_unit)
    sharpened_similarity_scores = angle_similarity_scores / (
        gathered_width
        * sharpness_divisor
        * question_reciprocal_length[:, None]
        * document_reciprocal_length[None, :]
    )
    query_total = ids_all.shape[0]
    offset = lax.axis_index("dp") * pass_count
    local_ids = ids_all - offset
    slot_ids = jnp.arange(ids_all.shape[1])
    usable = (
        (slot_ids[None, :] < count_all[:, None]) & (local_ids >= 0) & (local_ids < pass_count)
    ).astype(jnp.float32)
    rows_index = jnp.broadcast_to(jnp.arange(query_total)[:, None], ids_all.shape)
    members = (
        jnp.zeros((query_total, pass_count), jnp.float32)
        .at[rows_index, jnp.clip(local_ids, 0, pass_count - 1)]
        .add(usable)
    )
    matching_document = ((pos_all - offset)[:, None] == jnp.arange(pass_count)[None, :]).astype(
        jnp.float32
    )
    candidate_probabilities = jnp.exp(sharpened_similarity_scores) * (members + matching_document)
    length_one_vectors = (
        passage_emb.astype(jnp.float32)
        / (jnp.sqrt(jnp.float32(gathered_width)) * document_reciprocal_length)[:, None]
    )
    own_start = lax.axis_index("dp") * own_count
    line_aggregates, pos_score = lax.psum(
        (
            jnp.sum(candidate_probabilities, axis=1),
            jnp.sum(sharpened_similarity_scores * matching_document, axis=1),
        ),
        "dp",
    )
    attraction_sum = jnp.dot(
        candidate_probabilities / line_aggregates[:, None] - matching_document,
        length_one_vectors,
        precision=lax.Precision.HIGHEST,
        preferred_element_type=jnp.float32,
    )
    gradient_matrix = (
        lax.psum_scatter(attraction_sum, "dp", scatter_dimension=0, tiled=True) / sharpness_divisor
    )
    loss_all = jnp.log(line_aggregates) - pos_score
    loss_rows = lax.dynamic_slice_in_dim(loss_all, own_start, own_count, 0)
    handed = shifted((gradient_matrix, loss_rows), "grp", -1)
    question_direction_derivative = jnp.where(refresh_side, gradient_matrix, handed[0])
    query_loss = jnp.where(refresh_side, loss_rows, handed[1])
    return (encoded_part[None], question_direction_derivative, query_loss)


def solution(mesh):
    placed = (
        P("grp", "dp", None),
        P(("grp", "dp"), "mp"),
        P("mp"),
        P("mp", ("grp", "dp")),
        P(),
        P(),
        P(),
        P("dp"),
        P("dp", None),
        P("dp"),
        P("dp"),
    )
    return jax.shard_map(
        body,
        mesh=mesh,
        in_specs=placed,
        out_specs=(P("grp", "dp", "mp"), P("dp", "mp"), P("dp")),
        check_vma=False,
    )
```

profile of v0, /device:TPU:1, one launch (start us, length us, event | category | flops | bytes accessed | tf_op | source)
XLA Modules:
  0.0 582.3 jit_solution(8228991177301017083)
XLA Ops:
  7.2 0.7 all-gather.3.cloned.1.call-update
  7.9 0.7 all-gather.5.cloned.1.call-update
  8.7 1.3 dynamic-slice
  10.6 0.9 dynamic-update-slice
  11.5 0.8 dynamic-update-slice.1
  12.3 19.0 %all-reduce.2 = (s32[256]{0:T(256)S(1)}, s32[256]{0:T(256)S(1)}) all-reduce(s32[256]{0:T(256)S(1)} %dynamic-update-slice, s32[256]{0:T(256)S(1)} %dynamic-update-slice.1), channel_id=1, replica_groups=mesh['grp'=2,'dp'=32,'mp'=4] {'dp'}, use_global_device_ids=true, to_apply=%add | all-reduce | flops 512 | bytes 4096
  31.3 43.3 %all_gather.22 = s32[256,32]{1,0:T(8,128)S(1)} all-gather(s32[8,32]{1,0:T(8,128)} %param.19), channel_id=1, replica_groups=mesh['grp'=2,'dp'=32,'mp'=4] {'dp'}, dimensions={0}, use_global_device_ids=true | all-gather | bytes 33792 | tf_op jit(solution)/shard_map/all_gather | solution.py:61
  74.8 53.2 %all-gather.3.cloned.1.call-done = bf16[1024,1024]{1,0:T(8,128)(2,1)} async-done(((bf16[16,1024]{1,0:T(8,128)(2,1)}), bf16[1024,1024]{1,0:T(8,128)(2,1)}) %all-gather.3.cloned.1.call-update) | async-done | bytes 2097168 | tf_op jit(solution)/shard_map/all_gather | solution.py:31
  128.0 114.3 %all-gather.5.cloned.1.call-done = bf16[1024,1024]{0,1:T(8,128)(2,1)} async-done(((bf16[1024,16]{0,1:T(8,128)(2,1)}), bf16[1024,1024]{0,1:T(8,128)(2,1)}) %all-gather.5.cloned.1.call-update) | async-done | bytes 2097168 | tf_op jit(solution)/shard_map/all_gather | solution.py:37
  242.3 10.2 %fusion.12 = f32[512,1024]{1,0:T(8,128)} fusion(bf16[1024,1024]{0,1:T(8,128)(2,1)} %all-gather.5.cloned.1.call-done, bf16[1024,1024]{1,0:T(8,128)(2,1)} %all-gather.3.cloned.1.call-done, bf16[1,512,1024]{2,1,0:T(8,128)(2,1)} %param.11, f32[1024]{0:T(1024)} %param.13), kind=kOutput, calls=%fused_computation.24 | convolution fusion | flops 2182086656 | bytes 7344128 | tf_op jit(solution)/shard_map/dot_general | solution.py:35
  252.7 0.8 dynamic_slice.13
  253.4 0.8 dynamic_slice.14
  254.9 57.1 %scatter_fusion = f32[32768]{0:T(1024)S(1)} fusion(f32[32768]{0:T(1024)S(1)} %convert_bitcast_fusion, s32[8192]{0:T(1024)S(1)} %reshape.88, f32[8192]{0:T(1024)S(1)} %reshape.90), kind=kCustom, calls=%fused_computation | custom fusion | flops 8192 | bytes 131072
  312.3 2.3 all-reduce.8.cloned.1.call-done
  314.6 2.1 fusion.11
  316.8 0.5 multiply_reduce_fusion
  317.6 45.9 %all_gather.20 = bf16[256,256]{1,0:T(8,128)(2,1)S(1)} all-gather(bf16[8,256]{1,0:T(8,128)(2,1)S(1)} %multiply_convert_fusion), channel_id=1, replica_groups=mesh['grp'=2,'dp'=32,'mp'=4] {'dp'}, dimensions={0}, use_global_device_ids=true | all-gather | bytes 135168 | tf_op jit(solution)/shard_map/all_gather | solution.py:60
  363.5 2.4 collective-permute-start
  366.6 2.0 collective-permute-done
  368.6 0.8 fusion.60
  369.6 6.7 %all-reduce.4 = (f32[128]{0:T(128)S(1)}, f32[256]{0:T(256)S(1)}) all-reduce(f32[128]{0:T(128)S(1)} %get-tuple-element.13, f32[256]{0:T(256)S(1)} %multiply_reduce_fusion.2), channel_id=1, replica_groups=mesh['grp'=2,'dp'=32,'mp'=4] {'mp'}, use_global_device_ids=true, to_apply=%region_10.11 | all-reduce | flops 384 | bytes 3072 | tf_op jit(solution)/shard_map/psum | solution.py:72
  376.4 33.2 %all-reduce.10.cloned.1.call-done = f32[256,128]{1,0:T(8,128)} async-done(((f32[256,128]{1,0:T(8,128)}), f32[256,128]{1,0:T(8,128)}) %all-reduce.10.cloned.1.call-update) | async-done | bytes 131088 | tf_op jit(solution)/shard_map/psum | solution.py:72
  409.6 1.2 select_reduce_fusion
  410.7 72.4 %all-reduce.3 = (f32[256]{0:T(256)S(1)}, f32[256]{0:T(256)S(1)}) all-reduce(f32[256]{0:T(256)S(1)} %get-tuple-element.4, f32[256]{0:T(256)S(1)} %get-tuple-element.3), channel_id=1, replica_groups=mesh['grp'=2,'dp'=32,'mp'=4] {'dp'}, use_global_device_ids=true, to_apply=%region_13.14 | all-reduce | flops 512 | bytes 4096 | tf_op jit(solution)/shard_map/psum | solution.py:105
  483.1 2.1 fusion.50
  485.3 1.3 collective-permute-start.2
  486.6 82.8 %reduce-scatter.2.cloned.1.call-done = f32[8,256]{1,0:T(8,128)} async-done(((f32[256,256]{1,0:T(8,128)}), f32[8,256]{1,0:T(8,128)}) %reduce-scatter.2.cloned.1.call-update) | async-done | bytes 8208 | tf_op jit(solution)/shard_map/reduce_scatter | solution.py:119
  569.4 0.7 broadcast_multiply_fusion
  570.1 1.3 collective-permute-start.1
  571.4 0.6 broadcast_select_fusion.4
  572.0 2.5 collective-permute-done.1
  574.5 1.3 broadcast_select_fusion.3
  (52 shorter events, 2.5 us)
Async XLA Ops:
  7.2 120.8 %all-gather.3.cloned.1.call-start = ((), (), s32[]{:S(2)}) async-start(), calls=%async_computation.1 | async-start | bytes 2129920 | tf_op jit(solution)/shard_map/all_gather | solution.py:31
  7.9 234.4 %all-gather.5.cloned.1.call-start = ((), (), s32[]{:S(2)}) async-start(), calls=%async_computation.2 | async-start | bytes 2129920 | tf_op jit(solution)/shard_map/all_gather | solution.py:37
  8.6 306.0 %all-reduce.8.cloned.1.call-start = ((), (), s32[]{:S(2)}) async-start(), calls=%async_computation.3 | async-start | bytes 4194304 | tf_op jit(solution)/shard_map/psum | solution.py:40
  252.5 1.8 copy-start.6
  252.5 1.9 copy-start.5
  252.6 157.0 %all-reduce.10.cloned.1.call-start = ((), (), s32[]{:S(2)}) async-start(), calls=%async_computation.4 | async-start | bytes 262144 | tf_op jit(solution)/shard_map/psum | solution.py:72
  254.9 57.2 %copy-start.4 = (s32[128]{0:T(128)S(1)}, s32[128]{0:T(128)}, u32[]{:S(2)}) copy-start(s32[128]{0:T(128)} %param.18) | copy-start | bytes 1540
  254.9 59.7 %copy-start.1 = (bf16[1,512,1024]{2,1,0:T(8,128)(2,1)S(1)}, bf16[1,512,1024]{2,1,0:T(8,128)(2,1)}, u32[]{:S(2)}) copy-start(bf16[1,512,1024]{2,1,0:T(8,128)(2,1)} %param.11) | copy-start | bytes 3145732
  254.9 59.7 %copy-start.3 = (f32[1024]{0:T(1024)S(1)}, f32[1024]{0:T(1024)}, u32[]{:S(2)}) copy-start(f32[1024]{0:T(1024)} %param.15) | copy-start | bytes 12292
  314.6 2.2 copy-start
  317.5 167.7 %copy-start.2 = (bf16[512,256]{1,0:T(8,128)(2,1)}, bf16[512,256]{1,0:T(8,128)(2,1)S(1)}, u32[]{:S(2)}) copy-start(bf16[512,256]{1,0:T(8,128)(2,1)S(1)} %get-tuple-element.12) | copy-start | bytes 786436
  363.5 5.1 collective-permute-start
  369.5 199.9 %reduce-scatter.2.cloned.1.call-start = ((), (), s32[]{:S(2)}) async-start(), calls=%async_computation.5 | async-start | bytes 270336 | tf_op jit(solution)/shard_map/reduce_scatter | solution.py:119
  485.3 86.1 %collective-permute-start.2 = (f32[8]{0:T(128)S(1)}, f32[8]{0:T(128)S(1)}, u32[]{:S(2)}, u32[]{:S(2)}) collective-permute-start(f32[8]{0:T(128)S(1)} %dynamic_slice.15), channel_id=1, source_target_pairs={{128,0},{129,1},{130,2},{131,3},{132,4},{133,5},{134,6},{135,7},{1... | collective-permute-start | bytes 104 | tf_op jit(solution)/shard_map/ppermute | solution.py:19
  570.1 4.4 collective-permute-start.1
Sparse Core Ops, SparseCore 0:
  9.9 118.0 all-gather.2
  129.8 112.4 all-gather.4
  252.7 61.8 all-reduce.7
  369.6 39.9 all-reduce.9
  485.3 84.0 reduce-scatter.1
where the time goes:
time: 585 us; the launch traced here: 582 us
  waiting for transfers between devices  292 us (50%)
  blocking collectives  187 us (32%)
  other arithmetic  65.1 us (11%)
  between operations  14.7 us (3%)
  matrix products  13.1 us (2%)
    all_gather x1, waiting for transfers between devices, body(): lax.all_gather(w_out, ('grp', 'dp'), axis=1, tiled=True)  114 us
    reduce_scatter x1, waiting for transfers between devices, body(): lax.psum_scatter(attraction_sum, 'dp', scatter_dimension=0, tiled=True)  82.8 us
    psum x1, blocking collectives, body(): lax.psum((jnp.sum(candidate_probabilities, axis=1), jnp.sum(sharpened_sim...  72.4 us
    unnamed x5, other arithmetic  57.4 us
    all_gather x1, waiting for transfers between devices, body(): lax.all_gather(w_in, ('grp', 'dp'), axis=0, tiled=True)  53.2 us
    all_gather x1, blocking collectives, body(): lax.all_gather(query_own, 'dp', axis=0, tiled=True)  45.9 us
    all_gather x1, blocking collectives, body(): lax.all_gather(neg_ids, 'dp', axis=0, tiled=True)  43.3 us
    psum x1, waiting for transfers between devices, body(): lax.psum((angle_similarity_scores, query_sq, passage_sq), 'mp')  33.2 us
  transfers between devices with their start and end apart: 8, of which 7 were waited for; matrix products, arithmetic and copies ran while one was open for 11% of the time, Pallas kernels for 0%

commit v1 on v0

v1 whole, which is shorter than its diff:
```python
import functools

import jax
import jax.numpy as jnp
import numpy as np
from jax import lax
from jax.experimental import pallas as pl
from jax.experimental.pallas import tpu as pltpu
from jax.sharding import Mesh, PartitionSpec as P

WIN = 4
QLEN = 64
WINDOW_TOKENS = 128
SHARPNESS = 0.05
EPS_NORM = 1e-05
EPS_UNIT = 1e-06

N_GRP, N_ZH, N_Y, N_C, N_MP = 2, 4, 4, 2, 4
N_Z = N_GRP * N_ZH
BF = jnp.bfloat16
F32 = jnp.float32
VMEM = pl.BlockSpec(memory_space=pltpu.VMEM)
SMEM = pl.BlockSpec(memory_space=pltpu.SMEM)
ANY = pl.BlockSpec(memory_space=pl.ANY)
NT = (((1,), (1,)), ((), ()))


def params():
    return pltpu.CompilerParams(vmem_limit_bytes=40 * 1024 * 1024)


def cost(flops, size):
    return pl.CostEstimate(flops=flops, bytes_accessed=size, transcendentals=0)


def shift(block, axis, distance):
    n = lax.axis_size(axis)
    return lax.ppermute(block, axis, [(i, (i + distance) % n) for i in range(n)])


def shift_refresh(block, axis, distance):
    n = lax.axis_size(axis)
    route = [(n + i, n + (i + distance) % n) for i in range(n)]
    return lax.ppermute(block, ("grp", axis), route)


def spread(block, axes, n):
    filled = jnp.broadcast_to(block[None], (n,) + block.shape)
    return lax.all_to_all(filled, axes, 0, 0, tiled=True)


def assemble(place, sources, weights, sems):
    y, c = place[1], place[2]
    copies = []
    for other in range(N_C):
        core = c if other == 0 else 1 - c
        for k in range(N_Y):
            line = lax.rem(y - k + N_Y, N_Y)
            copies.append(
                pltpu.make_async_copy(
                    sources[other * N_Y + k],
                    weights.at[:, line * N_C + core],
                    sems.at[other * N_Y + k],
                )
            )
    for copy in copies:
        copy.start()
    for copy in copies:
        copy.wait()


def hidden_kernel(place, x_ref, b_ref, *rest):
    sources, (h_ref, weights, sems) = rest[:8], rest[8:]
    assemble(place, sources, weights, sems)
    depth = x_ref.shape[1]
    width = h_ref.shape[1]
    tile = 256
    for t in range(width // tile):
        cols = slice(t * tile, (t + 1) * tile)
        w = weights[:, :, :, cols].reshape(depth, tile)
        pre = jnp.dot(x_ref[...], w, preferred_element_type=F32) + b_ref[:, cols]
        h_ref[:, cols] = (0.5 * pre * (1.0 + lax.erf(pre * np.float32(0.5**0.5)))).astype(BF)


def partial_kernel(place, h_ref, *rest):
    sources, (own_ref, s1, s2, s3, weights, total, sems) = rest[:8], rest[8:]
    assemble(place, sources, weights, sems)
    m = place[3]
    width = weights.shape[-1]
    tile = 256
    planes = tile // 128
    for t in range(total.shape[1] // tile):
        w = weights[t * planes : (t + 1) * planes].reshape(tile, width)
        total[:, t * tile : (t + 1) * tile] = lax.dot_general(
            h_ref[...], w, NT, preferred_element_type=F32
        )
    rows = own_ref.shape[0]
    for k, out in ((0, own_ref), (1, s1), (2, s2), (3, s3)):
        j = lax.rem(m + k, N_MP)
        out[...] = total[pl.ds(pl.multiple_of(j * rows, rows), rows), :].astype(out.dtype)


def norm_kernel(place, own, r1, r2, r3, x_ref, b_out, gain, bias, lens, e0, e1, e2, e3, p_ref, q_ref, enc):
    m = place[3]
    rows, width = own.shape
    x = x_ref[pl.ds(pl.multiple_of(m * rows, rows), rows), :]
    summed = own[...] + r1[...].astype(F32) + r2[...].astype(F32) + r3[...].astype(F32)
    summed = x.astype(F32) + summed + b_out[...]
    center = jnp.mean(summed, axis=1, keepdims=True)
    off = summed - center
    spread_ = jnp.mean(off * off, axis=1, keepdims=True)
    coded = (off * lax.rsqrt(spread_ + EPS_NORM) * gain[...] + bias[...]).astype(BF)
    enc[...] = coded
    part = width // N_MP
    for k, out in ((0, e0), (1, e1), (2, e2), (3, e3)):
        j = lax.rem(m + k, N_MP)
        out[...] = enc[:, pl.ds(pl.multiple_of(j * part, part), part)]
    n_pass = p_ref.shape[0]
    lens_m = lens[pl.ds(pl.multiple_of(m * n_pass, n_pass), n_pass), :]
    row = lax.broadcasted_iota(jnp.int32, (n_pass, rows), 1)
    slab = lax.broadcasted_iota(jnp.int32, (n_pass, rows), 0)
    alive = (row // WIN == slab) & ((row % WIN) * WINDOW_TOKENS < lens_m)
    live = jnp.where(alive, 1.0, 0.0).astype(F32)
    count = jnp.sum(live, axis=1, keepdims=True)
    p_ref[...] = (jnp.dot(live.astype(BF), coded, preferred_element_type=F32) / count).astype(BF)
    n_q = q_ref.shape[0]
    rowq = lax.broadcasted_iota(jnp.int32, (16, rows), 1)
    slabq = lax.broadcasted_iota(jnp.int32, (16, rows), 0)
    pick = jnp.where(rowq // QLEN == slabq, 1.0, 0.0).astype(BF)
    qs = jnp.dot(pick, coded, preferred_element_type=F32) * (1.0 / QLEN)
    q_ref[...] = qs[:n_q].astype(BF)


def pieces(v):
    a = v.astype(BF)
    rest = v - a.astype(F32)
    b = rest.astype(BF)
    return a, b, (rest - b.astype(F32)).astype(BF)


def score_kernel(place, q_ref, ids, p0, p1, p2, p3, out):
    zh, y, c, m = place[0], place[1], place[2], place[3]
    blocks = (p0, p1, p2, p3)
    size, width = p0.shape
    n_q = q_ref.shape[0]
    each = size // N_ZH
    n_slots = 32
    q = q_ref[...]
    qf = q.astype(F32)
    a = jnp.sqrt(jnp.sum(qf * qf, axis=1, keepdims=True) / width + EPS_UNIT)
    ones = jnp.ones((16, width), BF)
    lane = lax.broadcasted_iota(jnp.int32, (1, size), 1)
    zh_of = lax.rem(zh - lane // each + N_ZH, N_ZH)
    neg = ids[:, :n_slots]
    count = ids[:, n_slots : n_slots + 1]
    pos = ids[:, n_slots + 1 : n_slots + 2]
    total = jnp.zeros((n_q, 1), F32)
    score_pos = jnp.zeros((n_q, 1), F32)
    grads = jnp.zeros((6 * n_q, width), F32)
    for k, block in enumerate(blocks):
        p = block[...]
        pf = p.astype(F32)
        sq = pf * pf
        hi = sq.astype(BF)
        lo = (sq - hi.astype(F32)).astype(BF)
        b2 = lax.dot_general(ones, hi, NT, preferred_element_type=F32)
        b2 = b2 + lax.dot_general(ones, lo, NT, preferred_element_type=F32)
        b = jnp.sqrt(b2[:1] / width + EPS_UNIT)
        dots = lax.dot_general(q, p, NT, preferred_element_type=F32)
        s = dots / (width * SHARPNESS * a * b)
        line = lax.rem(y - k + N_Y, N_Y)
        number = ((zh_of * N_Y + line) * N_C + c) * (each * N_MP) + m * each + lax.rem(lane, each)
        match = jnp.where(pos == number, 1.0, 0.0).astype(F32)
        cand = match
        for j in range(n_slots):
            hit = (neg[:, j : j + 1] == number) & (j < count)
            cand = cand + jnp.where(hit, 1.0, 0.0)
        w = jnp.exp(s) * cand
        total = total + jnp.sum(w, axis=1, keepdims=True)
        score_pos = score_pos + jnp.sum(s * match, axis=1, keepdims=True)
        unit = 1.0 / (np.float32(width**0.5) * b)
        coef = jnp.concatenate(pieces(w * unit) + pieces(match * unit), axis=0)
        grads = grads + jnp.dot(coef, p, preferred_element_type=F32)
    pull = grads[:n_q] + grads[n_q : 2 * n_q] + grads[2 * n_q : 3 * n_q]
    toward = grads[3 * n_q : 4 * n_q] + grads[4 * n_q : 5 * n_q] + grads[5 * n_q :]
    part = width // N_MP
    own = n_q // N_C
    half = part // 2
    stats = jnp.concatenate(
        [jnp.broadcast_to(total, (n_q, half)), jnp.broadcast_to(score_pos, (n_q, half))], axis=1
    )
    for g in range(N_GRP):
        for cc in range(N_C):
            rows = slice(cc * own, (cc + 1) * own)
            for mm in range(N_MP):
                cols = slice(mm * part, (mm + 1) * part)
                d = (g * N_C + cc) * N_MP + mm
                out[d, 0:own, :] = pull[rows, cols]
                out[d, own : 2 * own, :] = toward[rows, cols]
                out[d, 2 * own : 3 * own, :] = stats[rows]


def final_kernel(arrived, grad, loss):
    peers = arrived.shape[0] // N_GRP
    own, part = grad.shape
    acc = arrived[peers]
    for d in range(peers + 1, 2 * peers):
        acc = acc + arrived[d]
    total = acc[2 * own :, :1]
    score = acc[2 * own :, part // 2 : part // 2 + 1]
    grad[...] = (acc[:own] / total - acc[own : 2 * own]) / SHARPNESS
    loss[...] = jnp.broadcast_to(jnp.log(total) - score, loss.shape)


def body(states, w_in, b_in, w_out, b_out, ln_gain, ln_bias, lengths, neg_ids, neg_count, pos_ids):
    x = states[0]
    rows, width = x.shape
    hid = b_in.shape[0]
    shard = w_in.shape[0]
    place = jnp.stack([lax.axis_index(a) for a in ("zh", "y", "c", "mp")]).astype(jnp.int32)

    packed = jnp.concatenate([neg_ids, neg_count[:, None], pos_ids[:, None]], axis=1)
    other_packed = shift(packed, "c", 1)
    first = lax.axis_index("c") == 0
    ids = jnp.concatenate(
        [jnp.where(first, packed, other_packed), jnp.where(first, other_packed, packed)], axis=0
    )

    both = jnp.concatenate([w_in, w_out.T], axis=0)
    along_z = spread(both, ("grp", "zh"), N_Z)
    z_in, z_out = along_z[:, :shard], along_z[:, shard:]
    lines_in = [z_in] + [shift(z_in, "y", k) for k in (1, 2, 3)]
    lines_out = [z_out] + [shift(z_out, "y", k) for k in (1, 2, 3)]
    lines_in = lines_in + [shift(v, "c", 1) for v in lines_in]
    lines_out = lines_out + [shift(v, "c", 1) for v in lines_out]
    weight_scratch = [
        pltpu.VMEM((N_Z, N_Y * N_C, shard, hid), BF),
        pltpu.SemaphoreType.DMA((8,)),
    ]
    hidden = pl.pallas_call(
        hidden_kernel,
        out_shape=jax.ShapeDtypeStruct((rows, hid), BF),
        in_specs=[SMEM, VMEM, VMEM] + [ANY] * 8,
        out_specs=VMEM,
        scratch_shapes=weight_scratch,
        compiler_params=params(),
        cost_estimate=cost(2 * rows * width * hid * 3, 4 << 20),
        name="hidden",
    )(place, x, b_in[None], *lines_in)

    part_rows = rows // N_MP
    own, s1, s2, s3 = pl.pallas_call(
        partial_kernel,
        out_shape=[jax.ShapeDtypeStruct((part_rows, width), F32)]
        + [jax.ShapeDtypeStruct((part_rows, width), BF)] * 3,
        in_specs=[SMEM, VMEM] + [ANY] * 8,
        out_specs=[VMEM] * 4,
        scratch_shapes=[weight_scratch[0], pltpu.VMEM((rows, width), F32), weight_scratch[1]],
        compiler_params=params(),
        cost_estimate=cost(2 * rows * width * hid, 4 << 20),
        name="partial",
    )(place, hidden, *lines_out)
    r2, r1, r3 = shift(s2, "mp", 2), shift(s1, "mp", 1), shift(s3, "mp", 3)

    part = width // N_MP
    n_pass = part_rows // WIN
    n_own_q = part_rows // QLEN
    *enc, passages, queries = pl.pallas_call(
        norm_kernel,
        out_shape=[jax.ShapeDtypeStruct((part_rows, part), BF)] * 4
        + [
            jax.ShapeDtypeStruct((n_pass, width), BF),
            jax.ShapeDtypeStruct((n_own_q, width), BF),
        ],
        in_specs=[SMEM] + [VMEM] * 9,
        out_specs=[VMEM] * 6,
        scratch_shapes=[pltpu.VMEM((part_rows, width), BF)],
        compiler_params=params(),
        cost_estimate=cost(2 * part_rows * width * 64, 3 << 20),
        name="norm",
    )(place, own, r1, r2, r3, x, b_out[None], ln_gain[None], ln_bias[None], lengths[:, None])

    along_zh = jnp.concatenate(
        [passages] + [shift_refresh(passages, "zh", k) for k in (1, 2, 3)], axis=0
    )
    lines = [along_zh] + [shift_refresh(along_zh, "y", k) for k in (1, 2, 3)]
    arrived_q = spread(queries, ("grp", "c", "mp"), N_GRP * N_C * N_MP)
    q_all = arrived_q[: N_C * N_MP].reshape(N_C * N_MP * n_own_q, width)

    own_q = n_own_q * N_MP
    peers = N_GRP * N_C * N_MP
    shares = pl.pallas_call(
        score_kernel,
        out_shape=jax.ShapeDtypeStruct((peers, 3 * own_q, part), F32),
        in_specs=[SMEM] + [VMEM] * 6,
        out_specs=VMEM,
        compiler_params=params(),
        cost_estimate=cost(2 * 512 * width * 200, 3 << 20),
        name="score",
    )(place, q_all, ids, *lines)
    arrived = lax.all_to_all(shares, ("grp", "c", "mp"), 0, 0, tiled=True)
    grad, loss = pl.pallas_call(
        final_kernel,
        out_shape=[
            jax.ShapeDtypeStruct((own_q, part), F32),
            jax.ShapeDtypeStruct((own_q, 128), F32),
        ],
        in_specs=[VMEM],
        out_specs=[VMEM] * 2,
        compiler_params=params(),
        name="final",
    )(arrived)

    m = lax.axis_index("mp")
    placed = [enc[0]] + [shift(enc[k], "mp", k) for k in (1, 2, 3)]
    encoded = jnp.zeros((N_MP, part_rows, part), BF)
    for k in range(N_MP):
        encoded = lax.dynamic_update_slice_in_dim(encoded, placed[k][None], (m - k) % N_MP, 0)
    return encoded.reshape(1, rows, part), grad, loss[:, 0]


def solution(mesh):
    fine = Mesh(
        mesh.devices.reshape(N_GRP, N_ZH, N_Y, N_C, N_MP), ("grp", "zh", "y", "c", "mp")
    )
    dp = ("zh", "y", "c")
    placed = (
        P("grp", dp, None),
        P(("grp",) + dp, "mp"),
        P("mp"),
        P("mp", ("grp",) + dp),
        P(),
        P(),
        P(),
        P(dp),
        P(dp, None),
        P(dp),
        P(dp),
    )
    return jax.shard_map(
        body,
        mesh=fine,
        in_specs=placed,
        out_specs=(P("grp", dp, "mp"), P(dp, "mp"), P(dp)),
        check_vma=False,
    )
```

time: 585 us -> 137 us (0.23)
  waiting for transfers between devices: 292 us -> 20.2 us
  blocking collectives: 187 us -> 21.9 us
  starting transfers between devices: 5.13 us -> 76.2 us
  other arithmetic: 65.1 us -> 1.02 us
  between operations: 14.7 us -> 1.01 us
  matrix products: 13.1 us -> 0 us
  Pallas kernels: 0 us -> 10.4 us
    all_gather x2 -> x0, waiting for transfers between devices: 168 us -> none  [the longest x1 114 us: body(): lax.all_gather(w_out, ('grp', 'dp'), axis=1, tiled=True)]
    all_gather x2 -> x0, blocking collectives: 89.3 us -> none  [the longest x1 45.9 us: body(): lax.all_gather(query_own, 'dp', axis=0, tiled=True)]
    reduce_scatter x1 -> x0, waiting for transfers between devices: 82.8 us -> none  [body(): lax.psum_scatter(attraction_sum, 'dp', scatter_dimension=0, tiled=True)]
    psum x2 -> x0, blocking collectives: 79.1 us -> none  [the longest x1 72.4 us: body(): lax.psum((jnp.sum(candidate_probabilities, axis=1), jnp.sum(sharpened_sim...]
    unnamed x5 -> x0, other arithmetic: 57.4 us -> none
    all_to_all x0 -> x2, starting transfers between devices: none -> 36.8 us  [the longest x1 18.8 us: spread(): return lax.all_to_all(filled, axes, 0, 0, tiled=True)]
    psum x2 -> x0, waiting for transfers between devices: 35.5 us -> none  [the longest x1 33.2 us: body(): lax.psum((angle_similarity_scores, query_sq, passage_sq), 'mp')]
    ppermute x3 -> x27, starting transfers between devices: 4.93 us -> 39.5 us  [the longest x21 35.5 us: shift(): lax.ppermute(block, axis, [(i, (i + distance) % n) for i in range(n)])]
  transfers between devices with their start and end apart: 8 -> 29, of which waited for: 7 -> 6; matrix products, arithmetic and copies ran while one was open for 11% -> 1% of each run, Pallas kernels for 0% -> 5%
where the time goes in v1:
time: 137 us; the launch traced here: 136 us
  starting transfers between devices  76.2 us (56%)
  blocking collectives  21.9 us (16%)
  waiting for transfers between devices  20.2 us (15%)
  Pallas kernels  10.4 us (8%)
  local copies, waits for them, and re-layouts  5.68 us (4%)
    ppermute x21, starting transfers between devices, shift(): lax.ppermute(block, axis, [(i, (i + distance) % n) for i in range(n)])  35.5 us
    all_to_all x1, blocking collectives, spread(): return lax.all_to_all(filled, axes, 0, 0, tiled=True)  21.9 us
    all_to_all x1, starting transfers between devices, spread(): return lax.all_to_all(filled, axes, 0, 0, tiled=True)  18.8 us
    all_to_all x1, starting transfers between devices, body(): arrived = lax.all_to_all(shares, ('grp', 'c', 'mp'), 0, 0, tiled=True)  18 us
    ppermute x21, waiting for transfers between devices, shift(): lax.ppermute(block, axis, [(i, (i + distance) % n) for i in range(n)])  11.5 us
    all_to_all x1, waiting for transfers between devices, body(): arrived = lax.all_to_all(shares, ('grp', 'c', 'mp'), 0, 0, tiled=True)  8.75 us
    ppermute x6, starting transfers between devices, shift_refresh(): return lax.ppermute(block, ('grp', axis), route)  4.03 us
    unnamed x31, local copies, waits for them, and re-layouts  3.91 us
  transfers between devices with their start and end apart: 29, of which 6 were waited for; matrix products, arithmetic and copies ran while one was open for 1% of the time, Pallas kernels for 5%

profile of v1, /device:TPU:1, one launch (start us, length us, event | category | flops | bytes accessed | tf_op | source)
XLA Modules:
  0.0 136.5 jit_solution(13995468585626743910)
XLA Ops:
  0.6 0.8 pad_maximum_fusion
  1.5 21.9 %all_to_all.15 = bf16[8,32,1024]{2,1,0:T(8,128)(2,1)S(1)} all-to-all(bf16[8,32,1024]{2,1,0:T(8,128)(2,1)S(1)} %broadcast_in_dim.50), channel_id=1, replica_groups=mesh['grp'=2,'zh'=4,'y'=4,'c'=2,'mp'=4] {'grp','zh'}, dimensions={0} | all-to-all | bytes 1048576 | tf_op jit(solution)/shard_map/all_to_all | solution.py:49
  23.4 1.4 %collective-permute-start = (bf16[8,16,1024]{2,1,0:T(8,128)(2,1)S(1)}, bf16[8,16,1024]{2,1,0:T(8,128)(2,1)S(1)}, u32[]{:S(2)}, u32[]{:S(2)}) collective-permute-start(bf16[8,16,1024]{2,1,0:T(8,128)(2,1)S(1)} %get-tuple-element.28.rest_0_), channel_id=1, source_target_pairs={{0,8},{8,16},{16,24},{24,0},{1,9},{9,17},{17,25},{25,1},{2,10},{10... | collective-permute-start | bytes 786440 | tf_op jit(solution)/shard_map/ppermute | solution.py:38
  24.8 2.6 %collective-permute-start.1 = (bf16[8,16,1024]{2,1,0:T(8,128)(2,1)S(1)}, bf16[8,16,1024]{2,1,0:T(8,128)(2,1)S(1)}, u32[]{:S(2)}, u32[]{:S(2)}) collective-permute-start(bf16[8,16,1024]{2,1,0:T(8,128)(2,1)S(1)} %get-tuple-element.28.rest_0_), channel_id=1, source_target_pairs={{0,16},{8,24},{16,0},{24,8},{1,17},{9,25},{17,1},{25,9},{2,18},{10... | collective-permute-start | bytes 786440 | tf_op jit(solution)/shard_map/ppermute | solution.py:38
  27.4 1.1 collective-permute-start.2
  28.5 4.0 %collective-permute-start.3 = (bf16[8,16,1024]{2,1,0:T(8,128)(2,1)S(1)}, bf16[8,16,1024]{2,1,0:T(8,128)(2,1)S(1)}, u32[]{:S(2)}, u32[]{:S(2)}) collective-permute-start(bf16[8,16,1024]{2,1,0:T(8,128)(2,1)S(1)} %get-tuple-element.28.rest_0_), channel_id=1, source_target_pairs={{0,4},{4,0},{1,5},{5,1},{2,6},{6,2},{3,7},{7,3},{8,12},{12,8},{9,1... | collective-permute-start | bytes 786440 | tf_op jit(solution)/shard_map/ppermute | solution.py:38
  33.4 2.5 %collective-permute-done.1.rest_2_ = bf16[8,16,1024]{2,1,0:T(8,128)(2,1)S(1)} collective-permute-done((bf16[8,16,1024]{2,1,0:T(8,128)(2,1)S(1)}, bf16[8,16,1024]{2,1,0:T(8,128)(2,1)S(1)}, u32[]{:S(2)}, u32[]{:S(2)}) %collective-permute-start.1) | collective-permute-done | bytes 262176 | tf_op jit(solution)/shard_map/ppermute | solution.py:38
  36.0 9.7 %collective-permute-start.4 = (bf16[8,16,1024]{2,1,0:T(8,128)(2,1)S(1)}, bf16[8,16,1024]{2,1,0:T(8,128)(2,1)}, u32[]{:S(2)}, u32[]{:S(2)}) collective-permute-start(bf16[8,16,1024]{2,1,0:T(8,128)(2,1)S(1)} %collective-permute-done.rest_1_), channel_id=1, source_target_pairs={{0,4},{4,0},{1,5},{5,1},{2,6},{6,2},{3,7},{7,3},{8,12},{12,8},{9,1... | collective-permute-start | bytes 786440 | tf_op jit(solution)/shard_map/ppermute | solution.py:38
  45.7 0.7 copy-done.6
  46.4 1.3 collective-permute-done.7.rest_1_
  48.4 3.2 %collective-permute-start.10 = (bf16[8,16,1024]{2,1,0:T(8,128)(2,1)S(1)}, bf16[8,16,1024]{2,1,0:T(8,128)(2,1)S(1)}, u32[]{:S(2)}, u32[]{:S(2)}) collective-permute-start(bf16[8,16,1024]{2,1,0:T(8,128)(2,1)S(1)} %get-tuple-element.27.rest_0_), channel_id=1, source_target_pairs={{0,4},{4,0},{1,5},{5,1},{2,6},{6,2},{3,7},{7,3},{8,12},{12,8},{9,1... | collective-permute-start | bytes 786440 | tf_op jit(solution)/shard_map/ppermute | solution.py:38
  52.2 0.9 copy-done.7
  53.1 3.3 %hidden.1.h_ref = bf16[512,1024]{1,0:T(8,128)(2,1)S(1)} custom-call(s32[4]{0:T(128)S(1)} %pad_add_fusion.2.place, bf16[512,1024]{1,0:T(8,128)(2,1)S(1)} %bitcast.22, f32[1,1024]{1,0:T(1,128)S(1)} %bitcast.27, bf16[8,16,1024]{2,1,0:T(8,128)(2,1)S(1)} %get-tuple-element.28.rest_0_, bf16[8,16,1024]{2,1,0:T(8,128)(2,1)S(1)} %collective-permute-done.rest_1_, ...), custom_call_target="tpu_custom_call" | custom-call | flops 3221225472 | bytes 4194304 | tf_op jit(solution)/shard_map/hidden/pallas_call | solution.py:240
  56.5 0.9 copy-done.5
  57.4 2.2 %partial.1 = (f32[128,1024]{1,0:T(8,128)S(1)}, bf16[128,1024]{1,0:T(8,128)(2,1)S(1)}, bf16[128,1024]{1,0:T(8,128)(2,1)S(1)}, bf16[128,1024]{1,0:T(8,128)(2,1)S(1)}) custom-call(s32[4]{0:T(128)S(1)} %pad_add_fusion.2.place, bf16[512,1024]{1,0:T(8,128)(2,1)S(1)} %hidden.1.h_ref, bf16[8,16,1024]{2,1,0:T(8,128)(2,1)S(1)} %get-tuple-element.27.rest_0_, ...), custom_call_target="tpu_custom_call" | custom-call | flops 1073741824 | bytes 4194304 | tf_op jit(solution)/shard_map/partial/pallas_call | solution.py:252
  59.7 1.5 %collective-permute-start.14 = (bf16[128,1024]{1,0:T(8,128)(2,1)S(1)}, bf16[128,1024]{1,0:T(8,128)(2,1)S(1)}, u32[]{:S(2)}, u32[]{:S(2)}) collective-permute-start(bf16[128,1024]{1,0:T(8,128)(2,1)S(1)} %get-tuple-element.16), channel_id=1, source_target_pairs={{0,1},{1,2},{2,3},{3,0},{4,5},{5,6},{6,7},{7,4},{8,9},{9,10},{10,1... | collective-permute-start | bytes 786440 | tf_op jit(solution)/shard_map/ppermute | solution.py:38
  61.2 2.5 %collective-permute-start.15 = (bf16[128,1024]{1,0:T(8,128)(2,1)S(1)}, bf16[128,1024]{1,0:T(8,128)(2,1)S(1)}, u32[]{:S(2)}, u32[]{:S(2)}) collective-permute-start(bf16[128,1024]{1,0:T(8,128)(2,1)S(1)} %get-tuple-element.17), channel_id=1, source_target_pairs={{0,2},{1,3},{2,0},{3,1},{4,6},{5,7},{6,4},{7,5},{8,10},{9,11},{10,... | collective-permute-start | bytes 786440 | tf_op jit(solution)/shard_map/ppermute | solution.py:38
  63.6 1.2 collective-permute-start.16
  65.6 1.3 collective-permute-start.20
  67.7 0.9 collective-permute-done.14.r1
  68.6 6.6 %collective-permute-done.15.r2 = bf16[128,1024]{1,0:T(8,128)(2,1)S(1)} collective-permute-done((bf16[128,1024]{1,0:T(8,128)(2,1)S(1)}, bf16[128,1024]{1,0:T(8,128)(2,1)S(1)}, u32[]{:S(2)}, u32[]{:S(2)}) %collective-permute-start.15) | collective-permute-done | bytes 262176 | tf_op jit(solution)/shard_map/ppermute | solution.py:38
  75.3 1.1 norm.1
  79.1 18.8 %all-to-all-start.1 = ((bf16[16,2,1024]{2,1,0:T(2,128)(2,1)}), bf16[16,2,1024]{2,1,0:T(2,128)(2,1)S(1)}, u32[]{:S(2)}, u32[]{:S(2)}) async-start(bf16[16,2,1024]{2,1,0:T(2,128)(2,1)} %broadcast_in_dim.59), calls=%async_computation.1 | async-start | bytes 131072 | tf_op jit(solution)/shard_map/all_to_all | solution.py:49
  97.9 0.7 collective-permute-start.24
  98.6 0.7 collective-permute-start.25
  100.1 1.4 %collective-permute-start.17 = (bf16[128,256]{1,0:T(8,128)(2,1)S(1)}, bf16[128,256]{1,0:T(8,128)(2,1)S(1)}, u32[]{:S(2)}, u32[]{:S(2)}) collective-permute-start(bf16[128,256]{1,0:T(8,128)(2,1)S(1)} %get-tuple-element.20), channel_id=1, source_target_pairs={{0,1},{1,2},{2,3},{3,0},{4,5},{5,6},{6,7},{7,4},{8,9},{9,10},{10,1... | collective-permute-start | bytes 196616 | tf_op jit(solution)/shard_map/ppermute | solution.py:38
  101.5 2.4 %collective-permute-start.18 = (bf16[128,256]{1,0:T(8,128)(2,1)S(1)}, bf16[128,256]{1,0:T(8,128)(2,1)S(1)}, u32[]{:S(2)}, u32[]{:S(2)}) collective-permute-start(bf16[128,256]{1,0:T(8,128)(2,1)S(1)} %get-tuple-element.21), channel_id=1, source_target_pairs={{0,2},{1,3},{2,0},{3,1},{4,6},{5,7},{6,4},{7,5},{8,10},{9,11},{10,... | collective-permute-start | bytes 196616 | tf_op jit(solution)/shard_map/ppermute | solution.py:38
  103.9 1.3 collective-permute-start.19
  105.2 3.1 %score.1 = f32[16,24,256]{2,1,0:T(8,128)} custom-call(s32[4]{0:T(128)S(1)} %pad_add_fusion.2.place, bf16[16,1024]{1,0:T(8,128)(2,1)S(1)} %reshape.15.q_ref, s32[16,34]{1,0:T(8,128)S(1)} %pad_add_fusion.ids, bf16[128,1024]{1,0:T(8,128)(2,1)S(1)} %constant_dynamic-update-slice_fusion.p0, bf16[128,1024]{1,0:T(8,128)(2,1)S(1)} %collective-permute-done.24.p1, ...), custom_call_target="tpu_custom_call" | custom-call | flops 209715200 | bytes 3145728 | tf_op jit(solution)/shard_map/score/pallas_call | solution.py:292
  108.3 18.0 %all-to-all-start.2 = ((f32[16,24,256]{2,1,0:T(8,128)}), f32[16,24,256]{2,1,0:T(8,128)S(1)}, u32[]{:S(2)}, u32[]{:S(2)}) async-start(f32[16,24,256]{2,1,0:T(8,128)} %score.1), calls=%async_computation.2 | async-start | bytes 786432 | tf_op jit(solution)/shard_map/all_to_all | solution.py:301
  126.4 8.7 %all-to-all-done.2.arrived = f32[16,24,256]{2,1,0:T(8,128)S(1)} async-done(((f32[16,24,256]{2,1,0:T(8,128)}), f32[16,24,256]{2,1,0:T(8,128)S(1)}, u32[]{:S(2)}, u32[]{:S(2)}) %all-to-all-start.2) | async-done | bytes 393248 | tf_op jit(solution)/shard_map/all_to_all | solution.py:301
  135.2 0.7 final.1
  (83 shorter events, 8.3 us)
Async XLA Ops:
  1.5 50.7 %copy-start = (bf16[1,512,1024]{2,1,0:T(8,128)(2,1)S(1)}, bf16[1,512,1024]{2,1,0:T(8,128)(2,1)}, u32[]{:S(2)}) copy-start(bf16[1,512,1024]{2,1,0:T(8,128)(2,1)} %param.11) | copy-start | bytes 3145732
  23.4 9.5 %collective-permute-start = (bf16[8,16,1024]{2,1,0:T(8,128)(2,1)S(1)}, bf16[8,16,1024]{2,1,0:T(8,128)(2,1)S(1)}, u32[]{:S(2)}, u32[]{:S(2)}) collective-permute-start(bf16[8,16,1024]{2,1,0:T(8,128)(2,1)S(1)} %get-tuple-element.28.rest_0_), channel_id=1, source_target_pairs={{0,8},{8,16},{16,24},{24,0},{1,9},{9,17},{17,25},{25,1},{2,10},{10... | collective-permute-start | bytes 786440 | tf_op jit(solution)/shard_map/ppermute | solution.py:38
  24.8 11.1 %collective-permute-start.1 = (bf16[8,16,1024]{2,1,0:T(8,128)(2,1)S(1)}, bf16[8,16,1024]{2,1,0:T(8,128)(2,1)S(1)}, u32[]{:S(2)}, u32[]{:S(2)}) collective-permute-start(bf16[8,16,1024]{2,1,0:T(8,128)(2,1)S(1)} %get-tuple-element.28.rest_0_), channel_id=1, source_target_pairs={{0,16},{8,24},{16,0},{24,8},{1,17},{9,25},{17,1},{25,9},{2,18},{10... | collective-permute-start | bytes 786440 | tf_op jit(solution)/shard_map/ppermute | solution.py:38
  27.4 8.6 %collective-permute-start.2 = (bf16[8,16,1024]{2,1,0:T(8,128)(2,1)S(1)}, bf16[8,16,1024]{2,1,0:T(8,128)(2,1)S(1)}, u32[]{:S(2)}, u32[]{:S(2)}) collective-permute-start(bf16[8,16,1024]{2,1,0:T(8,128)(2,1)S(1)} %get-tuple-element.28.rest_0_), channel_id=1, source_target_pairs={{0,24},{8,0},{16,8},{24,16},{1,25},{9,1},{17,9},{25,17},{2,26},{10... | collective-permute-start | bytes 786440 | tf_op jit(solution)/shard_map/ppermute | solution.py:38
  28.5 17.2 %collective-permute-start.3 = (bf16[8,16,1024]{2,1,0:T(8,128)(2,1)S(1)}, bf16[8,16,1024]{2,1,0:T(8,128)(2,1)S(1)}, u32[]{:S(2)}, u32[]{:S(2)}) collective-permute-start(bf16[8,16,1024]{2,1,0:T(8,128)(2,1)S(1)} %get-tuple-element.28.rest_0_), channel_id=1, source_target_pairs={{0,4},{4,0},{1,5},{5,1},{2,6},{6,2},{3,7},{7,3},{8,12},{12,8},{9,1... | collective-permute-start | bytes 786440 | tf_op jit(solution)/shard_map/ppermute | solution.py:38
  32.5 15.2 %collective-permute-start.7 = (bf16[8,16,1024]{2,1,0:T(8,128)(2,1)S(1)}, bf16[8,16,1024]{2,1,0:T(8,128)(2,1)S(1)}, u32[]{:S(2)}, u32[]{:S(2)}) collective-permute-start(bf16[8,16,1024]{2,1,0:T(8,128)(2,1)S(1)} %get-tuple-element.27.rest_0_), channel_id=1, source_target_pairs={{0,8},{8,16},{16,24},{24,0},{1,9},{9,17},{17,25},{25,1},{2,10},{10... | collective-permute-start | bytes 786440 | tf_op jit(solution)/shard_map/ppermute | solution.py:38
  32.9 15.5 %collective-permute-start.8 = (bf16[8,16,1024]{2,1,0:T(8,128)(2,1)S(1)}, bf16[8,16,1024]{2,1,0:T(8,128)(2,1)S(1)}, u32[]{:S(2)}, u32[]{:S(2)}) collective-permute-start(bf16[8,16,1024]{2,1,0:T(8,128)(2,1)S(1)} %get-tuple-element.27.rest_0_), channel_id=1, source_target_pairs={{0,16},{8,24},{16,0},{24,8},{1,17},{9,25},{17,1},{25,9},{2,18},{10... | collective-permute-start | bytes 786440 | tf_op jit(solution)/shard_map/ppermute | solution.py:38
  35.9 15.7 %collective-permute-start.9 = (bf16[8,16,1024]{2,1,0:T(8,128)(2,1)S(1)}, bf16[8,16,1024]{2,1,0:T(8,128)(2,1)S(1)}, u32[]{:S(2)}, u32[]{:S(2)}) collective-permute-start(bf16[8,16,1024]{2,1,0:T(8,128)(2,1)S(1)} %get-tuple-element.27.rest_0_), channel_id=1, source_target_pairs={{0,24},{8,0},{16,8},{24,16},{1,25},{9,1},{17,9},{25,17},{2,26},{10... | collective-permute-start | bytes 786440 | tf_op jit(solution)/shard_map/ppermute | solution.py:38
  36.0 15.6 %collective-permute-start.4 = (bf16[8,16,1024]{2,1,0:T(8,128)(2,1)S(1)}, bf16[8,16,1024]{2,1,0:T(8,128)(2,1)}, u32[]{:S(2)}, u32[]{:S(2)}) collective-permute-start(bf16[8,16,1024]{2,1,0:T(8,128)(2,1)S(1)} %collective-permute-done.rest_1_), channel_id=1, source_target_pairs={{0,4},{4,0},{1,5},{5,1},{2,6},{6,2},{3,7},{7,3},{8,12},{12,8},{9,1... | collective-permute-start | bytes 786440 | tf_op jit(solution)/shard_map/ppermute | solution.py:38
  46.4 5.7 %collective-permute-start.5 = (bf16[8,16,1024]{2,1,0:T(8,128)(2,1)S(1)}, bf16[8,16,1024]{2,1,0:T(8,128)(2,1)}, u32[]{:S(2)}, u32[]{:S(2)}) collective-permute-start(bf16[8,16,1024]{2,1,0:T(8,128)(2,1)S(1)} %collective-permute-done.1.rest_2_), channel_id=1, source_target_pairs={{0,4},{4,0},{1,5},{5,1},{2,6},{6,2},{3,7},{7,3},{8,12},{12,8},{9,1... | collective-permute-start | bytes 786440 | tf_op jit(solution)/shard_map/ppermute | solution.py:38
  47.7 4.5 %collective-permute-start.6 = (bf16[8,16,1024]{2,1,0:T(8,128)(2,1)S(1)}, bf16[8,16,1024]{2,1,0:T(8,128)(2,1)}, u32[]{:S(2)}, u32[]{:S(2)}) collective-permute-start(bf16[8,16,1024]{2,1,0:T(8,128)(2,1)S(1)} %collective-permute-done.2.rest_3_), channel_id=1, source_target_pairs={{0,4},{4,0},{1,5},{5,1},{2,6},{6,2},{3,7},{7,3},{8,12},{12,8},{9,1... | collective-permute-start | bytes 786440 | tf_op jit(solution)/shard_map/ppermute | solution.py:38
  48.4 8.1 %collective-permute-start.10 = (bf16[8,16,1024]{2,1,0:T(8,128)(2,1)S(1)}, bf16[8,16,1024]{2,1,0:T(8,128)(2,1)S(1)}, u32[]{:S(2)}, u32[]{:S(2)}) collective-permute-start(bf16[8,16,1024]{2,1,0:T(8,128)(2,1)S(1)} %get-tuple-element.27.rest_0_), channel_id=1, source_target_pairs={{0,4},{4,0},{1,5},{5,1},{2,6},{6,2},{3,7},{7,3},{8,12},{12,8},{9,1... | collective-permute-start | bytes 786440 | tf_op jit(solution)/shard_map/ppermute | solution.py:38
  51.6 4.9 %collective-permute-start.11 = (bf16[8,16,1024]{2,1,0:T(8,128)(2,1)S(1)}, bf16[8,16,1024]{2,1,0:T(8,128)(2,1)S(1)}, u32[]{:S(2)}, u32[]{:S(2)}) collective-permute-start(bf16[8,16,1024]{2,1,0:T(8,128)(2,1)S(1)} %collective-permute-done.7.rest_1_), channel_id=1, source_target_pairs={{0,4},{4,0},{1,5},{5,1},{2,6},{6,2},{3,7},{7,3},{8,12},{12,8},{9,1... | collective-permute-start | bytes 786440 | tf_op jit(solution)/shard_map/ppermute | solution.py:38
  51.7 4.8 %collective-permute-start.12 = (bf16[8,16,1024]{2,1,0:T(8,128)(2,1)S(1)}, bf16[8,16,1024]{2,1,0:T(8,128)(2,1)S(1)}, u32[]{:S(2)}, u32[]{:S(2)}) collective-permute-start(bf16[8,16,1024]{2,1,0:T(8,128)(2,1)S(1)} %collective-permute-done.8.rest_2_), channel_id=1, source_target_pairs={{0,4},{4,0},{1,5},{5,1},{2,6},{6,2},{3,7},{7,3},{8,12},{12,8},{9,1... | collective-permute-start | bytes 786440 | tf_op jit(solution)/shard_map/ppermute | solution.py:38
  52.1 4.4 %collective-permute-start.13 = (bf16[8,16,1024]{2,1,0:T(8,128)(2,1)S(1)}, bf16[8,16,1024]{2,1,0:T(8,128)(2,1)S(1)}, u32[]{:S(2)}, u32[]{:S(2)}) collective-permute-start(bf16[8,16,1024]{2,1,0:T(8,128)(2,1)S(1)} %collective-permute-done.9.rest_3_), channel_id=1, source_target_pairs={{0,4},{4,0},{1,5},{5,1},{2,6},{6,2},{3,7},{7,3},{8,12},{12,8},{9,1... | collective-permute-start | bytes 786440 | tf_op jit(solution)/shard_map/ppermute | solution.py:38
  59.7 8.9 %collective-permute-start.14 = (bf16[128,1024]{1,0:T(8,128)(2,1)S(1)}, bf16[128,1024]{1,0:T(8,128)(2,1)S(1)}, u32[]{:S(2)}, u32[]{:S(2)}) collective-permute-start(bf16[128,1024]{1,0:T(8,128)(2,1)S(1)} %get-tuple-element.16), channel_id=1, source_target_pairs={{0,1},{1,2},{2,3},{3,0},{4,5},{5,6},{6,7},{7,4},{8,9},{9,10},{10,1... | collective-permute-start | bytes 786440 | tf_op jit(solution)/shard_map/ppermute | solution.py:38
  61.2 14.1 %collective-permute-start.15 = (bf16[128,1024]{1,0:T(8,128)(2,1)S(1)}, bf16[128,1024]{1,0:T(8,128)(2,1)S(1)}, u32[]{:S(2)}, u32[]{:S(2)}) collective-permute-start(bf16[128,1024]{1,0:T(8,128)(2,1)S(1)} %get-tuple-element.17), channel_id=1, source_target_pairs={{0,2},{1,3},{2,0},{3,1},{4,6},{5,7},{6,4},{7,5},{8,10},{9,11},{10,... | collective-permute-start | bytes 786440 | tf_op jit(solution)/shard_map/ppermute | solution.py:38
  63.6 11.6 %collective-permute-start.16 = (bf16[128,1024]{1,0:T(8,128)(2,1)S(1)}, bf16[128,1024]{1,0:T(8,128)(2,1)S(1)}, u32[]{:S(2)}, u32[]{:S(2)}) collective-permute-start(bf16[128,1024]{1,0:T(8,128)(2,1)S(1)} %get-tuple-element.18), channel_id=1, source_target_pairs={{0,3},{1,0},{2,1},{3,2},{4,7},{5,4},{6,5},{7,6},{8,11},{9,8},{10,9... | collective-permute-start | bytes 786440 | tf_op jit(solution)/shard_map/ppermute | solution.py:38
  65.6 34.4 %collective-permute-start.20 = (s32[8,34]{1,0:T(8,128)S(1)}, s32[8,34]{1,0:T(8,128)S(1)}, u32[]{:S(2)}, u32[]{:S(2)}) collective-permute-start(s32[8,34]{1,0:T(8,128)S(1)} %pad_add_fusion.1), channel_id=1, source_target_pairs={{0,4},{4,0},{1,5},{5,1},{2,6},{6,2},{3,7},{7,3},{8,12},{12,8},{9,1... | collective-permute-start | bytes 3272 | tf_op jit(solution)/shard_map/ppermute | solution.py:38
  67.7 7.6 %copy-start.3 = (f32[1024]{0:T(1024)S(1)}, f32[1024]{0:T(1024)}, u32[]{:S(2)}) copy-start(f32[1024]{0:T(1024)} %param.17) | copy-start | bytes 12292
  76.4 21.4 %collective-permute-start.21 = (bf16[32,1024]{1,0:T(8,128)(2,1)S(1)}, bf16[32,1024]{1,0:T(8,128)(2,1)S(1)}, u32[]{:S(2)}, u32[]{:S(2)}) collective-permute-start(bf16[32,1024]{1,0:T(8,128)(2,1)S(1)} %get-tuple-element.24), channel_id=1, source_target_pairs={{128,160},{160,192},{192,224},{224,128},{129,161},{161,193},{193,2... | collective-permute-start | bytes 196616 | tf_op jit(solution)/shard_map/ppermute | solution.py:44
  77.1 20.8 %collective-permute-start.22 = (bf16[32,1024]{1,0:T(8,128)(2,1)S(1)}, bf16[32,1024]{1,0:T(8,128)(2,1)S(1)}, u32[]{:S(2)}, u32[]{:S(2)}) collective-permute-start(bf16[32,1024]{1,0:T(8,128)(2,1)S(1)} %get-tuple-element.24), channel_id=1, source_target_pairs={{128,192},{160,224},{192,128},{224,160},{129,193},{161,225},{193,1... | collective-permute-start | bytes 196616 | tf_op jit(solution)/shard_map/ppermute | solution.py:44
  77.7 20.2 %collective-permute-start.23 = (bf16[32,1024]{1,0:T(8,128)(2,1)S(1)}, bf16[32,1024]{1,0:T(8,128)(2,1)S(1)}, u32[]{:S(2)}, u32[]{:S(2)}) collective-permute-start(bf16[32,1024]{1,0:T(8,128)(2,1)S(1)} %get-tuple-element.24), channel_id=1, source_target_pairs={{128,224},{160,128},{192,160},{224,192},{129,225},{161,129},{193,1... | collective-permute-start | bytes 196616 | tf_op jit(solution)/shard_map/ppermute | solution.py:44
  79.1 24.8 %all-to-all-start.1 = ((bf16[16,2,1024]{2,1,0:T(2,128)(2,1)}), bf16[16,2,1024]{2,1,0:T(2,128)(2,1)S(1)}, u32[]{:S(2)}, u32[]{:S(2)}) async-start(bf16[16,2,1024]{2,1,0:T(2,128)(2,1)} %broadcast_in_dim.59), calls=%async_computation.1 | async-start | bytes 131072 | tf_op jit(solution)/shard_map/all_to_all | solution.py:49
  97.9 6.0 %collective-permute-start.24 = (bf16[128,1024]{1,0:T(8,128)(2,1)S(1)}, bf16[128,1024]{1,0:T(8,128)(2,1)S(1)}, u32[]{:S(2)}, u32[]{:S(2)}) collective-permute-start(bf16[128,1024]{1,0:T(8,128)(2,1)S(1)} %constant_dynamic-update-slice_fusion.p0), channel_id=1, source_target_pairs={{128,136},{136,144},{144,152},{152,128},{129,137},{137,145},{145,1... | collective-permute-start | bytes 786440 | tf_op jit(solution)/shard_map/ppermute | solution.py:44
  98.6 6.6 %collective-permute-start.25 = (bf16[128,1024]{1,0:T(8,128)(2,1)S(1)}, bf16[128,1024]{1,0:T(8,128)(2,1)S(1)}, u32[]{:S(2)}, u32[]{:S(2)}) collective-permute-start(bf16[128,1024]{1,0:T(8,128)(2,1)S(1)} %constant_dynamic-update-slice_fusion.p0), channel_id=1, source_target_pairs={{128,144},{136,152},{144,128},{152,136},{129,145},{137,153},{145,1... | collective-permute-start | bytes 786440 | tf_op jit(solution)/shard_map/ppermute | solution.py:44
  99.3 5.9 %collective-permute-start.26 = (bf16[128,1024]{1,0:T(8,128)(2,1)S(1)}, bf16[128,1024]{1,0:T(8,128)(2,1)S(1)}, u32[]{:S(2)}, u32[]{:S(2)}) collective-permute-start(bf16[128,1024]{1,0:T(8,128)(2,1)S(1)} %constant_dynamic-update-slice_fusion.p0), channel_id=1, source_target_pairs={{128,152},{136,128},{144,136},{152,144},{129,153},{137,129},{145,1... | collective-permute-start | bytes 786440 | tf_op jit(solution)/shard_map/ppermute | solution.py:44
  100.1 26.2 %collective-permute-start.17 = (bf16[128,256]{1,0:T(8,128)(2,1)S(1)}, bf16[128,256]{1,0:T(8,128)(2,1)S(1)}, u32[]{:S(2)}, u32[]{:S(2)}) collective-permute-start(bf16[128,256]{1,0:T(8,128)(2,1)S(1)} %get-tuple-element.20), channel_id=1, source_target_pairs={{0,1},{1,2},{2,3},{3,0},{4,5},{5,6},{6,7},{7,4},{8,9},{9,10},{10,1... | collective-permute-start | bytes 196616 | tf_op jit(solution)/shard_map/ppermute | solution.py:38
  101.5 24.9 %collective-permute-start.18 = (bf16[128,256]{1,0:T(8,128)(2,1)S(1)}, bf16[128,256]{1,0:T(8,128)(2,1)S(1)}, u32[]{:S(2)}, u32[]{:S(2)}) collective-permute-start(bf16[128,256]{1,0:T(8,128)(2,1)S(1)} %get-tuple-element.21), channel_id=1, source_target_pairs={{0,2},{1,3},{2,0},{3,1},{4,6},{5,7},{6,4},{7,5},{8,10},{9,11},{10,... | collective-permute-start | bytes 196616 | tf_op jit(solution)/shard_map/ppermute | solution.py:38
  103.9 22.4 %collective-permute-start.19 = (bf16[128,256]{1,0:T(8,128)(2,1)S(1)}, bf16[128,256]{1,0:T(8,128)(2,1)S(1)}, u32[]{:S(2)}, u32[]{:S(2)}) collective-permute-start(bf16[128,256]{1,0:T(8,128)(2,1)S(1)} %get-tuple-element.22), channel_id=1, source_target_pairs={{0,3},{1,0},{2,1},{3,2},{4,7},{5,4},{6,5},{7,6},{8,11},{9,8},{10,9... | collective-permute-start | bytes 196616 | tf_op jit(solution)/shard_map/ppermute | solution.py:38
  108.3 26.9 %all-to-all-start.2 = ((f32[16,24,256]{2,1,0:T(8,128)}), f32[16,24,256]{2,1,0:T(8,128)S(1)}, u32[]{:S(2)}, u32[]{:S(2)}) async-start(f32[16,24,256]{2,1,0:T(8,128)} %score.1), calls=%async_computation.2 | async-start | bytes 786432 | tf_op jit(solution)/shard_map/all_to_all | solution.py:301
  126.4 10.1 %copy-start.9 = (bf16[4,128,256]{2,1,0:T(8,128)(2,1)}, bf16[4,128,256]{2,1,0:T(8,128)(2,1)S(1)}, u32[]{:S(2)}) copy-start(bf16[4,128,256]{2,1,0:T(8,128)(2,1)S(1)} %bitcast_dynamic-update-slice_fusion) | copy-start | bytes 786436
  (11 other events, 36.4 us)

commit v2 on v1

v2 whole, which is shorter than its diff:
```python
import jax
import jax.numpy as jnp
import numpy as np
from jax import lax
from jax.experimental import pallas as pl
from jax.experimental.pallas import tpu as pltpu
from jax.sharding import Mesh, PartitionSpec as P

WIN = 4
QLEN = 64
WINDOW_TOKENS = 128
SHARPNESS = 0.05
EPS_NORM = 1e-05
EPS_UNIT = 1e-06

N_GRP, N_ZH, N_Y, N_C, N_MP = 2, 4, 4, 2, 4
N_Z = N_GRP * N_ZH
BF = jnp.bfloat16
F32 = jnp.float32
VMEM = pl.BlockSpec(memory_space=pltpu.VMEM)
SMEM = pl.BlockSpec(memory_space=pltpu.SMEM)
ANY = pl.BlockSpec(memory_space=pl.ANY)
NT = (((1,), (1,)), ((), ()))
N_NEG = 32
DIGIT = 64


def params():
    return pltpu.CompilerParams(vmem_limit_bytes=40 * 1024 * 1024)


def cost(flops, size):
    return pl.CostEstimate(flops=flops, bytes_accessed=size, transcendentals=0)


def shift(block, axis, distance):
    n = lax.axis_size(axis)
    return lax.ppermute(block, axis, [(i, (i + distance) % n) for i in range(n)])


def shift_refresh(block, axis, distance):
    n = lax.axis_size(axis)
    route = [(n + i, n + (i + distance) % n) for i in range(n)]
    return lax.ppermute(block, ("grp", axis), route)


def spread(block, axes, n):
    filled = jnp.broadcast_to(block[None], (n,) + block.shape)
    return lax.all_to_all(filled, axes, 0, 0, tiled=True)


def ffn_kernel(place, x_ref, b_ref, *rest):
    firsts, seconds = rest[:8], rest[8:10]
    own_ref, s1, s2, s3, w1, w2, hidden, total, sems = rest[10:]
    y, c, m = place[1], place[2], place[3]
    hid = hidden.shape[1]
    half = seconds[0].shape[-1]
    early, late = [], []
    for other in range(N_C):
        core = c if other == 0 else 1 - c
        for k in range(N_Y):
            slot = lax.rem(y - k + N_Y, N_Y) * N_C + core
            first, second = firsts[other * N_Y + k], seconds[other]
            i = 3 * (other * N_Y + k)
            early.append(
                pltpu.make_async_copy(first.at[:, :, 0:hid], w1.at[:, slot], sems.at[i])
            )
            late.append(
                pltpu.make_async_copy(
                    first.at[:, :, hid : hid + half], w2.at[:, slot, :, 0:half], sems.at[i + 1]
                )
            )
            late.append(
                pltpu.make_async_copy(
                    second.at[:, k], w2.at[:, slot, :, half : 2 * half], sems.at[i + 2]
                )
            )
    for copy in early + late:
        copy.start()
    for copy in early:
        copy.wait()
    depth = x_ref.shape[1]
    tile = 256
    for t in range(hid // tile):
        cols = slice(t * tile, (t + 1) * tile)
        w = w1[:, :, :, cols].reshape(depth, tile)
        pre = jnp.dot(x_ref[...], w, preferred_element_type=F32) + b_ref[:, cols]
        hidden[:, cols] = (0.5 * pre * (1.0 + lax.erf(pre * np.float32(0.5**0.5)))).astype(BF)
    for copy in late:
        copy.wait()
    planes = tile // (w2.shape[1] * w2.shape[2])
    for t in range(total.shape[1] // tile):
        w = w2[t * planes : (t + 1) * planes].reshape(tile, hid)
        total[:, t * tile : (t + 1) * tile] = lax.dot_general(
            hidden[...], w, NT, preferred_element_type=F32
        )
    rows = own_ref.shape[0]
    for k, out in ((2, s2), (1, s1), (3, s3), (0, own_ref)):
        j = lax.rem(m + k, N_MP)
        out[...] = total[pl.ds(pl.multiple_of(j * rows, rows), rows), :].astype(out.dtype)


def norm_kernel(place, own, r1, r2, r3, x_ref, b_out, gain, bias, lens, lists, e0, e1, e2, e3, p_ref, q_ref, enc):
    m = place[3]
    rows, width = own.shape
    x = x_ref[pl.ds(pl.multiple_of(m * rows, rows), rows), :]
    summed = own[...] + r1[...].astype(F32) + r2[...].astype(F32) + r3[...].astype(F32)
    summed = x.astype(F32) + summed + b_out[...]
    center = jnp.mean(summed, axis=1, keepdims=True)
    off = summed - center
    spread_ = jnp.mean(off * off, axis=1, keepdims=True)
    coded = (off * lax.rsqrt(spread_ + EPS_NORM) * gain[...] + bias[...]).astype(BF)
    enc[...] = coded
    part = width // N_MP
    for k, out in ((0, e0), (1, e1), (2, e2), (3, e3)):
        j = lax.rem(m + k, N_MP)
        out[...] = enc[:, pl.ds(pl.multiple_of(j * part, part), part)]
    n_pass = p_ref.shape[0]
    lens_m = lens[pl.ds(pl.multiple_of(m * n_pass, n_pass), n_pass), :]
    row = lax.broadcasted_iota(jnp.int32, (n_pass, rows), 1)
    slab = lax.broadcasted_iota(jnp.int32, (n_pass, rows), 0)
    alive = (row // WIN == slab) & ((row % WIN) * WINDOW_TOKENS < lens_m)
    live = jnp.where(alive, 1.0, 0.0).astype(F32)
    count = jnp.sum(live, axis=1, keepdims=True)
    p_ref[...] = (jnp.dot(live.astype(BF), coded, preferred_element_type=F32) / count).astype(BF)
    n_q = q_ref.shape[0]
    rowq = lax.broadcasted_iota(jnp.int32, (16, rows), 1)
    slabq = lax.broadcasted_iota(jnp.int32, (16, rows), 0)
    pick = jnp.where(rowq // QLEN == slabq, 1.0, 0.0).astype(BF)
    qs = jnp.dot(pick, coded, preferred_element_type=F32) * (1.0 / QLEN)
    q_ref[:, :width] = qs[:n_q].astype(BF)
    q_ref[:, width:] = lists[...]


def pieces(v):
    a = v.astype(BF)
    rest = v - a.astype(F32)
    b = rest.astype(BF)
    return a, b, (rest - b.astype(F32)).astype(BF)


def score_kernel(place, q_ref, p0, p1, p2, p3, out):
    zh, y, c, m = place[0], place[1], place[2], place[3]
    size, width = p0.shape
    n_q = q_ref.shape[0]
    each = size // N_C
    q = q_ref[:, :width]
    lists = q_ref[:, width:].astype(F32)
    neg = lists[:, :N_NEG] * DIGIT + lists[:, N_NEG : 2 * N_NEG]
    count = lists[:, 2 * N_NEG : 2 * N_NEG + 1]
    pos = lists[:, 2 * N_NEG + 1 : 2 * N_NEG + 2] * DIGIT + lists[:, 2 * N_NEG + 2 : 2 * N_NEG + 3]
    slot = lax.broadcasted_iota(jnp.int32, neg.shape, 1).astype(F32)
    neg = jnp.where(slot < count, neg, -1.0)
    qf = q.astype(F32)
    a = jnp.sqrt(jnp.sum(qf * qf, axis=1, keepdims=True) / width + EPS_UNIT)
    p = jnp.concatenate([p0[...], p1[...], p2[...], p3[...]], axis=0)
    n_p = p.shape[0]
    pf = p.astype(F32)
    sq = pf * pf
    hi = sq.astype(BF)
    lo = (sq - hi.astype(F32)).astype(BF)
    ones = jnp.ones((16, width), BF)
    b2 = lax.dot_general(ones, hi, NT, preferred_element_type=F32)
    b2 = b2 + lax.dot_general(ones, lo, NT, preferred_element_type=F32)
    b = jnp.sqrt(b2[:1] / width + EPS_UNIT)
    dots = lax.dot_general(q, p, NT, preferred_element_type=F32)
    s = dots / (width * SHARPNESS * a * b)
    lane = lax.broadcasted_iota(jnp.int32, (1, n_p), 1)
    line = lax.rem(zh - lane // size + N_ZH, N_ZH)
    core = lax.rem(c + lax.rem(lane, size) // each, N_C)
    number = ((line * N_Y + y) * N_C + core) * (each * N_MP) + m * each + lax.rem(lane, each)
    number = number.astype(F32)
    match = jnp.where(pos == number, 1.0, 0.0).astype(F32)
    cand = jnp.zeros((n_q, n_p), F32)
    for j in range(N_NEG):
        cand = cand + jnp.where(neg[:, j : j + 1] == number, 1.0, 0.0)
    w = jnp.exp(s) * cand
    total = jnp.sum(w, axis=1, keepdims=True)
    score_pos = jnp.sum(s * match, axis=1, keepdims=True)
    unit = 1.0 / (np.float32(width**0.5) * b)
    coef = jnp.concatenate(pieces(w * unit) + pieces(match * unit), axis=0)
    grads = jnp.dot(coef, p, preferred_element_type=F32)
    pull = grads[:n_q] + grads[n_q : 2 * n_q] + grads[2 * n_q : 3 * n_q]
    toward = grads[3 * n_q : 4 * n_q] + grads[4 * n_q : 5 * n_q] + grads[5 * n_q :]
    part = width // N_MP
    own = n_q // N_Y
    wide = lax.broadcasted_iota(jnp.int32, (n_q, 128), 1)
    stats = jnp.where(wide < 64, total, score_pos)
    for g in range(N_GRP):
        for yy in range(N_Y):
            rows = slice(yy * own, (yy + 1) * own)
            for mm in range(N_MP):
                cols = slice(mm * part, (mm + 1) * part)
                d = (g * N_Y + yy) * N_MP + mm
                out[d, 0:own, 0:part] = pull[rows, cols]
                out[d, own : 2 * own, 0:part] = toward[rows, cols]
                out[d, 0:own, part:] = stats[rows]
                out[d, own : 2 * own, part:] = stats[rows]


def final_kernel(arrived, grad, loss):
    peers = arrived.shape[0] // N_GRP
    own, part = grad.shape
    acc = arrived[peers]
    for d in range(peers + 1, 2 * peers):
        acc = acc + arrived[d]
    others = acc[:own, part : part + 1]
    score = acc[:own, part + 64 : part + 65]
    total = others + jnp.exp(score)
    pull, toward = acc[:own, :part], acc[own:, :part]
    grad[...] = (pull / total - toward * (others / total)) / SHARPNESS
    column = jnp.log(total) - score
    diagonal = lax.broadcasted_iota(jnp.int32, (own, 128), 0) == lax.broadcasted_iota(
        jnp.int32, (own, 128), 1
    )
    row = jnp.sum(jnp.where(diagonal, column, 0.0), axis=0, keepdims=True)
    loss[...] = row[:, :own]


def body(states, w_in, b_in, w_out, b_out, ln_gain, ln_bias, lengths, neg_ids, neg_count, pos_ids):
    x = states[0]
    rows, width = x.shape
    hid = b_in.shape[0]
    half = hid // 2
    shard = w_in.shape[0]
    m = lax.axis_index("mp")
    place = jnp.stack([lax.axis_index(a) for a in ("zh", "y", "c", "mp")]).astype(jnp.int32)
    part_rows = rows // N_MP
    part = width // N_MP
    n_pass = part_rows // WIN
    n_own_q = part_rows // QLEN
    own_q = n_own_q * N_MP

    pos = pos_ids[:, None]
    lists = jnp.concatenate(
        [neg_ids // DIGIT, neg_ids % DIGIT, neg_count[:, None], pos // DIGIT, pos % DIGIT], axis=1
    ).astype(BF)
    lists = jnp.pad(lists, ((0, 0), (0, 128 - lists.shape[1])))
    lists = lax.dynamic_slice_in_dim(lists, m * n_own_q, n_own_q, 0)

    w_out_t = w_out.T
    first = jnp.concatenate([w_in, w_out_t[:, :half]], axis=1)
    second = w_out_t[:, half:]
    line = jnp.stack([second] + [shift(second, "y", k) for k in (1, 2, 3)])
    firsts = spread(first, ("grp", "zh"), N_Z)
    firsts = [firsts] + [shift(firsts, "y", k) for k in (1, 2, 3)]
    firsts = firsts + [shift(v, "c", 1) for v in firsts]
    seconds = spread(line, ("grp", "zh"), N_Z)
    seconds = [seconds, shift(seconds, "c", 1)]
    weights = pltpu.VMEM((N_Z, N_Y * N_C, shard, hid), BF)
    own, s1, s2, s3 = pl.pallas_call(
        ffn_kernel,
        out_shape=[jax.ShapeDtypeStruct((part_rows, width), F32)]
        + [jax.ShapeDtypeStruct((part_rows, width), BF)] * 3,
        in_specs=[SMEM, VMEM, VMEM] + [ANY] * 10,
        out_specs=[VMEM] * 4,
        scratch_shapes=[
            weights,
            weights,
            pltpu.VMEM((rows, hid), BF),
            pltpu.VMEM((rows, width), F32),
            pltpu.SemaphoreType.DMA((24,)),
        ],
        compiler_params=params(),
        cost_estimate=cost(4 * rows * width * hid, 8 << 20),
        name="ffn",
    )(place, x, b_in[None], *firsts, *seconds)
    r2, r1, r3 = shift(s2, "mp", 2), shift(s1, "mp", 1), shift(s3, "mp", 3)

    *enc, passages, queries = pl.pallas_call(
        norm_kernel,
        out_shape=[jax.ShapeDtypeStruct((part_rows, part), BF)] * 4
        + [
            jax.ShapeDtypeStruct((n_pass, width), BF),
            jax.ShapeDtypeStruct((n_own_q, width + 128), BF),
        ],
        in_specs=[SMEM] + [VMEM] * 10,
        out_specs=[VMEM] * 6,
        scratch_shapes=[pltpu.VMEM((part_rows, width), BF)],
        compiler_params=params(),
        cost_estimate=cost(2 * part_rows * width * 64, 3 << 20),
        name="norm",
    )(place, own, r1, r2, r3, x, b_out[None], ln_gain[None], ln_bias[None], lengths[:, None], lists)

    peers = N_GRP * N_Y * N_MP
    arrived_q = spread(queries, ("grp", "y", "mp"), peers)
    q_all = arrived_q[: peers // N_GRP].reshape(own_q * N_Y, width + 128)
    pair = jnp.concatenate([passages, shift(passages, "c", 1)], axis=0)
    lines = [pair] + [shift_refresh(pair, "zh", k) for k in (1, 2, 3)]
    shares = pl.pallas_call(
        score_kernel,
        out_shape=jax.ShapeDtypeStruct((peers, 2 * own_q, part + 128), F32),
        in_specs=[SMEM] + [VMEM] * 5,
        out_specs=VMEM,
        compiler_params=params(),
        cost_estimate=cost(2 * 256 * width * 300, 3 << 20),
        name="score",
    )(place, q_all, *lines)
    enc, shares = lax.optimization_barrier((enc, shares))
    arrived = lax.all_to_all(shares, ("grp", "y", "mp"), 0, 0, tiled=True)
    grad, loss = pl.pallas_call(
        final_kernel,
        out_shape=[
            jax.ShapeDtypeStruct((own_q, part), F32),
            jax.ShapeDtypeStruct((1, own_q), F32),
        ],
        in_specs=[VMEM],
        out_specs=[VMEM] * 2,
        compiler_params=params(),
        name="final",
    )(arrived)

    placed = [enc[0]] + [shift(enc[k], "mp", k) for k in (1, 2, 3)]
    encoded = jnp.zeros((N_MP, part_rows, part), BF)
    for k in range(N_MP):
        encoded = lax.dynamic_update_slice_in_dim(encoded, placed[k][None], (m - k) % N_MP, 0)
    return encoded.reshape(1, rows, part), grad, loss.reshape(own_q)


def solution(mesh):
    fine = Mesh(
        mesh.devices.reshape(N_GRP, N_ZH, N_Y, N_C, N_MP), ("grp", "zh", "y", "c", "mp")
    )
    dp = ("zh", "y", "c")
    placed = (
        P("grp", dp, None),
        P(("grp",) + dp, "mp"),
        P("mp"),
        P("mp", ("grp",) + dp),
        P(),
        P(),
        P(),
        P(dp),
        P(dp, None),
        P(dp),
        P(dp),
    )
    return jax.shard_map(
        body,
        mesh=fine,
        in_specs=placed,
        out_specs=(P("grp", dp, "mp"), P(dp, "mp"), P(dp)),
        check_vma=False,
    )
```

time: 137 us -> 130 us (0.949)
  blocking collectives: 21.9 us -> 0 us
  waiting for transfers between devices: 20.2 us -> 41.5 us
  starting transfers between devices: 76.2 us -> 69.1 us
  local copies, waits for them, and re-layouts: 5.68 us -> 7.07 us
    all_to_all x1 -> x0, blocking collectives: 21.9 us -> none  [spread(): return lax.all_to_all(filled, axes, 0, 0, tiled=True)]
    all_to_all x1 -> x3, waiting for transfers between devices: 0.01 us -> 15.5 us  [spread(): return lax.all_to_all(filled, axes, 0, 0, tiled=True)]
    ppermute x21 -> x18, waiting for transfers between devices: 11.5 us -> 26.1 us  [shift(): lax.ppermute(block, axis, [(i, (i + distance) % n) for i in range(n)])]
    all_to_all x1, waiting for transfers between devices: 8.75 us -> 0.01 us  [body(): arrived = lax.all_to_all(shares, ('grp', 'y', 'mp'), 0, 0, tiled=True)]
    ppermute x21 -> x18, starting transfers between devices: 35.5 us -> 27.5 us  [shift(): lax.ppermute(block, axis, [(i, (i + distance) % n) for i in range(n)])]
    all_to_all x1 -> x3, starting transfers between devices: 18.8 us -> 21.1 us  [spread(): return lax.all_to_all(filled, axes, 0, 0, tiled=True)]
    ppermute x6 -> x3, starting transfers between devices: 4.03 us -> 2.01 us  [shift_refresh(): return lax.ppermute(block, ('grp', axis), route)]
    broadcast_in_dim x2 -> x3, local copies, waits for them, and re-layouts: 0.72 us -> 2.38 us  [spread(): filled = jnp.broadcast_to(block[None], (n,) + block.shape)]
  transfers between devices with their start and end apart: 29 -> 25, of which waited for: 6 -> 11; matrix products, arithmetic and copies ran while one was open for 1% -> 1% of each run, Pallas kernels for 5% -> 0%
where the time goes in v2:
time: 130 us; the launch traced here: 129 us
  starting transfers between devices  69.1 us (53%)
  waiting for transfers between devices  41.5 us (32%)
  Pallas kernels  10.3 us (8%)
  local copies, waits for them, and re-layouts  7.07 us (5%)
    ppermute x18, starting transfers between devices, shift(): lax.ppermute(block, axis, [(i, (i + distance) % n) for i in range(n)])  27.5 us
    ppermute x18, waiting for transfers between devices, shift(): lax.ppermute(block, axis, [(i, (i + distance) % n) for i in range(n)])  26.1 us
    all_to_all x3, starting transfers between devices, spread(): return lax.all_to_all(filled, axes, 0, 0, tiled=True)  21.1 us
    all_to_all x1, starting transfers between devices, body(): arrived = lax.all_to_all(shares, ('grp', 'y', 'mp'), 0, 0, tiled=True)  18.5 us
    all_to_all x3, waiting for transfers between devices, spread(): return lax.all_to_all(filled, axes, 0, 0, tiled=True)  15.5 us
    pallas_call x1, Pallas kernels, body(): pl.pallas_call(ffn_kernel, out_shape=[jax.ShapeDtypeStruct((part_rows, wi...  5.91 us
    unnamed x27, local copies, waits for them, and re-layouts  3.29 us
  transfers between devices with their start and end apart: 25, of which 11 were waited for; matrix products, arithmetic and copies ran while one was open for 1% of the time, Pallas kernels for 0%

profile of v2, /device:TPU:1, one launch (start us, length us, event | category | flops | bytes accessed | tf_op | source)
XLA Modules:
  0.0 129.1 jit_solution(1252539007338625613)
XLA Ops:
  2.2 9.0 %all-to-all-start = ((bf16[8,16,1536]{2,1,0:T(8,128)(2,1)}), bf16[8,16,1536]{2,1,0:T(8,128)(2,1)S(1)}, u32[]{:S(2)}, u32[]{:S(2)}) async-start(bf16[8,16,1536]{2,1,0:T(8,128)(2,1)} %broadcast_in_dim.55), calls=%async_computation | async-start | bytes 786432 | tf_op jit(solution)/shard_map/all_to_all | solution.py:49
  11.2 2.8 %collective-permute-start.9 = (bf16[16,512]{1,0:T(8,128)(2,1)S(1)}, bf16[16,512]{1,0:T(8,128)(2,1)S(1)}, u32[]{:S(2)}, u32[]{:S(2)}) collective-permute-start(bf16[16,512]{1,0:T(8,128)(2,1)S(1)} %get-tuple-element.38), channel_id=1, source_target_pairs={{0,24},{8,0},{16,8},{24,16},{1,25},{9,1},{17,9},{25,17},{2,26},{10... | collective-permute-start | bytes 49160 | tf_op jit(solution)/shard_map/ppermute | solution.py:38
  14.0 1.6 %collective-permute-start.8 = (bf16[16,512]{1,0:T(8,128)(2,1)S(1)}, bf16[16,512]{1,0:T(8,128)(2,1)S(1)}, u32[]{:S(2)}, u32[]{:S(2)}) collective-permute-start(bf16[16,512]{1,0:T(8,128)(2,1)S(1)} %get-tuple-element.38), channel_id=1, source_target_pairs={{0,16},{8,24},{16,0},{24,8},{1,17},{9,25},{17,1},{25,9},{2,18},{10... | collective-permute-start | bytes 49160 | tf_op jit(solution)/shard_map/ppermute | solution.py:38
  15.6 2.3 %collective-permute-done.7 = bf16[16,512]{1,0:T(8,128)(2,1)S(1)} collective-permute-done((bf16[16,512]{1,0:T(8,128)(2,1)S(1)}, bf16[16,512]{1,0:T(8,128)(2,1)S(1)}, u32[]{:S(2)}, u32[]{:S(2)}) %collective-permute-start.7) | collective-permute-done | bytes 16416 | tf_op jit(solution)/shard_map/ppermute | solution.py:38
  18.1 3.6 %all-to-all-done.rest_0_ = bf16[8,16,1536]{2,1,0:T(8,128)(2,1)S(1)} async-done(((bf16[8,16,1536]{2,1,0:T(8,128)(2,1)}), bf16[8,16,1536]{2,1,0:T(8,128)(2,1)S(1)}, u32[]{:S(2)}, u32[]{:S(2)}) %all-to-all-start) | async-done | bytes 393248 | tf_op jit(solution)/shard_map/all_to_all | solution.py:49
  22.6 5.5 %all-to-all-start.1 = ((bf16[8,4,16,512]{3,2,1,0:T(8,128)(2,1)}), bf16[8,4,16,512]{3,2,1,0:T(8,128)(2,1)S(1)}, u32[]{:S(2)}, u32[]{:S(2)}) async-start(bf16[8,4,16,512]{3,2,1,0:T(8,128)(2,1)} %broadcast_in_dim.56), calls=%async_computation.1 | async-start | bytes 1048576 | tf_op jit(solution)/shard_map/all_to_all | solution.py:49
  28.1 1.3 %collective-permute-start = (bf16[8,16,1536]{2,1,0:T(8,128)(2,1)S(1)}, bf16[8,16,1536]{2,1,0:T(8,128)(2,1)S(1)}, u32[]{:S(2)}, u32[]{:S(2)}) collective-permute-start(bf16[8,16,1536]{2,1,0:T(8,128)(2,1)S(1)} %all-to-all-done.rest_0_), channel_id=1, source_target_pairs={{0,8},{8,16},{16,24},{24,0},{1,9},{9,17},{17,25},{25,1},{2,10},{10... | collective-permute-start | bytes 1179656 | tf_op jit(solution)/shard_map/ppermute | solution.py:38
  29.4 2.6 %collective-permute-start.1 = (bf16[8,16,1536]{2,1,0:T(8,128)(2,1)S(1)}, bf16[8,16,1536]{2,1,0:T(8,128)(2,1)S(1)}, u32[]{:S(2)}, u32[]{:S(2)}) collective-permute-start(bf16[8,16,1536]{2,1,0:T(8,128)(2,1)S(1)} %all-to-all-done.rest_0_), channel_id=1, source_target_pairs={{0,16},{8,24},{16,0},{24,8},{1,17},{9,25},{17,1},{25,9},{2,18},{10... | collective-permute-start | bytes 1179656 | tf_op jit(solution)/shard_map/ppermute | solution.py:38
  32.0 1.1 collective-permute-start.2
  33.1 2.4 %collective-permute-start.3 = (bf16[8,16,1536]{2,1,0:T(8,128)(2,1)S(1)}, bf16[8,16,1536]{2,1,0:T(8,128)(2,1)}, u32[]{:S(2)}, u32[]{:S(2)}) collective-permute-start(bf16[8,16,1536]{2,1,0:T(8,128)(2,1)S(1)} %all-to-all-done.rest_0_), channel_id=1, source_target_pairs={{0,4},{4,0},{1,5},{5,1},{2,6},{6,2},{3,7},{7,3},{8,12},{12,8},{9,1... | collective-permute-start | bytes 1179656 | tf_op jit(solution)/shard_map/ppermute | solution.py:38
  35.5 6.5 %all-to-all-done.1.rest_8_ = bf16[8,4,16,512]{3,2,1,0:T(8,128)(2,1)S(1)} async-done(((bf16[8,4,16,512]{3,2,1,0:T(8,128)(2,1)}), bf16[8,4,16,512]{3,2,1,0:T(8,128)(2,1)S(1)}, u32[]{:S(2)}, u32[]{:S(2)}) %all-to-all-start.1) | async-done | bytes 524320 | tf_op jit(solution)/shard_map/all_to_all | solution.py:49
  42.0 1.9 %collective-permute-start.10 = (bf16[8,4,16,512]{3,2,1,0:T(8,128)(2,1)S(1)}, bf16[8,4,16,512]{3,2,1,0:T(8,128)(2,1)S(1)}, u32[]{:S(2)}, u32[]{:S(2)}) collective-permute-start(bf16[8,4,16,512]{3,2,1,0:T(8,128)(2,1)S(1)} %all-to-all-done.1.rest_8_), channel_id=1, source_target_pairs={{0,4},{4,0},{1,5},{5,1},{2,6},{6,2},{3,7},{7,3},{8,12},{12,8},{9,1... | collective-permute-start | bytes 1572872 | tf_op jit(solution)/shard_map/ppermute | solution.py:38
  43.9 4.1 %collective-permute-done.1.rest_2_ = bf16[8,16,1536]{2,1,0:T(8,128)(2,1)S(1)} collective-permute-done((bf16[8,16,1536]{2,1,0:T(8,128)(2,1)S(1)}, bf16[8,16,1536]{2,1,0:T(8,128)(2,1)S(1)}, u32[]{:S(2)}, u32[]{:S(2)}) %collective-permute-start.1) | collective-permute-done | bytes 393248 | tf_op jit(solution)/shard_map/ppermute | solution.py:38
  48.0 2.5 %collective-permute-start.5 = (bf16[8,16,1536]{2,1,0:T(8,128)(2,1)S(1)}, bf16[8,16,1536]{2,1,0:T(8,128)(2,1)}, u32[]{:S(2)}, u32[]{:S(2)}) collective-permute-start(bf16[8,16,1536]{2,1,0:T(8,128)(2,1)S(1)} %collective-permute-done.1.rest_2_), channel_id=1, source_target_pairs={{0,4},{4,0},{1,5},{5,1},{2,6},{6,2},{3,7},{7,3},{8,12},{12,8},{9,1... | collective-permute-start | bytes 1179656 | tf_op jit(solution)/shard_map/ppermute | solution.py:38
  53.6 1.0 copy-done.5
  54.6 5.9 %ffn.1 = (f32[128,1024]{1,0:T(8,128)S(1)}, bf16[128,1024]{1,0:T(8,128)(2,1)}, bf16[128,1024]{1,0:T(8,128)(2,1)}, bf16[128,1024]{1,0:T(8,128)(2,1)}) custom-call(s32[4]{0:T(128)S(1)} %pad_add_fusion.place, bf16[512,1024]{1,0:T(8,128)(2,1)S(1)} %bitcast.32, f32[1,1024]{1,0:T(1,128)S(1)} %bitcast.37, bf16[8,16,1536]{2,1,0:T(8,128)(2,1)S(1)} %all-to-all-done.rest_0_, ...), custom_call_target="tpu_custom_call" | custom-call | flops 2147483648 | bytes 8388608 | tf_op jit(solution)/shard_map/ffn/pallas_call | solution.py:251
  60.5 1.3 collective-permute-start.11
  61.8 2.4 %collective-permute-start.12 = (bf16[128,1024]{1,0:T(8,128)(2,1)}, bf16[128,1024]{1,0:T(8,128)(2,1)S(1)}, u32[]{:S(2)}, u32[]{:S(2)}) collective-permute-start(bf16[128,1024]{1,0:T(8,128)(2,1)} %get-tuple-element.22), channel_id=1, source_target_pairs={{0,2},{1,3},{2,0},{3,1},{4,6},{5,7},{6,4},{7,5},{8,10},{9,11},{10,... | collective-permute-start | bytes 786440 | tf_op jit(solution)/shard_map/ppermute | solution.py:38
  64.3 1.2 collective-permute-start.13
  65.6 3.8 %collective-permute-done.11.r1 = bf16[128,1024]{1,0:T(8,128)(2,1)S(1)} collective-permute-done((bf16[128,1024]{1,0:T(8,128)(2,1)}, bf16[128,1024]{1,0:T(8,128)(2,1)S(1)}, u32[]{:S(2)}, u32[]{:S(2)}) %collective-permute-start.11) | collective-permute-done | bytes 262176 | tf_op jit(solution)/shard_map/ppermute | solution.py:38
  69.4 6.6 %collective-permute-done.12.r2 = bf16[128,1024]{1,0:T(8,128)(2,1)S(1)} collective-permute-done((bf16[128,1024]{1,0:T(8,128)(2,1)}, bf16[128,1024]{1,0:T(8,128)(2,1)S(1)}, u32[]{:S(2)}, u32[]{:S(2)}) %collective-permute-start.12) | collective-permute-done | bytes 262176 | tf_op jit(solution)/shard_map/ppermute | solution.py:38
  76.0 1.1 norm.1
  77.2 1.4 %collective-permute-start.14 = (bf16[32,1024]{1,0:T(8,128)(2,1)S(1)}, bf16[32,1024]{1,0:T(8,128)(2,1)S(1)}, u32[]{:S(2)}, u32[]{:S(2)}) collective-permute-start(bf16[32,1024]{1,0:T(8,128)(2,1)S(1)} %get-tuple-element.29), channel_id=1, source_target_pairs={{0,4},{4,0},{1,5},{5,1},{2,6},{6,2},{3,7},{7,3},{8,12},{12,8},{9,1... | collective-permute-start | bytes 196616 | tf_op jit(solution)/shard_map/ppermute | solution.py:38
  79.3 6.6 %all-to-all-start.2 = ((bf16[32,2,1152]{2,1,0:T(2,128)(2,1)}), bf16[32,2,1152]{2,1,0:T(2,128)(2,1)S(1)}, u32[]{:S(2)}, u32[]{:S(2)}) async-start(bf16[32,2,1152]{2,1,0:T(2,128)(2,1)} %broadcast_in_dim.62), calls=%async_computation.2 | async-start | bytes 294912 | tf_op jit(solution)/shard_map/all_to_all | solution.py:49
  88.0 5.4 %all-to-all-done.2 = bf16[32,2,1152]{2,1,0:T(2,128)(2,1)S(1)} async-done(((bf16[32,2,1152]{2,1,0:T(2,128)(2,1)}), bf16[32,2,1152]{2,1,0:T(2,128)(2,1)S(1)}, u32[]{:S(2)}, u32[]{:S(2)}) %all-to-all-start.2) | async-done | bytes 147488 | tf_op jit(solution)/shard_map/all_to_all | solution.py:49
  93.5 2.5 %score.1 = f32[32,16,384]{2,1,0:T(8,128)} custom-call(s32[4]{0:T(128)S(1)} %pad_add_fusion.place, bf16[32,1152]{1,0:T(8,128)(2,1)S(1)} %reshape.44.q_ref, bf16[64,1024]{1,0:T(8,128)(2,1)S(1)} %constant_dynamic-update-slice_fusion.p0, bf16[64,1024]{1,0:T(8,128)(2,1)S(1)} %collective-permute-done.15.p1, bf16[64,1024]{1,0:T(8,128)(2,1)S(1)} %collective-permute-done.16.p2, ...), custom_call_target="tpu_custom_call" | custom-call | flops 157286400 | bytes 3145728 | tf_op jit(solution)/shard_map/score/pallas_call | solution.py:290
  96.0 18.5 %all-to-all-start.3 = ((f32[32,16,384]{2,1,0:T(8,128)}), f32[32,16,384]{2,1,0:T(8,128)S(1)}, u32[]{:S(2)}, u32[]{:S(2)}) async-start(f32[32,16,384]{2,1,0:T(8,128)} %score.1), calls=%async_computation.3 | async-start | bytes 1572864 | tf_op jit(solution)/shard_map/all_to_all | solution.py:300
  114.6 1.3 %collective-permute-start.18 = (bf16[128,256]{1,0:T(8,128)(2,1)S(1)}, bf16[128,256]{1,0:T(8,128)(2,1)S(1)}, u32[]{:S(2)}, u32[]{:S(2)}) collective-permute-start(bf16[128,256]{1,0:T(8,128)(2,1)S(1)} %get-tuple-element.31), channel_id=1, source_target_pairs={{0,1},{1,2},{2,3},{3,0},{4,5},{5,6},{6,7},{7,4},{8,9},{9,10},{10,1... | collective-permute-start | bytes 196616 | tf_op jit(solution)/shard_map/ppermute | solution.py:38
  115.9 2.4 %collective-permute-start.19 = (bf16[128,256]{1,0:T(8,128)(2,1)S(1)}, bf16[128,256]{1,0:T(8,128)(2,1)S(1)}, u32[]{:S(2)}, u32[]{:S(2)}) collective-permute-start(bf16[128,256]{1,0:T(8,128)(2,1)S(1)} %get-tuple-element.32), channel_id=1, source_target_pairs={{0,2},{1,3},{2,0},{3,1},{4,6},{5,7},{6,4},{7,5},{8,10},{9,11},{10,... | collective-permute-start | bytes 196616 | tf_op jit(solution)/shard_map/ppermute | solution.py:38
  118.3 1.2 collective-permute-start.20
  119.5 3.5 %collective-permute-done.18 = bf16[128,256]{1,0:T(8,128)(2,1)S(1)} collective-permute-done((bf16[128,256]{1,0:T(8,128)(2,1)S(1)}, bf16[128,256]{1,0:T(8,128)(2,1)S(1)}, u32[]{:S(2)}, u32[]{:S(2)}) %collective-permute-start.18) | collective-permute-done | bytes 65568 | tf_op jit(solution)/shard_map/ppermute | solution.py:38
  123.0 5.3 %collective-permute-done.19 = bf16[128,256]{1,0:T(8,128)(2,1)S(1)} collective-permute-done((bf16[128,256]{1,0:T(8,128)(2,1)S(1)}, bf16[128,256]{1,0:T(8,128)(2,1)S(1)}, u32[]{:S(2)}, u32[]{:S(2)}) %collective-permute-start.19) | collective-permute-done | bytes 65568 | tf_op jit(solution)/shard_map/ppermute | solution.py:38
  (73 shorter events, 9.5 us)
Async XLA Ops:
  2.2 19.6 %all-to-all-start = ((bf16[8,16,1536]{2,1,0:T(8,128)(2,1)}), bf16[8,16,1536]{2,1,0:T(8,128)(2,1)S(1)}, u32[]{:S(2)}, u32[]{:S(2)}) async-start(bf16[8,16,1536]{2,1,0:T(8,128)(2,1)} %broadcast_in_dim.55), calls=%async_computation | async-start | bytes 786432 | tf_op jit(solution)/shard_map/all_to_all | solution.py:49
  11.2 42.1 %copy-start = (bf16[1,512,1024]{2,1,0:T(8,128)(2,1)S(1)}, bf16[1,512,1024]{2,1,0:T(8,128)(2,1)}, u32[]{:S(2)}) copy-start(bf16[1,512,1024]{2,1,0:T(8,128)(2,1)} %param.11) | copy-start | bytes 3145732
  11.2 4.5 %collective-permute-start.9 = (bf16[16,512]{1,0:T(8,128)(2,1)S(1)}, bf16[16,512]{1,0:T(8,128)(2,1)S(1)}, u32[]{:S(2)}, u32[]{:S(2)}) collective-permute-start(bf16[16,512]{1,0:T(8,128)(2,1)S(1)} %get-tuple-element.38), channel_id=1, source_target_pairs={{0,24},{8,0},{16,8},{24,16},{1,25},{9,1},{17,9},{25,17},{2,26},{10... | collective-permute-start | bytes 49160 | tf_op jit(solution)/shard_map/ppermute | solution.py:38
  14.0 3.9 %collective-permute-start.7 = (bf16[16,512]{1,0:T(8,128)(2,1)S(1)}, bf16[16,512]{1,0:T(8,128)(2,1)S(1)}, u32[]{:S(2)}, u32[]{:S(2)}) collective-permute-start(bf16[16,512]{1,0:T(8,128)(2,1)S(1)} %get-tuple-element.38), channel_id=1, source_target_pairs={{0,8},{8,16},{16,24},{24,0},{1,9},{9,17},{17,25},{25,1},{2,10},{10... | collective-permute-start | bytes 49160 | tf_op jit(solution)/shard_map/ppermute | solution.py:38
  14.0 4.1 %collective-permute-start.8 = (bf16[16,512]{1,0:T(8,128)(2,1)S(1)}, bf16[16,512]{1,0:T(8,128)(2,1)S(1)}, u32[]{:S(2)}, u32[]{:S(2)}) collective-permute-start(bf16[16,512]{1,0:T(8,128)(2,1)S(1)} %get-tuple-element.38), channel_id=1, source_target_pairs={{0,16},{8,24},{16,0},{24,8},{1,17},{9,25},{17,1},{25,9},{2,18},{10... | collective-permute-start | bytes 49160 | tf_op jit(solution)/shard_map/ppermute | solution.py:38
  22.6 28.7 %copy-start.11 = (s32[8]{0:T(128)S(1)}, s32[8]{0:T(128)}, u32[]{:S(2)}) copy-start(s32[8]{0:T(128)} %param.21) | copy-start | bytes 100
  22.6 19.4 %all-to-all-start.1 = ((bf16[8,4,16,512]{3,2,1,0:T(8,128)(2,1)}), bf16[8,4,16,512]{3,2,1,0:T(8,128)(2,1)S(1)}, u32[]{:S(2)}, u32[]{:S(2)}) async-start(bf16[8,4,16,512]{3,2,1,0:T(8,128)(2,1)} %broadcast_in_dim.56), calls=%async_computation.1 | async-start | bytes 1048576 | tf_op jit(solution)/shard_map/all_to_all | solution.py:49
  28.1 15.8 %collective-permute-start = (bf16[8,16,1536]{2,1,0:T(8,128)(2,1)S(1)}, bf16[8,16,1536]{2,1,0:T(8,128)(2,1)S(1)}, u32[]{:S(2)}, u32[]{:S(2)}) collective-permute-start(bf16[8,16,1536]{2,1,0:T(8,128)(2,1)S(1)} %all-to-all-done.rest_0_), channel_id=1, source_target_pairs={{0,8},{8,16},{16,24},{24,0},{1,9},{9,17},{17,25},{25,1},{2,10},{10... | collective-permute-start | bytes 1179656 | tf_op jit(solution)/shard_map/ppermute | solution.py:38
  29.4 18.6 %collective-permute-start.1 = (bf16[8,16,1536]{2,1,0:T(8,128)(2,1)S(1)}, bf16[8,16,1536]{2,1,0:T(8,128)(2,1)S(1)}, u32[]{:S(2)}, u32[]{:S(2)}) collective-permute-start(bf16[8,16,1536]{2,1,0:T(8,128)(2,1)S(1)} %all-to-all-done.rest_0_), channel_id=1, source_target_pairs={{0,16},{8,24},{16,0},{24,8},{1,17},{9,25},{17,1},{25,9},{2,18},{10... | collective-permute-start | bytes 1179656 | tf_op jit(solution)/shard_map/ppermute | solution.py:38
  32.0 19.2 %collective-permute-start.2 = (bf16[8,16,1536]{2,1,0:T(8,128)(2,1)S(1)}, bf16[8,16,1536]{2,1,0:T(8,128)(2,1)}, u32[]{:S(2)}, u32[]{:S(2)}) collective-permute-start(bf16[8,16,1536]{2,1,0:T(8,128)(2,1)S(1)} %all-to-all-done.rest_0_), channel_id=1, source_target_pairs={{0,24},{8,0},{16,8},{24,16},{1,25},{9,1},{17,9},{25,17},{2,26},{10... | collective-permute-start | bytes 1179656 | tf_op jit(solution)/shard_map/ppermute | solution.py:38
  33.1 19.9 %collective-permute-start.3 = (bf16[8,16,1536]{2,1,0:T(8,128)(2,1)S(1)}, bf16[8,16,1536]{2,1,0:T(8,128)(2,1)}, u32[]{:S(2)}, u32[]{:S(2)}) collective-permute-start(bf16[8,16,1536]{2,1,0:T(8,128)(2,1)S(1)} %all-to-all-done.rest_0_), channel_id=1, source_target_pairs={{0,4},{4,0},{1,5},{5,1},{2,6},{6,2},{3,7},{7,3},{8,12},{12,8},{9,1... | collective-permute-start | bytes 1179656 | tf_op jit(solution)/shard_map/ppermute | solution.py:38
  42.0 11.0 %collective-permute-start.10 = (bf16[8,4,16,512]{3,2,1,0:T(8,128)(2,1)S(1)}, bf16[8,4,16,512]{3,2,1,0:T(8,128)(2,1)S(1)}, u32[]{:S(2)}, u32[]{:S(2)}) collective-permute-start(bf16[8,4,16,512]{3,2,1,0:T(8,128)(2,1)S(1)} %all-to-all-done.1.rest_8_), channel_id=1, source_target_pairs={{0,4},{4,0},{1,5},{5,1},{2,6},{6,2},{3,7},{7,3},{8,12},{12,8},{9,1... | collective-permute-start | bytes 1572872 | tf_op jit(solution)/shard_map/ppermute | solution.py:38
  43.9 9.2 %collective-permute-start.4 = (bf16[8,16,1536]{2,1,0:T(8,128)(2,1)S(1)}, bf16[8,16,1536]{2,1,0:T(8,128)(2,1)}, u32[]{:S(2)}, u32[]{:S(2)}) collective-permute-start(bf16[8,16,1536]{2,1,0:T(8,128)(2,1)S(1)} %collective-permute-done.rest_1_), channel_id=1, source_target_pairs={{0,4},{4,0},{1,5},{5,1},{2,6},{6,2},{3,7},{7,3},{8,12},{12,8},{9,1... | collective-permute-start | bytes 1179656 | tf_op jit(solution)/shard_map/ppermute | solution.py:38
  48.0 5.0 %collective-permute-start.5 = (bf16[8,16,1536]{2,1,0:T(8,128)(2,1)S(1)}, bf16[8,16,1536]{2,1,0:T(8,128)(2,1)}, u32[]{:S(2)}, u32[]{:S(2)}) collective-permute-start(bf16[8,16,1536]{2,1,0:T(8,128)(2,1)S(1)} %collective-permute-done.1.rest_2_), channel_id=1, source_target_pairs={{0,4},{4,0},{1,5},{5,1},{2,6},{6,2},{3,7},{7,3},{8,12},{12,8},{9,1... | collective-permute-start | bytes 1179656 | tf_op jit(solution)/shard_map/ppermute | solution.py:38
  51.3 2.1 %collective-permute-start.6 = (bf16[8,16,1536]{2,1,0:T(8,128)(2,1)}, bf16[8,16,1536]{2,1,0:T(8,128)(2,1)}, u32[]{:S(2)}, u32[]{:S(2)}) collective-permute-start(bf16[8,16,1536]{2,1,0:T(8,128)(2,1)} %collective-permute-done.2.rest_3_), channel_id=1, source_target_pairs={{0,4},{4,0},{1,5},{5,1},{2,6},{6,2},{3,7},{7,3},{8,12},{12,8},{9,1... | collective-permute-start | bytes 1179656 | tf_op jit(solution)/shard_map/ppermute | solution.py:38
  53.6 1.0 copy-start.5
  60.5 4.9 %copy-start.9 = (s32[8,32]{1,0:T(8,128)S(1)}, s32[8,32]{1,0:T(8,128)}, u32[]{:S(2)}) copy-start(s32[8,32]{1,0:T(8,128)} %param.19) | copy-start | bytes 3076
  60.5 8.9 %collective-permute-start.11 = (bf16[128,1024]{1,0:T(8,128)(2,1)}, bf16[128,1024]{1,0:T(8,128)(2,1)S(1)}, u32[]{:S(2)}, u32[]{:S(2)}) collective-permute-start(bf16[128,1024]{1,0:T(8,128)(2,1)} %get-tuple-element.21), channel_id=1, source_target_pairs={{0,1},{1,2},{2,3},{3,0},{4,5},{5,6},{6,7},{7,4},{8,9},{9,10},{10,1... | collective-permute-start | bytes 786440 | tf_op jit(solution)/shard_map/ppermute | solution.py:38
  61.8 14.2 %collective-permute-start.12 = (bf16[128,1024]{1,0:T(8,128)(2,1)}, bf16[128,1024]{1,0:T(8,128)(2,1)S(1)}, u32[]{:S(2)}, u32[]{:S(2)}) collective-permute-start(bf16[128,1024]{1,0:T(8,128)(2,1)} %get-tuple-element.22), channel_id=1, source_target_pairs={{0,2},{1,3},{2,0},{3,1},{4,6},{5,7},{6,4},{7,5},{8,10},{9,11},{10,... | collective-permute-start | bytes 786440 | tf_op jit(solution)/shard_map/ppermute | solution.py:38
  64.3 11.7 %collective-permute-start.13 = (bf16[128,1024]{1,0:T(8,128)(2,1)}, bf16[128,1024]{1,0:T(8,128)(2,1)S(1)}, u32[]{:S(2)}, u32[]{:S(2)}) collective-permute-start(bf16[128,1024]{1,0:T(8,128)(2,1)} %get-tuple-element.23), channel_id=1, source_target_pairs={{0,3},{1,0},{2,1},{3,2},{4,7},{5,4},{6,5},{7,6},{8,11},{9,8},{10,9... | collective-permute-start | bytes 786440 | tf_op jit(solution)/shard_map/ppermute | solution.py:38
  65.4 10.6 %copy-start.3 = (f32[1024]{0:T(1024)S(1)}, f32[1024]{0:T(1024)}, u32[]{:S(2)}) copy-start(f32[1024]{0:T(1024)} %param.17) | copy-start | bytes 12292
  65.5 10.5 %copy-start.2 = (f32[1024]{0:T(1024)S(1)}, f32[1024]{0:T(1024)}, u32[]{:S(2)}) copy-start(f32[1024]{0:T(1024)} %param.16) | copy-start | bytes 12292
  65.6 10.4 %copy-start.1 = (f32[1024]{0:T(1024)S(1)}, f32[1024]{0:T(1024)}, u32[]{:S(2)}) copy-start(f32[1024]{0:T(1024)} %param.15) | copy-start | bytes 12292
  77.2 8.8 %collective-permute-start.14 = (bf16[32,1024]{1,0:T(8,128)(2,1)S(1)}, bf16[32,1024]{1,0:T(8,128)(2,1)S(1)}, u32[]{:S(2)}, u32[]{:S(2)}) collective-permute-start(bf16[32,1024]{1,0:T(8,128)(2,1)S(1)} %get-tuple-element.29), channel_id=1, source_target_pairs={{0,4},{4,0},{1,5},{5,1},{2,6},{6,2},{3,7},{7,3},{8,12},{12,8},{9,1... | collective-permute-start | bytes 196616 | tf_op jit(solution)/shard_map/ppermute | solution.py:38
  79.3 14.0 %all-to-all-start.2 = ((bf16[32,2,1152]{2,1,0:T(2,128)(2,1)}), bf16[32,2,1152]{2,1,0:T(2,128)(2,1)S(1)}, u32[]{:S(2)}, u32[]{:S(2)}) async-start(bf16[32,2,1152]{2,1,0:T(2,128)(2,1)} %broadcast_in_dim.62), calls=%async_computation.2 | async-start | bytes 294912 | tf_op jit(solution)/shard_map/all_to_all | solution.py:49
  86.0 7.5 %collective-permute-start.15 = (bf16[64,1024]{1,0:T(8,128)(2,1)S(1)}, bf16[64,1024]{1,0:T(8,128)(2,1)S(1)}, u32[]{:S(2)}, u32[]{:S(2)}) collective-permute-start(bf16[64,1024]{1,0:T(8,128)(2,1)S(1)} %constant_dynamic-update-slice_fusion.p0), channel_id=1, source_target_pairs={{128,160},{160,192},{192,224},{224,128},{129,161},{161,193},{193,2... | collective-permute-start | bytes 393224 | tf_op jit(solution)/shard_map/ppermute | solution.py:44
  86.6 6.8 %collective-permute-start.16 = (bf16[64,1024]{1,0:T(8,128)(2,1)S(1)}, bf16[64,1024]{1,0:T(8,128)(2,1)S(1)}, u32[]{:S(2)}, u32[]{:S(2)}) collective-permute-start(bf16[64,1024]{1,0:T(8,128)(2,1)S(1)} %constant_dynamic-update-slice_fusion.p0), channel_id=1, source_target_pairs={{128,192},{160,224},{192,128},{224,160},{129,193},{161,225},{193,1... | collective-permute-start | bytes 393224 | tf_op jit(solution)/shard_map/ppermute | solution.py:44
  87.3 6.2 %collective-permute-start.17 = (bf16[64,1024]{1,0:T(8,128)(2,1)S(1)}, bf16[64,1024]{1,0:T(8,128)(2,1)S(1)}, u32[]{:S(2)}, u32[]{:S(2)}) collective-permute-start(bf16[64,1024]{1,0:T(8,128)(2,1)S(1)} %constant_dynamic-update-slice_fusion.p0), channel_id=1, source_target_pairs={{128,224},{160,128},{192,160},{224,192},{129,225},{161,129},{193,1... | collective-permute-start | bytes 393224 | tf_op jit(solution)/shard_map/ppermute | solution.py:44
  96.0 32.3 %all-to-all-start.3 = ((f32[32,16,384]{2,1,0:T(8,128)}), f32[32,16,384]{2,1,0:T(8,128)S(1)}, u32[]{:S(2)}, u32[]{:S(2)}) async-start(f32[32,16,384]{2,1,0:T(8,128)} %score.1), calls=%async_computation.3 | async-start | bytes 1572864 | tf_op jit(solution)/shard_map/all_to_all | solution.py:300
  114.6 8.4 %collective-permute-start.18 = (bf16[128,256]{1,0:T(8,128)(2,1)S(1)}, bf16[128,256]{1,0:T(8,128)(2,1)S(1)}, u32[]{:S(2)}, u32[]{:S(2)}) collective-permute-start(bf16[128,256]{1,0:T(8,128)(2,1)S(1)} %get-tuple-element.31), channel_id=1, source_target_pairs={{0,1},{1,2},{2,3},{3,0},{4,5},{5,6},{6,7},{7,4},{8,9},{9,10},{10,1... | collective-permute-start | bytes 196616 | tf_op jit(solution)/shard_map/ppermute | solution.py:38
  115.9 12.4 %collective-permute-start.19 = (bf16[128,256]{1,0:T(8,128)(2,1)S(1)}, bf16[128,256]{1,0:T(8,128)(2,1)S(1)}, u32[]{:S(2)}, u32[]{:S(2)}) collective-permute-start(bf16[128,256]{1,0:T(8,128)(2,1)S(1)} %get-tuple-element.32), channel_id=1, source_target_pairs={{0,2},{1,3},{2,0},{3,1},{4,6},{5,7},{6,4},{7,5},{8,10},{9,11},{10,... | collective-permute-start | bytes 196616 | tf_op jit(solution)/shard_map/ppermute | solution.py:38
  118.3 10.0 %collective-permute-start.20 = (bf16[128,256]{1,0:T(8,128)(2,1)S(1)}, bf16[128,256]{1,0:T(8,128)(2,1)S(1)}, u32[]{:S(2)}, u32[]{:S(2)}) collective-permute-start(bf16[128,256]{1,0:T(8,128)(2,1)S(1)} %get-tuple-element.33), channel_id=1, source_target_pairs={{0,3},{1,0},{2,1},{3,2},{4,7},{5,4},{6,5},{7,6},{8,11},{9,8},{10,9... | collective-permute-start | bytes 196616 | tf_op jit(solution)/shard_map/ppermute | solution.py:38
  (6 other events, 4.3 us)

commit v3 on v2

v3 whole, which is shorter than its diff:
```python
import jax
import jax.numpy as jnp
import numpy as np
from jax import lax
from jax.experimental import pallas as pl
from jax.experimental.pallas import tpu as pltpu
from jax.sharding import Mesh, PartitionSpec as P

WIN = 4
QLEN = 64
WINDOW_TOKENS = 128
SHARPNESS = 0.05
EPS_NORM = 1e-05
EPS_UNIT = 1e-06

N_GRP, N_ZH, N_Y, N_C, N_MP = 2, 4, 4, 2, 4
N_Z = N_GRP * N_ZH
BF = jnp.bfloat16
F32 = jnp.float32
VMEM = pl.BlockSpec(memory_space=pltpu.VMEM)
SMEM = pl.BlockSpec(memory_space=pltpu.SMEM)
ANY = pl.BlockSpec(memory_space=pl.ANY)
HBM = pl.BlockSpec(memory_space=pltpu.HBM)
NT = (((1,), (1,)), ((), ()))
N_NEG = 32
DIGIT = 64


def params():
    return pltpu.CompilerParams(vmem_limit_bytes=40 * 1024 * 1024)


def cost(flops, size):
    return pl.CostEstimate(flops=flops, bytes_accessed=size, transcendentals=0)


def shift(block, axis, distance):
    n = lax.axis_size(axis)
    return lax.ppermute(block, axis, [(i, (i + distance) % n) for i in range(n)])


def at(axis):
    return lax.axis_index(axis)


def iota(shape, axis):
    return lax.broadcasted_iota(jnp.int32, shape, axis)


def onehot(hit):
    return jnp.where(hit, 1.0, 0.0).astype(BF)


def pack_kernel(w_in, w_out_t, packed, sems):
    shard = w_in.shape[0]
    copies = []
    for z in range(packed.shape[0]):
        copies.append(pltpu.make_async_copy(w_in, packed.at[z, 0:shard], sems.at[2 * z]))
        copies.append(
            pltpu.make_async_copy(w_out_t, packed.at[z, shard : 2 * shard], sems.at[2 * z + 1])
        )
    for copy in copies:
        copy.start()
    for copy in copies:
        copy.wait()


def slots():
    y, c = at("y"), at("c")
    found = []
    for other in range(N_C):
        core = c if other == 0 else 1 - c
        for k in range(N_Y):
            found.append(lax.rem(y - k + N_Y, N_Y) * N_C + core)
    return found


def ffn_kernel(x_any, b_any, *rest):
    sources, small = rest[:8], rest[8:15]
    own_ref, s1, s2, s3 = rest[15:19]
    small_out = rest[19:26]
    w1, w2, x_ref, b_ref, hidden, total, sems = rest[26:]
    m = at("mp")
    hid = hidden.shape[1]
    shard = w1.shape[2]
    early = [
        pltpu.make_async_copy(x_any, x_ref, sems.at[16]),
        pltpu.make_async_copy(b_any, b_ref, sems.at[17]),
    ]
    late = []
    for i, slot in enumerate(slots()):
        early.append(
            pltpu.make_async_copy(sources[i].at[:, 0:shard], w1.at[:, slot], sems.at[2 * i])
        )
        late.append(
            pltpu.make_async_copy(
                sources[i].at[:, shard : 2 * shard], w2.at[:, slot], sems.at[2 * i + 1]
            )
        )
    for i, (source, target) in enumerate(zip(small, small_out)):
        late.append(pltpu.make_async_copy(source, target, sems.at[18 + i]))
    for copy in early + late:
        copy.start()
    for copy in early:
        copy.wait()
    depth = x_ref.shape[1]
    tile = 256
    for t in range(hid // tile):
        cols = slice(t * tile, (t + 1) * tile)
        w = w1[:, :, :, cols].reshape(depth, tile)
        pre = jnp.dot(x_ref[...], w, preferred_element_type=F32) + b_ref[:, cols]
        hidden[:, cols] = (0.5 * pre * (1.0 + lax.erf(pre * np.float32(0.5**0.5)))).astype(BF)
    for copy in late:
        copy.wait()
    planes = tile // (w2.shape[1] * w2.shape[2])
    for t in range(total.shape[1] // tile):
        w = w2[t * planes : (t + 1) * planes].reshape(tile, hid)
        total[:, t * tile : (t + 1) * tile] = lax.dot_general(
            hidden[...], w, NT, preferred_element_type=F32
        )
    rows = own_ref.shape[0]
    for k, out in ((2, s2), (1, s1), (3, s3), (0, own_ref)):
        j = lax.rem(m + k, N_MP)
        block = pl.ds(pl.multiple_of(j * rows, rows), rows)
        if k == 0:
            out[...] = total[block, :] + x_ref[block, :].astype(F32)
        else:
            out[...] = total[block, :].astype(BF)


def pieces(v):
    a = v.astype(BF)
    rest = v - a.astype(F32)
    b = rest.astype(BF)
    return a, b, (rest - b.astype(F32)).astype(BF)


def norm_kernel(
    own, r1, r2, r3, b_out, gain, bias, lens, negs, counts, poss, p_ref, send
):
    m = at("mp")
    rows, width = own.shape
    summed = own[...] + r1[...].astype(F32) + r2[...].astype(F32) + r3[...].astype(F32)
    summed = summed + b_out[...]
    center = jnp.mean(summed, axis=1, keepdims=True)
    off = summed - center
    spread_ = jnp.mean(off * off, axis=1, keepdims=True)
    coded = (off * lax.rsqrt(spread_ + EPS_NORM) * gain[...] + bias[...]).astype(BF)

    n_pass = p_ref.shape[0]
    n_all = lens.shape[1]
    chosen = iota((n_pass, n_all), 1) == iota((n_pass, n_all), 0) + m * n_pass
    length = jnp.sum(jnp.where(chosen, lens[...].astype(F32), 0.0), axis=1, keepdims=True)
    row = iota((n_pass, rows), 1)
    slab = iota((n_pass, rows), 0)
    begin = ((row % WIN) * WINDOW_TOKENS).astype(F32)
    live = jnp.where((row // WIN == slab) & (begin < length), 1.0, 0.0).astype(F32)
    count = jnp.sum(live, axis=1, keepdims=True)
    p = (jnp.dot(live.astype(BF), coded, preferred_element_type=F32) / count).astype(BF)
    p_ref[:, :width] = p
    pf = p.astype(F32)
    square = pieces(jnp.sum(pf * pf, axis=1, keepdims=True))
    lane = iota((n_pass, 128), 1)
    tail = jnp.zeros((n_pass, 128), F32)
    for i, piece in enumerate(square):
        tail = jnp.where(lane == i, piece.astype(F32), tail)
    p_ref[:, width:] = tail.astype(BF)

    pick = onehot(iota((16, rows), 1) // QLEN == iota((16, rows), 0))
    q = (jnp.dot(pick, coded, preferred_element_type=F32) * (1.0 / QLEN)).astype(BF)
    part = send.shape[2]
    block = jnp.zeros((16, part), F32)
    r16, c16 = iota((16, 16), 0), iota((16, 16), 1)
    n_q = rows // QLEN
    for j in range(N_MP):
        move = onehot((r16 == c16 + j * n_q) & (c16 < n_q))
        block = block + jnp.dot(
            move, q[:, j * part : (j + 1) * part], preferred_element_type=F32
        )
    own_q, n_neg = negs.shape
    ids = negs[...]
    diag = iota((own_q, own_q), 0) == iota((own_q, own_q), 1)
    n_used = jnp.sum(jnp.where(diag, counts[...].astype(F32), 0.0), axis=1, keepdims=True)
    pos = jnp.sum(jnp.where(diag, poss[...].astype(F32), 0.0), axis=1, keepdims=True)
    pos = pos.astype(jnp.int32)
    wide = iota((n_neg, part), 1)
    deep = iota((n_neg, part), 0)
    high = (ids // DIGIT).astype(F32).astype(BF)
    low = (ids % DIGIT).astype(F32).astype(BF)
    lists = jnp.dot(high, onehot(wide == deep), preferred_element_type=F32)
    lists = lists + jnp.dot(low, onehot(wide == deep + n_neg), preferred_element_type=F32)
    lane = iota((own_q, part), 1)
    lists = jnp.where(lane == 2 * n_neg, n_used, lists)
    lists = jnp.where(lane == 2 * n_neg + 1, (pos // DIGIT).astype(F32), lists)
    lists = jnp.where(lane == 2 * n_neg + 2, (pos % DIGIT).astype(F32), lists)
    r8, c8 = iota((16, own_q), 0), iota((16, own_q), 1)
    base = N_MP * n_q
    move = onehot((r8 >= base) & (r8 < base + n_q) & (c8 == m * n_q + r8 - base))
    block = (block + jnp.dot(move, lists.astype(BF), preferred_element_type=F32)).astype(BF)
    for g in range(N_GRP):
        for j in range(N_MP):
            send[g * N_MP + j, :rows, :] = coded[:, j * part : (j + 1) * part]
            send[g * N_MP + j, rows:, :] = block


def unpack_kernel(arrived, encoded, q_ref, lists):
    grp = at("grp")
    part = encoded.shape[1]
    rows = encoded.shape[0] // N_MP
    for j in range(N_MP):
        encoded[j * rows : (j + 1) * rows, :] = arrived[grp * N_MP + j, 0:rows, :]
    blocks = arrived[0:N_MP, rows : rows + 16, :].reshape(N_MP * 16, part)
    n_q = rows // QLEN
    shape = (16, N_MP * 16)
    r, c = iota(shape, 0), iota(shape, 1)
    for j in range(N_MP + 1):
        take = onehot((c // 16 == r // n_q) & (c % 16 == j * n_q + r % n_q))
        got = jnp.dot(take, blocks, preferred_element_type=F32)
        if j < N_MP:
            q_ref[:, j * part : (j + 1) * part] = got.astype(BF)
        else:
            lists[...] = got


def score_kernel(q_ref, lists_ref, *rest):
    blocks, out = rest[:-1], rest[-1]
    zh, y, c, m = at("zh"), at("y"), at("c"), at("mp")
    size = blocks[0].shape[0]
    width = q_ref.shape[1]
    each = size // N_ZH
    n_q = out.shape[1] // 2
    q = q_ref[...]
    qf = q.astype(F32)
    a = jnp.sqrt(jnp.sum(qf * qf, axis=1, keepdims=True) / width + EPS_UNIT)[:n_q]
    lists = lists_ref[:n_q, :]
    neg = lists[:, :N_NEG] * DIGIT + lists[:, N_NEG : 2 * N_NEG]
    count = lists[:, 2 * N_NEG : 2 * N_NEG + 1]
    pos = lists[:, 2 * N_NEG + 1 : 2 * N_NEG + 2] * DIGIT + lists[:, 2 * N_NEG + 2 : 2 * N_NEG + 3]
    slot = iota(neg.shape, 1).astype(F32)
    neg = jnp.where(slot < count, neg, -1.0)
    dots, squares = [], []
    first_three = onehot(iota((16, 128), 1) < 3)
    for block in blocks:
        dots.append(
            lax.dot_general(q, block[:, :width], NT, preferred_element_type=F32)[:n_q]
        )
        squares.append(
            lax.dot_general(first_three, block[:, width:], NT, preferred_element_type=F32)[:1]
        )
    dots = jnp.concatenate(dots, axis=1)
    b = jnp.sqrt(jnp.concatenate(squares, axis=1) / width + EPS_UNIT)
    n_p = dots.shape[1]
    s = dots / (width * SHARPNESS * a * b)
    lane = iota((1, n_p), 1)
    per_core = size * N_Y
    core = lax.rem(c + lane // per_core, N_C)
    line = lax.rem(y - lax.rem(lane, per_core) // size + N_Y, N_Y)
    slab = lax.rem(zh - lax.rem(lane, size) // each + N_ZH, N_ZH)
    number = ((slab * N_Y + line) * N_C + core) * (each * N_MP) + m * each + lax.rem(lane, each)
    number = number.astype(F32)
    match = jnp.where(pos == number, 1.0, 0.0).astype(F32)
    cand = jnp.zeros((n_q, n_p), F32)
    for j in range(N_NEG):
        cand = cand + jnp.where(neg[:, j : j + 1] == number, 1.0, 0.0)
    w = jnp.exp(s) * cand
    total = jnp.sum(w, axis=1, keepdims=True)
    score_pos = jnp.sum(s * match, axis=1, keepdims=True)
    unit = 1.0 / (np.float32(width**0.5) * b)
    coef = jnp.concatenate(pieces(w * unit) + pieces(match * unit), axis=0)
    grads = jnp.zeros((6 * n_q, width), F32)
    for i, block in enumerate(blocks):
        grads = grads + jnp.dot(
            coef[:, i * size : (i + 1) * size], block[:, :width], preferred_element_type=F32
        )
    pull = grads[:n_q] + grads[n_q : 2 * n_q] + grads[2 * n_q : 3 * n_q]
    toward = grads[3 * n_q : 4 * n_q] + grads[4 * n_q : 5 * n_q] + grads[5 * n_q :]
    part = width // N_MP
    stats = jnp.where(iota((n_q, 128), 1) < 64, total, score_pos)
    for g in range(N_GRP):
        for mm in range(N_MP):
            cols = slice(mm * part, (mm + 1) * part)
            d = g * N_MP + mm
            out[d, 0:n_q, 0:part] = pull[:, cols]
            out[d, n_q:, 0:part] = toward[:, cols]
            out[d, 0:n_q, part:] = stats
            out[d, n_q:, part:] = stats


def final_kernel(arrived, grad, loss):
    peers = arrived.shape[0] // N_GRP
    own, part = grad.shape
    acc = arrived[peers]
    for d in range(peers + 1, 2 * peers):
        acc = acc + arrived[d]
    others = acc[:own, part : part + 1]
    score = acc[:own, part + 64 : part + 65]
    total = others + jnp.exp(score)
    pull, toward = acc[:own, :part], acc[own:, :part]
    grad[...] = (pull / total - toward * (others / total)) / SHARPNESS
    column = jnp.log(total) - score
    diagonal = iota((own, 128), 0) == iota((own, 128), 1)
    row = jnp.sum(jnp.where(diagonal, column, 0.0), axis=0, keepdims=True)
    loss[...] = row[:, :own]


def body(states, w_in, b_in, w_out, b_out, ln_gain, ln_bias, lengths, neg_ids, neg_count, pos_ids):
    x = states[0]
    rows, width = x.shape
    hid = b_in.shape[0]
    shard = w_in.shape[0]
    part_rows = rows // N_MP
    part = width // N_MP
    n_pass = part_rows // WIN
    own_q = part_rows // QLEN * N_MP
    peers = N_GRP * N_MP
    shape = jax.ShapeDtypeStruct

    packed = pl.pallas_call(
        pack_kernel,
        out_shape=shape((N_Z, 2 * shard, hid), BF),
        in_specs=[HBM] * 2,
        out_specs=VMEM,
        scratch_shapes=[pltpu.SemaphoreType.DMA((2 * N_Z,))],
        compiler_params=params(),
        name="pack",
    )(w_in, w_out.T)
    lines = [lax.all_to_all(packed, ("grp", "zh"), 0, 0, tiled=True)]
    lines = lines + [shift(lines[0], "y", k) for k in (1, 2, 3)]
    lines = lines + [shift(v, "c", 1) for v in lines]
    small = [
        b_out[None],
        ln_gain[None],
        ln_bias[None],
        lengths[None],
        neg_ids,
        neg_count[None],
        pos_ids[None],
    ]
    weights = pltpu.VMEM((N_Z, N_Y * N_C, shard, hid), BF)
    own, s1, s2, s3, *small = pl.pallas_call(
        ffn_kernel,
        out_shape=[shape((part_rows, width), F32)]
        + [shape((part_rows, width), BF)] * 3
        + [shape(v.shape, v.dtype) for v in small],
        in_specs=[HBM] * 2 + [ANY] * 8 + [HBM] * 7,
        out_specs=[VMEM] * 11,
        scratch_shapes=[
            weights,
            weights,
            pltpu.VMEM((rows, width), BF),
            pltpu.VMEM((1, hid), F32),
            pltpu.VMEM((rows, hid), BF),
            pltpu.VMEM((rows, width), F32),
            pltpu.SemaphoreType.DMA((25,)),
        ],
        compiler_params=params(),
        cost_estimate=cost(4 * rows * width * hid, 8 << 20),
        name="ffn",
    )(x, b_in[None], *lines, *small)
    r2, r1, r3 = shift(s2, "mp", 2), shift(s1, "mp", 1), shift(s3, "mp", 3)

    passages, send = pl.pallas_call(
        norm_kernel,
        out_shape=[
            shape((n_pass, width + 128), BF),
            shape((peers, part_rows + 16, part), BF),
        ],
        in_specs=[VMEM] * 11,
        out_specs=[VMEM] * 2,
        compiler_params=params(),
        cost_estimate=cost(2 * part_rows * width * 64, 3 << 20),
        name="norm",
    )(own, r1, r2, r3, *small)

    slab = jnp.concatenate(
        [passages] + [shift(passages, "zh", k) for k in (1, 2, 3)], axis=0
    )
    lines = [slab] + [shift(slab, "y", k) for k in (1, 2, 3)]
    lines = lines + [shift(v, "c", 1) for v in lines]
    arrived = lax.all_to_all(send, ("grp", "mp"), 0, 0, tiled=True)
    encoded, q_all, lists = pl.pallas_call(
        unpack_kernel,
        out_shape=[shape((rows, part), BF), shape((16, width), BF), shape((16, part), F32)],
        in_specs=[VMEM],
        out_specs=[VMEM] * 3,
        compiler_params=params(),
        name="unpack",
    )(arrived)
    shares = pl.pallas_call(
        score_kernel,
        out_shape=shape((peers, 2 * own_q, part + 128), F32),
        in_specs=[VMEM] * 10,
        out_specs=VMEM,
        compiler_params=params(),
        cost_estimate=cost(2 * 1024 * width * 100, 3 << 20),
        name="score",
    )(q_all, lists, *lines)
    arrived = lax.all_to_all(shares, ("grp", "mp"), 0, 0, tiled=True)
    grad, loss = pl.pallas_call(
        final_kernel,
        out_shape=[shape((own_q, part), F32), shape((1, own_q), F32)],
        in_specs=[VMEM],
        out_specs=[VMEM] * 2,
        compiler_params=params(),
        name="final",
    )(arrived)
    return encoded[None], grad, loss.reshape(own_q)


def solution(mesh):
    fine = Mesh(
        mesh.devices.reshape(N_GRP, N_ZH, N_Y, N_C, N_MP), ("grp", "zh", "y", "c", "mp")
    )
    dp = ("zh", "y", "c")
    placed = (
        P("grp", dp, None),
        P(("grp",) + dp, "mp"),
        P("mp"),
        P("mp", ("grp",) + dp),
        P(),
        P(),
        P(),
        P(dp),
        P(dp, None),
        P(dp),
        P(dp),
    )
    return jax.shard_map(
        body,
        mesh=fine,
        in_specs=placed,
        out_specs=(P("grp", dp, "mp"), P(dp, "mp"), P(dp)),
        check_vma=False,
    )
```

time: 130 us -> 123 us (0.946)
  blocking collectives: 0 us -> 33.4 us
  waiting for transfers between devices: 41.5 us -> 24.2 us
  starting transfers between devices: 69.1 us -> 53 us
  local copies, waits for them, and re-layouts: 7.07 us -> 2.25 us
  Pallas kernels: 10.3 us -> 8.62 us
    all_to_all x4 -> x1, starting transfers between devices: 39.6 us -> 5.75 us  [body(): arrived = lax.all_to_all(send, ('grp', 'mp'), 0, 0, tiled=True)]
    all_to_all x0 -> x2, blocking collectives: none -> 33.4 us  [the longest x1 21.9 us: body(): lines = [lax.all_to_all(packed, ('grp', 'zh'), 0, 0, tiled=True)]]
    ppermute x18 -> x20, starting transfers between devices: 27.5 us -> 47.3 us  [shift(): lax.ppermute(block, axis, [(i, (i + distance) % n) for i in range(n)])]
    all_to_all x4 -> x1, waiting for transfers between devices: 15.5 us -> 0.01 us  [body(): arrived = lax.all_to_all(send, ('grp', 'mp'), 0, 0, tiled=True)]
    broadcast_in_dim x6 -> x0, local copies, waits for them, and re-layouts: 2.61 us -> none  [the longest x3 2.38 us: spread(): filled = jnp.broadcast_to(block[None], (n,) + block.shape)]
    ppermute x3 -> x0, starting transfers between devices: 2.01 us -> none  [shift_refresh(): return lax.ppermute(block, ('grp', axis), route)]
    ppermute x18 -> x20, waiting for transfers between devices: 26.1 us -> 24.2 us  [shift(): lax.ppermute(block, axis, [(i, (i + distance) % n) for i in range(n)])]
    pallas_call x4 -> x6, Pallas kernels: 10.3 us -> 8.62 us  [the longest x1 3.64 us: body(): pl.pallas_call(ffn_kernel, out_shape=[shape((part_rows, width), F32)] + [...]
  transfers between devices with their start and end apart: 25 -> 21, of which waited for: 11 -> 8; matrix products, arithmetic and copies ran while one was open for 1% -> 0% of each run, Pallas kernels for 0% -> 1%
where the time goes in v3:
time: 123 us; the launch traced here: 122 us
  starting transfers between devices  53 us (43%)
  blocking collectives  33.4 us (27%)
  waiting for transfers between devices  24.2 us (20%)
  Pallas kernels  8.62 us (7%)
  local copies, waits for them, and re-layouts  2.25 us (2%)
    ppermute x20, starting transfers between devices, shift(): lax.ppermute(block, axis, [(i, (i + distance) % n) for i in range(n)])  47.3 us
    ppermute x20, waiting for transfers between devices, shift(): lax.ppermute(block, axis, [(i, (i + distance) % n) for i in range(n)])  24.2 us
    all_to_all x1, blocking collectives, body(): lines = [lax.all_to_all(packed, ('grp', 'zh'), 0, 0, tiled=True)]  21.9 us
    all_to_all x1, blocking collectives, body(): arrived = lax.all_to_all(shares, ('grp', 'mp'), 0, 0, tiled=True)  11.5 us
    all_to_all x1, starting transfers between devices, body(): arrived = lax.all_to_all(send, ('grp', 'mp'), 0, 0, tiled=True)  5.75 us
    pallas_call x1, Pallas kernels, body(): pl.pallas_call(ffn_kernel, out_shape=[shape((part_rows, width), F32)] + [...  3.64 us
  transfers between devices with their start and end apart: 21, of which 8 were waited for; matrix products, arithmetic and copies ran while one was open for 0% of the time, Pallas kernels for 1%

profile of v3, /device:TPU:1, one launch (start us, length us, event | category | flops | bytes accessed | tf_op | source)
XLA Modules:
  0.0 122.3 jit_solution(14641572888174900333)
XLA Ops:
  0.6 0.7 copy-done
  1.4 0.8 copy-done.1
  2.1 0.8 pack.1
  3.0 21.9 %all_to_all.15.rest_0_ = bf16[8,32,1024]{2,1,0:T(8,128)(2,1)S(1)} all-to-all(bf16[8,32,1024]{2,1,0:T(8,128)(2,1)S(1)} %pack.1), channel_id=1, replica_groups=mesh['grp'=2,'zh'=4,'y'=4,'c'=2,'mp'=4] {'grp','zh'}, dimensions={0} | all-to-all | bytes 1048576 | tf_op jit(solution)/shard_map/all_to_all | solution.py:327
  24.9 2.7 %collective-permute-start.2 = (bf16[8,32,1024]{2,1,0:T(8,128)(2,1)S(1)}, bf16[8,32,1024]{2,1,0:T(8,128)(2,1)S(1)}, u32[]{:S(2)}, u32[]{:S(2)}) collective-permute-start(bf16[8,32,1024]{2,1,0:T(8,128)(2,1)S(1)} %all_to_all.15.rest_0_), channel_id=1, source_target_pairs={{0,24},{8,0},{16,8},{24,16},{1,25},{9,1},{17,9},{25,17},{2,26},{10... | collective-permute-start | bytes 1572872 | tf_op jit(solution)/shard_map/ppermute | solution.py:39
  28.7 4.0 %collective-permute-start.3 = (bf16[8,32,1024]{2,1,0:T(8,128)(2,1)S(1)}, bf16[8,32,1024]{2,1,0:T(8,128)(2,1)S(1)}, u32[]{:S(2)}, u32[]{:S(2)}) collective-permute-start(bf16[8,32,1024]{2,1,0:T(8,128)(2,1)S(1)} %all_to_all.15.rest_0_), channel_id=1, source_target_pairs={{0,4},{4,0},{1,5},{5,1},{2,6},{6,2},{3,7},{7,3},{8,12},{12,8},{9,1... | collective-permute-start | bytes 1572872 | tf_op jit(solution)/shard_map/ppermute | solution.py:39
  32.7 4.1 %collective-permute-done.2.rest_3_ = bf16[8,32,1024]{2,1,0:T(8,128)(2,1)S(1)} collective-permute-done((bf16[8,32,1024]{2,1,0:T(8,128)(2,1)S(1)}, bf16[8,32,1024]{2,1,0:T(8,128)(2,1)S(1)}, u32[]{:S(2)}, u32[]{:S(2)}) %collective-permute-start.2) | collective-permute-done | bytes 524320 | tf_op jit(solution)/shard_map/ppermute | solution.py:39
  36.7 14.3 %collective-permute-start.6 = (bf16[8,32,1024]{2,1,0:T(8,128)(2,1)S(1)}, bf16[8,32,1024]{2,1,0:T(8,128)(2,1)S(1)}, u32[]{:S(2)}, u32[]{:S(2)}) collective-permute-start(bf16[8,32,1024]{2,1,0:T(8,128)(2,1)S(1)} %collective-permute-done.2.rest_3_), channel_id=1, source_target_pairs={{0,4},{4,0},{1,5},{5,1},{2,6},{6,2},{3,7},{7,3},{8,12},{12,8},{9,1... | collective-permute-start | bytes 1572872 | tf_op jit(solution)/shard_map/ppermute | solution.py:39
  51.0 3.2 %collective-permute-done.rest_1_ = bf16[8,32,1024]{2,1,0:T(8,128)(2,1)S(1)} collective-permute-done((bf16[8,32,1024]{2,1,0:T(8,128)(2,1)S(1)}, bf16[8,32,1024]{2,1,0:T(8,128)(2,1)S(1)}, u32[]{:S(2)}, u32[]{:S(2)}) %collective-permute-start) | collective-permute-done | bytes 524320 | tf_op jit(solution)/shard_map/ppermute | solution.py:39
  54.7 1.5 %collective-permute-done.4.rest_5_ = bf16[8,32,1024]{2,1,0:T(8,128)(2,1)S(1)} collective-permute-done((bf16[8,32,1024]{2,1,0:T(8,128)(2,1)S(1)}, bf16[8,32,1024]{2,1,0:T(8,128)(2,1)S(1)}, u32[]{:S(2)}, u32[]{:S(2)}) %collective-permute-start.4) | collective-permute-done | bytes 524320 | tf_op jit(solution)/shard_map/ppermute | solution.py:39
  57.0 3.6 %ffn.1 = (f32[128,1024]{1,0:T(8,128)S(1)}, bf16[128,1024]{1,0:T(8,128)(2,1)S(1)}, bf16[128,1024]{1,0:T(8,128)(2,1)S(1)}, bf16[128,1024]{1,0:T(8,128)(2,1)S(1)}, ...) custom-call(bf16[512,1024]{1,0:T(8,128)(2,1)S(1)} %bitcast.12, ...), custom_call_target="tpu_custom_call" | custom-call | flops 2147483648 | bytes 8388608 | tf_op jit(solution)/shard_map/ffn/pallas_call | solution.py:340
  60.6 1.3 %collective-permute-start.7 = (bf16[128,1024]{1,0:T(8,128)(2,1)S(1)}, bf16[128,1024]{1,0:T(8,128)(2,1)S(1)}, u32[]{:S(2)}, u32[]{:S(2)}) collective-permute-start(bf16[128,1024]{1,0:T(8,128)(2,1)S(1)} %get-tuple-element.22), channel_id=1, source_target_pairs={{0,1},{1,2},{2,3},{3,0},{4,5},{5,6},{6,7},{7,4},{8,9},{9,10},{10,1... | collective-permute-start | bytes 786440 | tf_op jit(solution)/shard_map/ppermute | solution.py:39
  61.9 2.5 %collective-permute-start.8 = (bf16[128,1024]{1,0:T(8,128)(2,1)S(1)}, bf16[128,1024]{1,0:T(8,128)(2,1)S(1)}, u32[]{:S(2)}, u32[]{:S(2)}) collective-permute-start(bf16[128,1024]{1,0:T(8,128)(2,1)S(1)} %get-tuple-element.23), channel_id=1, source_target_pairs={{0,2},{1,3},{2,0},{3,1},{4,6},{5,7},{6,4},{7,5},{8,10},{9,11},{10,... | collective-permute-start | bytes 786440 | tf_op jit(solution)/shard_map/ppermute | solution.py:39
  64.4 1.2 collective-permute-start.9
  65.5 3.9 %collective-permute-done.7.r1 = bf16[128,1024]{1,0:T(8,128)(2,1)S(1)} collective-permute-done((bf16[128,1024]{1,0:T(8,128)(2,1)S(1)}, bf16[128,1024]{1,0:T(8,128)(2,1)S(1)}, u32[]{:S(2)}, u32[]{:S(2)}) %collective-permute-start.7) | collective-permute-done | bytes 262176 | tf_op jit(solution)/shard_map/ppermute | solution.py:39
  69.4 6.6 %collective-permute-done.8.r2 = bf16[128,1024]{1,0:T(8,128)(2,1)S(1)} collective-permute-done((bf16[128,1024]{1,0:T(8,128)(2,1)S(1)}, bf16[128,1024]{1,0:T(8,128)(2,1)S(1)}, u32[]{:S(2)}, u32[]{:S(2)}) %collective-permute-start.8) | collective-permute-done | bytes 262176 | tf_op jit(solution)/shard_map/ppermute | solution.py:39
  76.0 1.6 %norm.1 = (bf16[32,1152]{1,0:T(8,128)(2,1)S(1)}, bf16[8,144,256]{2,1,0:T(8,128)(2,1)}) custom-call(f32[128,1024]{1,0:T(8,128)S(1)} %get-tuple-element.21.own, bf16[128,1024]{1,0:T(8,128)(2,1)S(1)} %collective-permute-done.7.r1, bf16[128,1024]{1,0:T(8,128)(2,1)S(1)} %collective-permute-done.8.r2, bf16[128,1024]{1,0:T(8,128)(2,1)S(1)} %collective-permute-done.9.r3, ...), custom_call_target="tpu_custom_call" | custom-call | flops 16777216 | bytes 3145728 | tf_op jit(solution)/shard_map/norm/pallas_call | solution.py:362
  77.6 2.9 %collective-permute-start.12 = (bf16[32,1152]{1,0:T(8,128)(2,1)S(1)}, bf16[32,1152]{1,0:T(8,128)(2,1)S(1)}, u32[]{:S(2)}, u32[]{:S(2)}) collective-permute-start(bf16[32,1152]{1,0:T(8,128)(2,1)S(1)} %get-tuple-element.36), channel_id=1, source_target_pairs={{0,96},{32,0},{64,32},{96,64},{1,97},{33,1},{65,33},{97,65},{2,98}... | collective-permute-start | bytes 221192 | tf_op jit(solution)/shard_map/ppermute | solution.py:39
  80.5 1.1 collective-permute-start.11
  81.6 2.0 %collective-permute-start.10 = (bf16[32,1152]{1,0:T(8,128)(2,1)S(1)}, bf16[32,1152]{1,0:T(8,128)(2,1)S(1)}, u32[]{:S(2)}, u32[]{:S(2)}) collective-permute-start(bf16[32,1152]{1,0:T(8,128)(2,1)S(1)} %get-tuple-element.36), channel_id=1, source_target_pairs={{0,32},{32,64},{64,96},{96,0},{1,33},{33,65},{65,97},{97,1},{2,34}... | collective-permute-start | bytes 221192 | tf_op jit(solution)/shard_map/ppermute | solution.py:39
  83.6 5.7 %all-to-all-start.1 = ((bf16[8,144,256]{2,1,0:T(8,128)(2,1)}), bf16[8,144,256]{2,1,0:T(8,128)(2,1)S(1)}, u32[]{:S(2)}, u32[]{:S(2)}) async-start(bf16[8,144,256]{2,1,0:T(8,128)(2,1)} %get-tuple-element.32), calls=%async_computation.1 | async-start | bytes 1179648 | tf_op jit(solution)/shard_map/all_to_all | solution.py:380
  89.4 1.3 %collective-permute-start.15 = (bf16[128,1152]{1,0:T(8,128)(2,1)S(1)}, bf16[128,1152]{1,0:T(8,128)(2,1)S(1)}, u32[]{:S(2)}, u32[]{:S(2)}) collective-permute-start(bf16[128,1152]{1,0:T(8,128)(2,1)S(1)} %constant_dynamic-update-slice_fusion.rest_0_), channel_id=1, source_target_pairs={{0,24},{8,0},{16,8},{24,16},{1,25},{9,1},{17,9},{25,17},{2,26},{10... | collective-permute-start | bytes 884744 | tf_op jit(solution)/shard_map/ppermute | solution.py:39
  91.4 2.6 %collective-permute-start.16 = (bf16[128,1152]{1,0:T(8,128)(2,1)S(1)}, bf16[128,1152]{1,0:T(8,128)(2,1)S(1)}, u32[]{:S(2)}, u32[]{:S(2)}) collective-permute-start(bf16[128,1152]{1,0:T(8,128)(2,1)S(1)} %constant_dynamic-update-slice_fusion.rest_0_), channel_id=1, source_target_pairs={{0,4},{4,0},{1,5},{5,1},{2,6},{6,2},{3,7},{7,3},{8,12},{12,8},{9,1... | collective-permute-start | bytes 884744 | tf_op jit(solution)/shard_map/ppermute | solution.py:39
  94.0 2.0 %collective-permute-done.15.rest_3_ = bf16[128,1152]{1,0:T(8,128)(2,1)S(1)} collective-permute-done((bf16[128,1152]{1,0:T(8,128)(2,1)S(1)}, bf16[128,1152]{1,0:T(8,128)(2,1)S(1)}, u32[]{:S(2)}, u32[]{:S(2)}) %collective-permute-start.15) | collective-permute-done | bytes 294944 | tf_op jit(solution)/shard_map/ppermute | solution.py:39
  96.0 5.5 %collective-permute-start.19 = (bf16[128,1152]{1,0:T(8,128)(2,1)S(1)}, bf16[128,1152]{1,0:T(8,128)(2,1)S(1)}, u32[]{:S(2)}, u32[]{:S(2)}) collective-permute-start(bf16[128,1152]{1,0:T(8,128)(2,1)S(1)} %collective-permute-done.15.rest_3_), channel_id=1, source_target_pairs={{0,4},{4,0},{1,5},{5,1},{2,6},{6,2},{3,7},{7,3},{8,12},{12,8},{9,1... | collective-permute-start | bytes 884744 | tf_op jit(solution)/shard_map/ppermute | solution.py:39
  101.5 3.0 %collective-permute-start.18 = (bf16[128,1152]{1,0:T(8,128)(2,1)S(1)}, bf16[128,1152]{1,0:T(8,128)(2,1)S(1)}, u32[]{:S(2)}, u32[]{:S(2)}) collective-permute-start(bf16[128,1152]{1,0:T(8,128)(2,1)S(1)} %collective-permute-done.14.rest_2_), channel_id=1, source_target_pairs={{0,4},{4,0},{1,5},{5,1},{2,6},{6,2},{3,7},{7,3},{8,12},{12,8},{9,1... | collective-permute-start | bytes 884744 | tf_op jit(solution)/shard_map/ppermute | solution.py:39
  104.5 2.4 %collective-permute-done.13.rest_1_ = bf16[128,1152]{1,0:T(8,128)(2,1)S(1)} collective-permute-done((bf16[128,1152]{1,0:T(8,128)(2,1)S(1)}, bf16[128,1152]{1,0:T(8,128)(2,1)S(1)}, u32[]{:S(2)}, u32[]{:S(2)}) %collective-permute-start.13) | collective-permute-done | bytes 294944 | tf_op jit(solution)/shard_map/ppermute | solution.py:39
  106.8 0.8 collective-permute-start.17
  107.7 0.7 unpack.1
  108.9 1.1 score.1
  110.0 11.5 %all_to_all.16.arrived = f32[8,16,384]{2,1,0:T(8,128)S(1)} all-to-all(f32[8,16,384]{2,1,0:T(8,128)S(1)} %score.1), channel_id=1, replica_groups=mesh['grp'=2,'zh'=4,'y'=4,'c'=2,'mp'=4] {'grp','mp'}, dimensions={0} | all-to-all | bytes 393216 | tf_op jit(solution)/shard_map/all_to_all | solution.py:398
  121.5 0.8 final.1
  (44 shorter events, 3.4 us)
Async XLA Ops:
  0.6 0.8 copy-start
  1.4 0.8 copy-start.1
  2.1 54.1 %copy-start.2 = (bf16[1,512,1024]{2,1,0:T(8,128)(2,1)S(1)}, bf16[1,512,1024]{2,1,0:T(8,128)(2,1)}, u32[]{:S(2)}) copy-start(bf16[1,512,1024]{2,1,0:T(8,128)(2,1)} %param.11) | copy-start | bytes 3145732
  3.0 53.3 %copy-start.5 = (f32[1024]{0:T(1024)S(1)}, f32[1024]{0:T(1024)}, u32[]{:S(2)}) copy-start(f32[1024]{0:T(1024)} %param.16) | copy-start | bytes 12292
  3.0 53.3 %copy-start.6 = (f32[1024]{0:T(1024)S(1)}, f32[1024]{0:T(1024)}, u32[]{:S(2)}) copy-start(f32[1024]{0:T(1024)} %param.17) | copy-start | bytes 12292
  3.0 53.3 %copy-start.7 = (s32[8,32]{1,0:T(8,128)S(1)}, s32[8,32]{1,0:T(8,128)}, u32[]{:S(2)}) copy-start(s32[8,32]{1,0:T(8,128)} %rest_12_.1) | copy-start | bytes 3076
  3.0 53.3 %copy-start.10 = (s32[8]{0:T(128)S(1)}, s32[8]{0:T(128)}, u32[]{:S(2)}) copy-start(s32[8]{0:T(128)} %param.21) | copy-start | bytes 100
  24.9 11.8 %collective-permute-start.2 = (bf16[8,32,1024]{2,1,0:T(8,128)(2,1)S(1)}, bf16[8,32,1024]{2,1,0:T(8,128)(2,1)S(1)}, u32[]{:S(2)}, u32[]{:S(2)}) collective-permute-start(bf16[8,32,1024]{2,1,0:T(8,128)(2,1)S(1)} %all_to_all.15.rest_0_), channel_id=1, source_target_pairs={{0,24},{8,0},{16,8},{24,16},{1,25},{9,1},{17,9},{25,17},{2,26},{10... | collective-permute-start | bytes 1572872 | tf_op jit(solution)/shard_map/ppermute | solution.py:39
  27.6 23.4 %collective-permute-start.1 = (bf16[8,32,1024]{2,1,0:T(8,128)(2,1)S(1)}, bf16[8,32,1024]{2,1,0:T(8,128)(2,1)S(1)}, u32[]{:S(2)}, u32[]{:S(2)}) collective-permute-start(bf16[8,32,1024]{2,1,0:T(8,128)(2,1)S(1)} %all_to_all.15.rest_0_), channel_id=1, source_target_pairs={{0,16},{8,24},{16,0},{24,8},{1,17},{9,25},{17,1},{25,9},{2,18},{10... | collective-permute-start | bytes 1572872 | tf_op jit(solution)/shard_map/ppermute | solution.py:39
  28.0 26.2 %collective-permute-start = (bf16[8,32,1024]{2,1,0:T(8,128)(2,1)S(1)}, bf16[8,32,1024]{2,1,0:T(8,128)(2,1)S(1)}, u32[]{:S(2)}, u32[]{:S(2)}) collective-permute-start(bf16[8,32,1024]{2,1,0:T(8,128)(2,1)S(1)} %all_to_all.15.rest_0_), channel_id=1, source_target_pairs={{0,8},{8,16},{16,24},{24,0},{1,9},{9,17},{17,25},{25,1},{2,10},{10... | collective-permute-start | bytes 1572872 | tf_op jit(solution)/shard_map/ppermute | solution.py:39
  28.7 26.0 %collective-permute-start.3 = (bf16[8,32,1024]{2,1,0:T(8,128)(2,1)S(1)}, bf16[8,32,1024]{2,1,0:T(8,128)(2,1)S(1)}, u32[]{:S(2)}, u32[]{:S(2)}) collective-permute-start(bf16[8,32,1024]{2,1,0:T(8,128)(2,1)S(1)} %all_to_all.15.rest_0_), channel_id=1, source_target_pairs={{0,4},{4,0},{1,5},{5,1},{2,6},{6,2},{3,7},{7,3},{8,12},{12,8},{9,1... | collective-permute-start | bytes 1572872 | tf_op jit(solution)/shard_map/ppermute | solution.py:39
  36.7 18.0 %collective-permute-start.6 = (bf16[8,32,1024]{2,1,0:T(8,128)(2,1)S(1)}, bf16[8,32,1024]{2,1,0:T(8,128)(2,1)S(1)}, u32[]{:S(2)}, u32[]{:S(2)}) collective-permute-start(bf16[8,32,1024]{2,1,0:T(8,128)(2,1)S(1)} %collective-permute-done.2.rest_3_), channel_id=1, source_target_pairs={{0,4},{4,0},{1,5},{5,1},{2,6},{6,2},{3,7},{7,3},{8,12},{12,8},{9,1... | collective-permute-start | bytes 1572872 | tf_op jit(solution)/shard_map/ppermute | solution.py:39
  51.0 3.7 %collective-permute-start.5 = (bf16[8,32,1024]{2,1,0:T(8,128)(2,1)S(1)}, bf16[8,32,1024]{2,1,0:T(8,128)(2,1)S(1)}, u32[]{:S(2)}, u32[]{:S(2)}) collective-permute-start(bf16[8,32,1024]{2,1,0:T(8,128)(2,1)S(1)} %collective-permute-done.1.rest_2_), channel_id=1, source_target_pairs={{0,4},{4,0},{1,5},{5,1},{2,6},{6,2},{3,7},{7,3},{8,12},{12,8},{9,1... | collective-permute-start | bytes 1572872 | tf_op jit(solution)/shard_map/ppermute | solution.py:39
  54.2 2.0 %collective-permute-start.4 = (bf16[8,32,1024]{2,1,0:T(8,128)(2,1)S(1)}, bf16[8,32,1024]{2,1,0:T(8,128)(2,1)S(1)}, u32[]{:S(2)}, u32[]{:S(2)}) collective-permute-start(bf16[8,32,1024]{2,1,0:T(8,128)(2,1)S(1)} %collective-permute-done.rest_1_), channel_id=1, source_target_pairs={{0,4},{4,0},{1,5},{5,1},{2,6},{6,2},{3,7},{7,3},{8,12},{12,8},{9,1... | collective-permute-start | bytes 1572872 | tf_op jit(solution)/shard_map/ppermute | solution.py:39
  56.3 0.7 copy-start.4
  56.3 0.7 copy-start.3
  56.3 0.7 copy-start.8
  56.3 0.7 copy-start.9
  60.6 8.8 %collective-permute-start.7 = (bf16[128,1024]{1,0:T(8,128)(2,1)S(1)}, bf16[128,1024]{1,0:T(8,128)(2,1)S(1)}, u32[]{:S(2)}, u32[]{:S(2)}) collective-permute-start(bf16[128,1024]{1,0:T(8,128)(2,1)S(1)} %get-tuple-element.22), channel_id=1, source_target_pairs={{0,1},{1,2},{2,3},{3,0},{4,5},{5,6},{6,7},{7,4},{8,9},{9,10},{10,1... | collective-permute-start | bytes 786440 | tf_op jit(solution)/shard_map/ppermute | solution.py:39
  61.9 14.1 %collective-permute-start.8 = (bf16[128,1024]{1,0:T(8,128)(2,1)S(1)}, bf16[128,1024]{1,0:T(8,128)(2,1)S(1)}, u32[]{:S(2)}, u32[]{:S(2)}) collective-permute-start(bf16[128,1024]{1,0:T(8,128)(2,1)S(1)} %get-tuple-element.23), channel_id=1, source_target_pairs={{0,2},{1,3},{2,0},{3,1},{4,6},{5,7},{6,4},{7,5},{8,10},{9,11},{10,... | collective-permute-start | bytes 786440 | tf_op jit(solution)/shard_map/ppermute | solution.py:39
  64.4 11.7 %collective-permute-start.9 = (bf16[128,1024]{1,0:T(8,128)(2,1)S(1)}, bf16[128,1024]{1,0:T(8,128)(2,1)S(1)}, u32[]{:S(2)}, u32[]{:S(2)}) collective-permute-start(bf16[128,1024]{1,0:T(8,128)(2,1)S(1)} %get-tuple-element.24), channel_id=1, source_target_pairs={{0,3},{1,0},{2,1},{3,2},{4,7},{5,4},{6,5},{7,6},{8,11},{9,8},{10,9... | collective-permute-start | bytes 786440 | tf_op jit(solution)/shard_map/ppermute | solution.py:39
  77.6 11.8 %collective-permute-start.12 = (bf16[32,1152]{1,0:T(8,128)(2,1)S(1)}, bf16[32,1152]{1,0:T(8,128)(2,1)S(1)}, u32[]{:S(2)}, u32[]{:S(2)}) collective-permute-start(bf16[32,1152]{1,0:T(8,128)(2,1)S(1)} %get-tuple-element.36), channel_id=1, source_target_pairs={{0,96},{32,0},{64,32},{96,64},{1,97},{33,1},{65,33},{97,65},{2,98}... | collective-permute-start | bytes 221192 | tf_op jit(solution)/shard_map/ppermute | solution.py:39
  80.5 8.9 %collective-permute-start.11 = (bf16[32,1152]{1,0:T(8,128)(2,1)S(1)}, bf16[32,1152]{1,0:T(8,128)(2,1)S(1)}, u32[]{:S(2)}, u32[]{:S(2)}) collective-permute-start(bf16[32,1152]{1,0:T(8,128)(2,1)S(1)} %get-tuple-element.36), channel_id=1, source_target_pairs={{0,64},{32,96},{64,0},{96,32},{1,65},{33,97},{65,1},{97,33},{2,66}... | collective-permute-start | bytes 221192 | tf_op jit(solution)/shard_map/ppermute | solution.py:39
  81.6 7.8 %collective-permute-start.10 = (bf16[32,1152]{1,0:T(8,128)(2,1)S(1)}, bf16[32,1152]{1,0:T(8,128)(2,1)S(1)}, u32[]{:S(2)}, u32[]{:S(2)}) collective-permute-start(bf16[32,1152]{1,0:T(8,128)(2,1)S(1)} %get-tuple-element.36), channel_id=1, source_target_pairs={{0,32},{32,64},{64,96},{96,0},{1,33},{33,65},{65,97},{97,1},{2,34}... | collective-permute-start | bytes 221192 | tf_op jit(solution)/shard_map/ppermute | solution.py:39
  83.6 24.1 %all-to-all-start.1 = ((bf16[8,144,256]{2,1,0:T(8,128)(2,1)}), bf16[8,144,256]{2,1,0:T(8,128)(2,1)S(1)}, u32[]{:S(2)}, u32[]{:S(2)}) async-start(bf16[8,144,256]{2,1,0:T(8,128)(2,1)} %get-tuple-element.32), calls=%async_computation.1 | async-start | bytes 1179648 | tf_op jit(solution)/shard_map/all_to_all | solution.py:380
  89.4 6.6 %collective-permute-start.15 = (bf16[128,1152]{1,0:T(8,128)(2,1)S(1)}, bf16[128,1152]{1,0:T(8,128)(2,1)S(1)}, u32[]{:S(2)}, u32[]{:S(2)}) collective-permute-start(bf16[128,1152]{1,0:T(8,128)(2,1)S(1)} %constant_dynamic-update-slice_fusion.rest_0_), channel_id=1, source_target_pairs={{0,24},{8,0},{16,8},{24,16},{1,25},{9,1},{17,9},{25,17},{2,26},{10... | collective-permute-start | bytes 884744 | tf_op jit(solution)/shard_map/ppermute | solution.py:39
  90.7 10.8 %collective-permute-start.14 = (bf16[128,1152]{1,0:T(8,128)(2,1)S(1)}, bf16[128,1152]{1,0:T(8,128)(2,1)S(1)}, u32[]{:S(2)}, u32[]{:S(2)}) collective-permute-start(bf16[128,1152]{1,0:T(8,128)(2,1)S(1)} %constant_dynamic-update-slice_fusion.rest_0_), channel_id=1, source_target_pairs={{0,16},{8,24},{16,0},{24,8},{1,17},{9,25},{17,1},{25,9},{2,18},{10... | collective-permute-start | bytes 884744 | tf_op jit(solution)/shard_map/ppermute | solution.py:39
  90.7 16.1 %collective-permute-start.13 = (bf16[128,1152]{1,0:T(8,128)(2,1)S(1)}, bf16[128,1152]{1,0:T(8,128)(2,1)S(1)}, u32[]{:S(2)}, u32[]{:S(2)}) collective-permute-start(bf16[128,1152]{1,0:T(8,128)(2,1)S(1)} %constant_dynamic-update-slice_fusion.rest_0_), channel_id=1, source_target_pairs={{0,8},{8,16},{16,24},{24,0},{1,9},{9,17},{17,25},{25,1},{2,10},{10... | collective-permute-start | bytes 884744 | tf_op jit(solution)/shard_map/ppermute | solution.py:39
  91.4 17.0 %collective-permute-start.16 = (bf16[128,1152]{1,0:T(8,128)(2,1)S(1)}, bf16[128,1152]{1,0:T(8,128)(2,1)S(1)}, u32[]{:S(2)}, u32[]{:S(2)}) collective-permute-start(bf16[128,1152]{1,0:T(8,128)(2,1)S(1)} %constant_dynamic-update-slice_fusion.rest_0_), channel_id=1, source_target_pairs={{0,4},{4,0},{1,5},{5,1},{2,6},{6,2},{3,7},{7,3},{8,12},{12,8},{9,1... | collective-permute-start | bytes 884744 | tf_op jit(solution)/shard_map/ppermute | solution.py:39
  96.0 12.4 %collective-permute-start.19 = (bf16[128,1152]{1,0:T(8,128)(2,1)S(1)}, bf16[128,1152]{1,0:T(8,128)(2,1)S(1)}, u32[]{:S(2)}, u32[]{:S(2)}) collective-permute-start(bf16[128,1152]{1,0:T(8,128)(2,1)S(1)} %collective-permute-done.15.rest_3_), channel_id=1, source_target_pairs={{0,4},{4,0},{1,5},{5,1},{2,6},{6,2},{3,7},{7,3},{8,12},{12,8},{9,1... | collective-permute-start | bytes 884744 | tf_op jit(solution)/shard_map/ppermute | solution.py:39
  101.5 7.0 %collective-permute-start.18 = (bf16[128,1152]{1,0:T(8,128)(2,1)S(1)}, bf16[128,1152]{1,0:T(8,128)(2,1)S(1)}, u32[]{:S(2)}, u32[]{:S(2)}) collective-permute-start(bf16[128,1152]{1,0:T(8,128)(2,1)S(1)} %collective-permute-done.14.rest_2_), channel_id=1, source_target_pairs={{0,4},{4,0},{1,5},{5,1},{2,6},{6,2},{3,7},{7,3},{8,12},{12,8},{9,1... | collective-permute-start | bytes 884744 | tf_op jit(solution)/shard_map/ppermute | solution.py:39
  106.8 2.1 %collective-permute-start.17 = (bf16[128,1152]{1,0:T(8,128)(2,1)S(1)}, bf16[128,1152]{1,0:T(8,128)(2,1)S(1)}, u32[]{:S(2)}, u32[]{:S(2)}) collective-permute-start(bf16[128,1152]{1,0:T(8,128)(2,1)S(1)} %collective-permute-done.13.rest_1_), channel_id=1, source_target_pairs={{0,4},{4,0},{1,5},{5,1},{2,6},{6,2},{3,7},{7,3},{8,12},{12,8},{9,1... | collective-permute-start | bytes 884744 | tf_op jit(solution)/shard_map/ppermute | solution.py:39

commit v4 on v3

--- a/solution.py
+++ b/solution.py
@@ -39,6 +39,23 @@
     return lax.ppermute(block, axis, [(i, (i + distance) % n) for i in range(n)])
 
 
+def cross(block, up):
+    route = []
+    for i in range(N_ZH):
+        j = i if up else (i - 1) % N_ZH
+        route += [(i, N_ZH + j), (N_ZH + j, i)]
+    return lax.ppermute(block, ("grp", "zh"), route)
+
+
+def reroute(block, target):
+    route = []
+    for g in range(N_GRP):
+        for z in range(N_ZH):
+            to_g, to_z = target(g, z)
+            route.append((g * N_ZH + z, to_g * N_ZH + to_z % N_ZH))
+    return lax.ppermute(block, ("grp", "zh"), route)
+
+
 def at(axis):
     return lax.axis_index(axis)
 
@@ -66,39 +83,36 @@
 
 
 def slots():
-    y, c = at("y"), at("c")
+    g, y, c = at("grp"), at("y"), at("c")
     found = []
     for other in range(N_C):
         core = c if other == 0 else 1 - c
-        for k in range(N_Y):
-            found.append(lax.rem(y - k + N_Y, N_Y) * N_C + core)
+        for far in range(N_GRP):
+            group = g if far == 0 else 1 - g
+            for k in range(N_Y):
+                found.append((group, lax.rem(y - k + N_Y, N_Y) * N_C + core))
     return found
 
 
 def ffn_kernel(x_any, b_any, *rest):
-    sources, small = rest[:8], rest[8:15]
-    own_ref, s1, s2, s3 = rest[15:19]
-    small_out = rest[19:26]
-    w1, w2, x_ref, b_ref, hidden, total, sems = rest[26:]
+    sources, small = rest[:16], rest[16:23]
+    own_ref, s1, s2, s3 = rest[23:27]
+    small_out = rest[27:34]
+    w, x_ref, b_ref, hidden, total, sems = rest[34:]
     m = at("mp")
     hid = hidden.shape[1]
-    shard = w1.shape[2]
+    shard = w.shape[3] // 2
     early = [
-        pltpu.make_async_copy(x_any, x_ref, sems.at[16]),
-        pltpu.make_async_copy(b_any, b_ref, sems.at[17]),
+        pltpu.make_async_copy(x_any, x_ref, sems.at[32]),
+        pltpu.make_async_copy(b_any, b_ref, sems.at[33]),
     ]
     late = []
-    for i, slot in enumerate(slots()):
+    for i, (group, slot) in enumerate(slots()):
         early.append(
-            pltpu.make_async_copy(sources[i].at[:, 0:shard], w1.at[:, slot], sems.at[2 * i])
-        )
-        late.append(
-            pltpu.make_async_copy(
-                sources[i].at[:, shard : 2 * shard], w2.at[:, slot], sems.at[2 * i + 1]
-            )
+            pltpu.make_async_copy(sources[i], w.at[group, :, slot], sems.at[i])
         )
     for i, (source, target) in enumerate(zip(small, small_out)):
-        late.append(pltpu.make_async_copy(source, target, sems.at[18 + i]))
+        late.append(pltpu.make_async_copy(source, target, sems.at[34 + i]))
     for copy in early + late:
         copy.start()
     for copy in early:
@@ -107,16 +121,18 @@
     tile = 256
     for t in range(hid // tile):
         cols = slice(t * tile, (t + 1) * tile)
-        w = w1[:, :, :, cols].reshape(depth, tile)
-        pre = jnp.dot(x_ref[...], w, preferred_element_type=F32) + b_ref[:, cols]
+        w_in = w[:, :, :, 0:shard, cols].reshape(depth, tile)
+        pre = jnp.dot(x_ref[...], w_in, preferred_element_type=F32) + b_ref[:, cols]
         hidden[:, cols] = (0.5 * pre * (1.0 + lax.erf(pre * np.float32(0.5**0.5)))).astype(BF)
     for copy in late:
         copy.wait()
-    planes = tile // (w2.shape[1] * w2.shape[2])
+    planes = tile // (w.shape[2] * shard)
+    per_group = w.shape[1] // planes
     for t in range(total.shape[1] // tile):
-        w = w2[t * planes : (t + 1) * planes].reshape(tile, hid)
+        begin = t % per_group * planes
+        w_out = w[t // per_group, begin : begin + planes, :, shard:, :].reshape(tile, hid)
         total[:, t * tile : (t + 1) * tile] = lax.dot_general(
-            hidden[...], w, NT, preferred_element_type=F32
+            hidden[...], w_out, NT, preferred_element_type=F32
         )
     rows = own_ref.shape[0]
     for k, out in ((2, s2), (1, s1), (3, s3), (0, own_ref)):
@@ -224,10 +240,10 @@
 
 def score_kernel(q_ref, lists_ref, *rest):
     blocks, out = rest[:-1], rest[-1]
-    zh, y, c, m = at("zh"), at("y"), at("c"), at("mp")
+    g, zh, y, c, m = at("grp"), at("zh"), at("y"), at("c"), at("mp")
     size = blocks[0].shape[0]
     width = q_ref.shape[1]
-    each = size // N_ZH
+    each = size // N_GRP
     n_q = out.shape[1] // 2
     q = q_ref[...]
     qf = q.astype(F32)
@@ -255,7 +271,8 @@
     per_core = size * N_Y
     core = lax.rem(c + lane // per_core, N_C)
     line = lax.rem(y - lax.rem(lane, per_core) // size + N_Y, N_Y)
-    slab = lax.rem(zh - lax.rem(lane, size) // each + N_ZH, N_ZH)
+    piece = lax.rem(lane, size) // each
+    slab = lax.rem(zh + g * piece + (1 - g) * (N_ZH - 1) * (1 + piece), N_ZH)
     number = ((slab * N_Y + line) * N_C + core) * (each * N_MP) + m * each + lax.rem(lane, each)
     number = number.astype(F32)
     match = jnp.where(pos == number, 1.0, 0.0).astype(F32)
@@ -287,10 +304,9 @@
 
 
 def final_kernel(arrived, grad, loss):
-    peers = arrived.shape[0] // N_GRP
     own, part = grad.shape
-    acc = arrived[peers]
-    for d in range(peers + 1, 2 * peers):
+    acc = arrived[0]
+    for d in range(1, arrived.shape[0]):
         acc = acc + arrived[d]
     others = acc[:own, part : part + 1]
     score = acc[:own, part + 64 : part + 65]
@@ -317,15 +333,16 @@
 
     packed = pl.pallas_call(
         pack_kernel,
-        out_shape=shape((N_Z, 2 * shard, hid), BF),
+        out_shape=shape((N_ZH, 2 * shard, hid), BF),
         in_specs=[HBM] * 2,
         out_specs=VMEM,
-        scratch_shapes=[pltpu.SemaphoreType.DMA((2 * N_Z,))],
+        scratch_shapes=[pltpu.SemaphoreType.DMA((2 * N_ZH,))],
         compiler_params=params(),
         name="pack",
     )(w_in, w_out.T)
-    lines = [lax.all_to_all(packed, ("grp", "zh"), 0, 0, tiled=True)]
+    lines = [lax.all_to_all(packed, "zh", 0, 0, tiled=True)]
     lines = lines + [shift(lines[0], "y", k) for k in (1, 2, 3)]
+    lines = lines + [cross(v, k % 2 == 0) for k, v in enumerate(lines)]
     lines = lines + [shift(v, "c", 1) for v in lines]
     small = [
         b_out[None],
@@ -336,22 +353,21 @@
         neg_count[None],
         pos_ids[None],
     ]
-    weights = pltpu.VMEM((N_Z, N_Y * N_C, shard, hid), BF)
+    weights = pltpu.VMEM((N_GRP, N_ZH, N_Y * N_C, 2 * shard, hid), BF)
     own, s1, s2, s3, *small = pl.pallas_call(
         ffn_kernel,
         out_shape=[shape((part_rows, width), F32)]
         + [shape((part_rows, width), BF)] * 3
         + [shape(v.shape, v.dtype) for v in small],
-        in_specs=[HBM] * 2 + [ANY] * 8 + [HBM] * 7,
+        in_specs=[HBM] * 2 + [ANY] * 16 + [HBM] * 7,
         out_specs=[VMEM] * 11,
         scratch_shapes=[
-            weights,
             weights,
             pltpu.VMEM((rows, width), BF),
             pltpu.VMEM((1, hid), F32),
             pltpu.VMEM((rows, hid), BF),
             pltpu.VMEM((rows, width), F32),
-            pltpu.SemaphoreType.DMA((25,)),
+            pltpu.SemaphoreType.DMA((41,)),
         ],
         compiler_params=params(),
         cost_estimate=cost(4 * rows * width * hid, 8 << 20),
@@ -372,8 +388,12 @@
         name="norm",
     )(own, r1, r2, r3, *small)
 
+    far = reroute(passages, lambda g, z: (1 - g, z - 2 if g else z + 2))
+    mid = reroute(passages, lambda g, z: (g, z - 1))
+    near = reroute(passages, lambda g, z: (1 - g, z + 1 if g else z - 1))
+    refresh = at("grp") == 1
     slab = jnp.concatenate(
-        [passages] + [shift(passages, "zh", k) for k in (1, 2, 3)], axis=0
+        [jnp.where(refresh, passages, near), jnp.where(refresh, mid, far)], axis=0
     )
     lines = [slab] + [shift(slab, "y", k) for k in (1, 2, 3)]
     lines = lines + [shift(v, "c", 1) for v in lines]
@@ -392,7 +412,7 @@
         in_specs=[VMEM] * 10,
         out_specs=VMEM,
         compiler_params=params(),
-        cost_estimate=cost(2 * 1024 * width * 100, 3 << 20),
+        cost_estimate=cost(2 * 512 * width * 100, 3 << 20),
         name="score",
     )(q_all, lists, *lines)
     arrived = lax.all_to_all(shares, ("grp", "mp"), 0, 0, tiled=True)

time: 123 us -> 108 us (0.88)
  waiting for transfers between devices: 24.2 us -> 15.9 us
  starting transfers between devices: 53 us -> 47.9 us
  blocking collectives: 33.4 us -> 31.5 us
    ppermute x20 -> x21, starting transfers between devices: 47.3 us -> 34.2 us  [shift(): lax.ppermute(block, axis, [(i, (i + distance) % n) for i in range(n)])]
    ppermute x20 -> x21, waiting for transfers between devices: 24.2 us -> 15 us  [shift(): lax.ppermute(block, axis, [(i, (i + distance) % n) for i in range(n)])]
    ppermute x0 -> x7, starting transfers between devices: none -> 9.08 us  [the longest x4 6.14 us: cross(): return lax.ppermute(block, ('grp', 'zh'), route)]
    all_to_all x1, blocking collectives: 21.9 us -> 18 us  [body(): lines = [lax.all_to_all(packed, 'zh', 0, 0, tiled=True)]]
    all_to_all x1, blocking collectives: 11.5 us -> 13.5 us  [body(): arrived = lax.all_to_all(shares, ('grp', 'mp'), 0, 0, tiled=True)]
    unnamed x25 -> x22, local copies, waits for them, and re-layouts: 2.23 us -> 3.43 us
  transfers between devices with their start and end apart: 21 -> 29, of which waited for: 8 -> 9; matrix products, arithmetic and copies ran while one was open for 0% -> 0% of each run, Pallas kernels for 1% -> 1%
where the time goes in v4:
time: 108 us
  starting transfers between devices  47.9 us (44%)
  blocking collectives  31.5 us (29%)
  waiting for transfers between devices  15.9 us (15%)
  Pallas kernels  8.05 us (7%)
  local copies, waits for them, and re-layouts  3.43 us (3%)
    ppermute x21, starting transfers between devices, shift(): lax.ppermute(block, axis, [(i, (i + distance) % n) for i in range(n)])  34.2 us
    all_to_all x1, blocking collectives, body(): lines = [lax.all_to_all(packed, 'zh', 0, 0, tiled=True)]  18 us
    ppermute x21, waiting for transfers between devices, shift(): lax.ppermute(block, axis, [(i, (i + distance) % n) for i in range(n)])  15 us
    all_to_all x1, blocking collectives, body(): arrived = lax.all_to_all(shares, ('grp', 'mp'), 0, 0, tiled=True)  13.5 us
    ppermute x4, starting transfers between devices, cross(): return lax.ppermute(block, ('grp', 'zh'), route)  6.14 us
    all_to_all x1, starting transfers between devices, body(): arrived = lax.all_to_all(send, ('grp', 'mp'), 0, 0, tiled=True)  4.61 us
    pallas_call x1, Pallas kernels, body(): pl.pallas_call(ffn_kernel, out_shape=[shape((part_rows, width), F32)] + [...  3.78 us
    unnamed x22, local copies, waits for them, and re-layouts  3.43 us
  transfers between devices with their start and end apart: 29, of which 9 were waited for; matrix products, arithmetic and copies ran while one was open for 0% of the time, Pallas kernels for 1%

profile of v4, /device:TPU:1, one launch (start us, length us, event | category | flops | bytes accessed | tf_op | source)
XLA Modules:
  0.0 107.6 jit_solution(9931282605393769864)
XLA Ops:
  2.6 18.0 %all_to_all.15.rest_0_ = bf16[4,32,1024]{2,1,0:T(8,128)(2,1)S(1)} all-to-all(bf16[4,32,1024]{2,1,0:T(8,128)(2,1)S(1)} %pack.1), channel_id=1, replica_groups=mesh['grp'=2,'zh'=4,'y'=4,'c'=2,'mp'=4] {'zh'}, dimensions={0} | all-to-all | bytes 524288 | tf_op jit(solution)/shard_map/all_to_all | solution.py:343
  20.6 1.3 %collective-permute-start = (bf16[4,32,1024]{2,1,0:T(8,128)(2,1)S(1)}, bf16[4,32,1024]{2,1,0:T(8,128)(2,1)S(1)}, u32[]{:S(2)}, u32[]{:S(2)}) collective-permute-start(bf16[4,32,1024]{2,1,0:T(8,128)(2,1)S(1)} %all_to_all.15.rest_0_), channel_id=1, source_target_pairs={{0,8},{8,16},{16,24},{24,0},{1,9},{9,17},{17,25},{25,1},{2,10},{10... | collective-permute-start | bytes 786440 | tf_op jit(solution)/shard_map/ppermute | solution.py:39
  21.9 2.6 %collective-permute-start.1 = (bf16[4,32,1024]{2,1,0:T(8,128)(2,1)S(1)}, bf16[4,32,1024]{2,1,0:T(8,128)(2,1)S(1)}, u32[]{:S(2)}, u32[]{:S(2)}) collective-permute-start(bf16[4,32,1024]{2,1,0:T(8,128)(2,1)S(1)} %all_to_all.15.rest_0_), channel_id=1, source_target_pairs={{0,16},{8,24},{16,0},{24,8},{1,17},{9,25},{17,1},{25,9},{2,18},{10... | collective-permute-start | bytes 786440 | tf_op jit(solution)/shard_map/ppermute | solution.py:39
  24.5 1.1 collective-permute-start.2
  25.6 1.2 %collective-permute-start.3 = (bf16[4,32,1024]{2,1,0:T(8,128)(2,1)S(1)}, bf16[4,32,1024]{2,1,0:T(8,128)(2,1)S(1)}, u32[]{:S(2)}, u32[]{:S(2)}) collective-permute-start(bf16[4,32,1024]{2,1,0:T(8,128)(2,1)S(1)} %all_to_all.15.rest_0_), channel_id=1, source_target_pairs={{0,128},{128,0},{32,160},{160,32},{64,192},{192,64},{96,224},{224,... | collective-permute-start | bytes 786440 | tf_op jit(solution)/shard_map/ppermute | solution.py:47
  26.8 3.6 %collective-permute-start.7 = (bf16[4,32,1024]{2,1,0:T(8,128)(2,1)S(1)}, bf16[4,32,1024]{2,1,0:T(8,128)(2,1)S(1)}, u32[]{:S(2)}, u32[]{:S(2)}) collective-permute-start(bf16[4,32,1024]{2,1,0:T(8,128)(2,1)S(1)} %all_to_all.15.rest_0_), channel_id=1, source_target_pairs={{0,4},{4,0},{1,5},{5,1},{2,6},{6,2},{3,7},{7,3},{8,12},{12,8},{9,1... | collective-permute-start | bytes 786440 | tf_op jit(solution)/shard_map/ppermute | solution.py:39
  30.6 2.6 %collective-permute-done.1.rest_2_ = bf16[4,32,1024]{2,1,0:T(8,128)(2,1)S(1)} collective-permute-done((bf16[4,32,1024]{2,1,0:T(8,128)(2,1)S(1)}, bf16[4,32,1024]{2,1,0:T(8,128)(2,1)S(1)}, u32[]{:S(2)}, u32[]{:S(2)}) %collective-permute-start.1) | collective-permute-done | bytes 262176 | tf_op jit(solution)/shard_map/ppermute | solution.py:39
  33.2 1.7 %collective-permute-start.5 = (bf16[4,32,1024]{2,1,0:T(8,128)(2,1)S(1)}, bf16[4,32,1024]{2,1,0:T(8,128)(2,1)S(1)}, u32[]{:S(2)}, u32[]{:S(2)}) collective-permute-start(bf16[4,32,1024]{2,1,0:T(8,128)(2,1)S(1)} %collective-permute-done.1.rest_2_), channel_id=1, source_target_pairs={{0,128},{128,0},{32,160},{160,32},{64,192},{192,64},{96,224},{224,... | collective-permute-start | bytes 786440 | tf_op jit(solution)/shard_map/ppermute | solution.py:47
  34.9 3.0 %collective-permute-start.6 = (bf16[4,32,1024]{2,1,0:T(8,128)(2,1)S(1)}, bf16[4,32,1024]{2,1,0:T(8,128)(2,1)S(1)}, u32[]{:S(2)}, u32[]{:S(2)}) collective-permute-start(bf16[4,32,1024]{2,1,0:T(8,128)(2,1)S(1)} %collective-permute-done.2.rest_3_), channel_id=1, source_target_pairs={{0,224},{224,0},{32,128},{128,32},{64,160},{160,64},{96,192},{192,... | collective-permute-start | bytes 786440 | tf_op jit(solution)/shard_map/ppermute | solution.py:47
  37.9 2.7 %collective-permute-start.10 = (bf16[4,32,1024]{2,1,0:T(8,128)(2,1)S(1)}, bf16[4,32,1024]{2,1,0:T(8,128)(2,1)S(1)}, u32[]{:S(2)}, u32[]{:S(2)}) collective-permute-start(bf16[4,32,1024]{2,1,0:T(8,128)(2,1)S(1)} %collective-permute-done.2.rest_3_), channel_id=1, source_target_pairs={{0,4},{4,0},{1,5},{5,1},{2,6},{6,2},{3,7},{7,3},{8,12},{12,8},{9,1... | collective-permute-start | bytes 786440 | tf_op jit(solution)/shard_map/ppermute | solution.py:39
  40.7 2.9 %collective-permute-start.9 = (bf16[4,32,1024]{2,1,0:T(8,128)(2,1)S(1)}, bf16[4,32,1024]{2,1,0:T(8,128)(2,1)S(1)}, u32[]{:S(2)}, u32[]{:S(2)}) collective-permute-start(bf16[4,32,1024]{2,1,0:T(8,128)(2,1)S(1)} %collective-permute-done.1.rest_2_), channel_id=1, source_target_pairs={{0,4},{4,0},{1,5},{5,1},{2,6},{6,2},{3,7},{7,3},{8,12},{12,8},{9,1... | collective-permute-start | bytes 786440 | tf_op jit(solution)/shard_map/ppermute | solution.py:39
  43.7 0.9 collective-permute-done.6.rest_7_
  44.6 2.5 %collective-permute-start.12 = (bf16[4,32,1024]{2,1,0:T(8,128)(2,1)S(1)}, bf16[4,32,1024]{2,1,0:T(8,128)(2,1)S(1)}, u32[]{:S(2)}, u32[]{:S(2)}) collective-permute-start(bf16[4,32,1024]{2,1,0:T(8,128)(2,1)S(1)} %collective-permute-done.4.rest_5_), channel_id=1, source_target_pairs={{0,4},{4,0},{1,5},{5,1},{2,6},{6,2},{3,7},{7,3},{8,12},{12,8},{9,1... | collective-permute-start | bytes 786440 | tf_op jit(solution)/shard_map/ppermute | solution.py:39
  49.8 1.2 %copy-done.2 = bf16[1,512,1024]{2,1,0:T(8,128)(2,1)S(1)} copy-done((bf16[1,512,1024]{2,1,0:T(8,128)(2,1)S(1)}, bf16[1,512,1024]{2,1,0:T(8,128)(2,1)}, u32[]{:S(2)}) %copy-start.2) | copy-done | bytes 1048600
  51.0 3.8 %ffn.1 = (f32[128,1024]{1,0:T(8,128)S(1)}, bf16[128,1024]{1,0:T(8,128)(2,1)S(1)}, bf16[128,1024]{1,0:T(8,128)(2,1)S(1)}, bf16[128,1024]{1,0:T(8,128)(2,1)S(1)}, ...) custom-call(bf16[512,1024]{1,0:T(8,128)(2,1)S(1)} %bitcast.12, ...), custom_call_target="tpu_custom_call" | custom-call | flops 2147483648 | bytes 8388608 | tf_op jit(solution)/shard_map/ffn/pallas_call | solution.py:357
  54.8 1.5 %collective-permute-start.15 = (bf16[128,1024]{1,0:T(8,128)(2,1)S(1)}, bf16[128,1024]{1,0:T(8,128)(2,1)S(1)}, u32[]{:S(2)}, u32[]{:S(2)}) collective-permute-start(bf16[128,1024]{1,0:T(8,128)(2,1)S(1)} %get-tuple-element.22), channel_id=1, source_target_pairs={{0,1},{1,2},{2,3},{3,0},{4,5},{5,6},{6,7},{7,4},{8,9},{9,10},{10,1... | collective-permute-start | bytes 786440 | tf_op jit(solution)/shard_map/ppermute | solution.py:39
  56.3 2.5 %collective-permute-start.16 = (bf16[128,1024]{1,0:T(8,128)(2,1)S(1)}, bf16[128,1024]{1,0:T(8,128)(2,1)S(1)}, u32[]{:S(2)}, u32[]{:S(2)}) collective-permute-start(bf16[128,1024]{1,0:T(8,128)(2,1)S(1)} %get-tuple-element.23), channel_id=1, source_target_pairs={{0,2},{1,3},{2,0},{3,1},{4,6},{5,7},{6,4},{7,5},{8,10},{9,11},{10,... | collective-permute-start | bytes 786440 | tf_op jit(solution)/shard_map/ppermute | solution.py:39
  58.7 1.2 %collective-permute-start.17 = (bf16[128,1024]{1,0:T(8,128)(2,1)S(1)}, bf16[128,1024]{1,0:T(8,128)(2,1)S(1)}, u32[]{:S(2)}, u32[]{:S(2)}) collective-permute-start(bf16[128,1024]{1,0:T(8,128)(2,1)S(1)} %get-tuple-element.24), channel_id=1, source_target_pairs={{0,3},{1,0},{2,1},{3,2},{4,7},{5,4},{6,5},{7,6},{8,11},{9,8},{10,9... | collective-permute-start | bytes 786440 | tf_op jit(solution)/shard_map/ppermute | solution.py:39
  59.9 3.9 %collective-permute-done.15.r1 = bf16[128,1024]{1,0:T(8,128)(2,1)S(1)} collective-permute-done((bf16[128,1024]{1,0:T(8,128)(2,1)S(1)}, bf16[128,1024]{1,0:T(8,128)(2,1)S(1)}, u32[]{:S(2)}, u32[]{:S(2)}) %collective-permute-start.15) | collective-permute-done | bytes 262176 | tf_op jit(solution)/shard_map/ppermute | solution.py:39
  63.8 6.6 %collective-permute-done.16.r2 = bf16[128,1024]{1,0:T(8,128)(2,1)S(1)} collective-permute-done((bf16[128,1024]{1,0:T(8,128)(2,1)S(1)}, bf16[128,1024]{1,0:T(8,128)(2,1)S(1)}, u32[]{:S(2)}, u32[]{:S(2)}) %collective-permute-start.16) | collective-permute-done | bytes 262176 | tf_op jit(solution)/shard_map/ppermute | solution.py:39
  70.4 1.6 %norm.1 = (bf16[32,1152]{1,0:T(8,128)(2,1)S(1)}, bf16[8,144,256]{2,1,0:T(8,128)(2,1)}) custom-call(f32[128,1024]{1,0:T(8,128)S(1)} %get-tuple-element.21.own, bf16[128,1024]{1,0:T(8,128)(2,1)S(1)} %collective-permute-done.15.r1, bf16[128,1024]{1,0:T(8,128)(2,1)S(1)} %collective-permute-done.16.r2, bf16[128,1024]{1,0:T(8,128)(2,1)S(1)} %collective-permute-done.17.r3, ...), custom_call_target="tpu_custom_call" | custom-call | flops 16777216 | bytes 3145728 | tf_op jit(solution)/shard_map/norm/pallas_call | solution.py:378
  72.7 2.2 %collective-permute-start.20 = (bf16[32,1152]{1,0:T(8,128)(2,1)S(1)}, bf16[32,1152]{1,0:T(8,128)(2,1)S(1)}, u32[]{:S(2)}, u32[]{:S(2)}) collective-permute-start(bf16[32,1152]{1,0:T(8,128)(2,1)S(1)} %get-tuple-element.36), channel_id=1, source_target_pairs={{0,192},{32,224},{64,128},{96,160},{128,64},{160,96},{192,0},{224,... | collective-permute-start | bytes 221192 | tf_op jit(solution)/shard_map/ppermute | solution.py:56
  74.9 4.6 %all-to-all-start.1 = ((bf16[8,144,256]{2,1,0:T(8,128)(2,1)}), bf16[8,144,256]{2,1,0:T(8,128)(2,1)S(1)}, u32[]{:S(2)}, u32[]{:S(2)}) async-start(bf16[8,144,256]{2,1,0:T(8,128)(2,1)} %get-tuple-element.32), calls=%async_computation.1 | async-start | bytes 1179648 | tf_op jit(solution)/shard_map/all_to_all | solution.py:400
  79.6 0.9 collective-permute-start.21
  80.5 2.8 %collective-permute-start.22 = (bf16[64,1152]{1,0:T(8,128)(2,1)S(1)}, bf16[64,1152]{1,0:T(8,128)(2,1)S(1)}, u32[]{:S(2)}, u32[]{:S(2)}) collective-permute-start(bf16[64,1152]{1,0:T(8,128)(2,1)S(1)} %pad_maximum_fusion.rest_0_), channel_id=1, source_target_pairs={{0,16},{8,24},{16,0},{24,8},{1,17},{9,25},{17,1},{25,9},{2,18},{10... | collective-permute-start | bytes 442376 | tf_op jit(solution)/shard_map/ppermute | solution.py:39
  83.3 2.0 %collective-permute-start.23 = (bf16[64,1152]{1,0:T(8,128)(2,1)S(1)}, bf16[64,1152]{1,0:T(8,128)(2,1)S(1)}, u32[]{:S(2)}, u32[]{:S(2)}) collective-permute-start(bf16[64,1152]{1,0:T(8,128)(2,1)S(1)} %pad_maximum_fusion.rest_0_), channel_id=1, source_target_pairs={{0,24},{8,0},{16,8},{24,16},{1,25},{9,1},{17,9},{25,17},{2,26},{10... | collective-permute-start | bytes 442376 | tf_op jit(solution)/shard_map/ppermute | solution.py:39
  85.3 2.9 %collective-permute-start.24 = (bf16[64,1152]{1,0:T(8,128)(2,1)S(1)}, bf16[64,1152]{1,0:T(8,128)(2,1)S(1)}, u32[]{:S(2)}, u32[]{:S(2)}) collective-permute-start(bf16[64,1152]{1,0:T(8,128)(2,1)S(1)} %pad_maximum_fusion.rest_0_), channel_id=1, source_target_pairs={{0,4},{4,0},{1,5},{5,1},{2,6},{6,2},{3,7},{7,3},{8,12},{12,8},{9,1... | collective-permute-start | bytes 442376 | tf_op jit(solution)/shard_map/ppermute | solution.py:39
  88.2 1.4 %collective-permute-start.25 = (bf16[64,1152]{1,0:T(8,128)(2,1)S(1)}, bf16[64,1152]{1,0:T(8,128)(2,1)S(1)}, u32[]{:S(2)}, u32[]{:S(2)}) collective-permute-start(bf16[64,1152]{1,0:T(8,128)(2,1)S(1)} %collective-permute-done.21.rest_1_), channel_id=1, source_target_pairs={{0,4},{4,0},{1,5},{5,1},{2,6},{6,2},{3,7},{7,3},{8,12},{12,8},{9,1... | collective-permute-start | bytes 442376 | tf_op jit(solution)/shard_map/ppermute | solution.py:39
  89.6 1.6 %collective-permute-start.26 = (bf16[64,1152]{1,0:T(8,128)(2,1)S(1)}, bf16[64,1152]{1,0:T(8,128)(2,1)S(1)}, u32[]{:S(2)}, u32[]{:S(2)}) collective-permute-start(bf16[64,1152]{1,0:T(8,128)(2,1)S(1)} %collective-permute-done.22.rest_2_), channel_id=1, source_target_pairs={{0,4},{4,0},{1,5},{5,1},{2,6},{6,2},{3,7},{7,3},{8,12},{12,8},{9,1... | collective-permute-start | bytes 442376 | tf_op jit(solution)/shard_map/ppermute | solution.py:39
  92.6 0.8 score.1
  93.4 13.5 %all_to_all.16.arrived = f32[8,16,384]{2,1,0:T(8,128)S(1)} all-to-all(f32[8,16,384]{2,1,0:T(8,128)S(1)} %score.1), channel_id=1, replica_groups=mesh['grp'=2,'zh'=4,'y'=4,'c'=2,'mp'=4] {'grp','mp'}, dimensions={0} | all-to-all | bytes 393216 | tf_op jit(solution)/shard_map/all_to_all | solution.py:418
  106.9 0.8 final.1
  (59 shorter events, 7.2 us)
Async XLA Ops:
  2.5 46.6 %copy-start.5 = (f32[1024]{0:T(1024)S(1)}, f32[1024]{0:T(1024)}, u32[]{:S(2)}) copy-start(f32[1024]{0:T(1024)} %param.16) | copy-start | bytes 12292
  2.6 46.5 %copy-start.6 = (f32[1024]{0:T(1024)S(1)}, f32[1024]{0:T(1024)}, u32[]{:S(2)}) copy-start(f32[1024]{0:T(1024)} %param.17) | copy-start | bytes 12292
  2.6 46.5 %copy-start.7 = (s32[8,32]{1,0:T(8,128)S(1)}, s32[8,32]{1,0:T(8,128)}, u32[]{:S(2)}) copy-start(s32[8,32]{1,0:T(8,128)} %rest_20_.1) | copy-start | bytes 3076
  20.6 9.8 %collective-permute-start = (bf16[4,32,1024]{2,1,0:T(8,128)(2,1)S(1)}, bf16[4,32,1024]{2,1,0:T(8,128)(2,1)S(1)}, u32[]{:S(2)}, u32[]{:S(2)}) collective-permute-start(bf16[4,32,1024]{2,1,0:T(8,128)(2,1)S(1)} %all_to_all.15.rest_0_), channel_id=1, source_target_pairs={{0,8},{8,16},{16,24},{24,0},{1,9},{9,17},{17,25},{25,1},{2,10},{10... | collective-permute-start | bytes 786440 | tf_op jit(solution)/shard_map/ppermute | solution.py:39
  21.9 11.3 %collective-permute-start.1 = (bf16[4,32,1024]{2,1,0:T(8,128)(2,1)S(1)}, bf16[4,32,1024]{2,1,0:T(8,128)(2,1)S(1)}, u32[]{:S(2)}, u32[]{:S(2)}) collective-permute-start(bf16[4,32,1024]{2,1,0:T(8,128)(2,1)S(1)} %all_to_all.15.rest_0_), channel_id=1, source_target_pairs={{0,16},{8,24},{16,0},{24,8},{1,17},{9,25},{17,1},{25,9},{2,18},{10... | collective-permute-start | bytes 786440 | tf_op jit(solution)/shard_map/ppermute | solution.py:39
  24.5 10.4 %collective-permute-start.2 = (bf16[4,32,1024]{2,1,0:T(8,128)(2,1)S(1)}, bf16[4,32,1024]{2,1,0:T(8,128)(2,1)S(1)}, u32[]{:S(2)}, u32[]{:S(2)}) collective-permute-start(bf16[4,32,1024]{2,1,0:T(8,128)(2,1)S(1)} %all_to_all.15.rest_0_), channel_id=1, source_target_pairs={{0,24},{8,0},{16,8},{24,16},{1,25},{9,1},{17,9},{25,17},{2,26},{10... | collective-permute-start | bytes 786440 | tf_op jit(solution)/shard_map/ppermute | solution.py:39
  25.6 12.3 %collective-permute-start.3 = (bf16[4,32,1024]{2,1,0:T(8,128)(2,1)S(1)}, bf16[4,32,1024]{2,1,0:T(8,128)(2,1)S(1)}, u32[]{:S(2)}, u32[]{:S(2)}) collective-permute-start(bf16[4,32,1024]{2,1,0:T(8,128)(2,1)S(1)} %all_to_all.15.rest_0_), channel_id=1, source_target_pairs={{0,128},{128,0},{32,160},{160,32},{64,192},{192,64},{96,224},{224,... | collective-permute-start | bytes 786440 | tf_op jit(solution)/shard_map/ppermute | solution.py:47
  26.8 13.9 %collective-permute-start.7 = (bf16[4,32,1024]{2,1,0:T(8,128)(2,1)S(1)}, bf16[4,32,1024]{2,1,0:T(8,128)(2,1)S(1)}, u32[]{:S(2)}, u32[]{:S(2)}) collective-permute-start(bf16[4,32,1024]{2,1,0:T(8,128)(2,1)S(1)} %all_to_all.15.rest_0_), channel_id=1, source_target_pairs={{0,4},{4,0},{1,5},{5,1},{2,6},{6,2},{3,7},{7,3},{8,12},{12,8},{9,1... | collective-permute-start | bytes 786440 | tf_op jit(solution)/shard_map/ppermute | solution.py:39
  30.4 10.4 %collective-permute-start.4 = (bf16[4,32,1024]{2,1,0:T(8,128)(2,1)S(1)}, bf16[4,32,1024]{2,1,0:T(8,128)(2,1)S(1)}, u32[]{:S(2)}, u32[]{:S(2)}) collective-permute-start(bf16[4,32,1024]{2,1,0:T(8,128)(2,1)S(1)} %collective-permute-done.rest_1_), channel_id=1, source_target_pairs={{0,224},{224,0},{32,128},{128,32},{64,160},{160,64},{96,192},{192,... | collective-permute-start | bytes 786440 | tf_op jit(solution)/shard_map/ppermute | solution.py:47
  33.2 10.4 %collective-permute-start.5 = (bf16[4,32,1024]{2,1,0:T(8,128)(2,1)S(1)}, bf16[4,32,1024]{2,1,0:T(8,128)(2,1)S(1)}, u32[]{:S(2)}, u32[]{:S(2)}) collective-permute-start(bf16[4,32,1024]{2,1,0:T(8,128)(2,1)S(1)} %collective-permute-done.1.rest_2_), channel_id=1, source_target_pairs={{0,128},{128,0},{32,160},{160,32},{64,192},{192,64},{96,224},{224,... | collective-permute-start | bytes 786440 | tf_op jit(solution)/shard_map/ppermute | solution.py:47
  34.9 9.8 %collective-permute-start.6 = (bf16[4,32,1024]{2,1,0:T(8,128)(2,1)S(1)}, bf16[4,32,1024]{2,1,0:T(8,128)(2,1)S(1)}, u32[]{:S(2)}, u32[]{:S(2)}) collective-permute-start(bf16[4,32,1024]{2,1,0:T(8,128)(2,1)S(1)} %collective-permute-done.2.rest_3_), channel_id=1, source_target_pairs={{0,224},{224,0},{32,128},{128,32},{64,160},{160,64},{96,192},{192,... | collective-permute-start | bytes 786440 | tf_op jit(solution)/shard_map/ppermute | solution.py:47
  37.9 9.3 %collective-permute-start.10 = (bf16[4,32,1024]{2,1,0:T(8,128)(2,1)S(1)}, bf16[4,32,1024]{2,1,0:T(8,128)(2,1)S(1)}, u32[]{:S(2)}, u32[]{:S(2)}) collective-permute-start(bf16[4,32,1024]{2,1,0:T(8,128)(2,1)S(1)} %collective-permute-done.2.rest_3_), channel_id=1, source_target_pairs={{0,4},{4,0},{1,5},{5,1},{2,6},{6,2},{3,7},{7,3},{8,12},{12,8},{9,1... | collective-permute-start | bytes 786440 | tf_op jit(solution)/shard_map/ppermute | solution.py:39
  40.6 6.6 %collective-permute-start.8 = (bf16[4,32,1024]{2,1,0:T(8,128)(2,1)S(1)}, bf16[4,32,1024]{2,1,0:T(8,128)(2,1)S(1)}, u32[]{:S(2)}, u32[]{:S(2)}) collective-permute-start(bf16[4,32,1024]{2,1,0:T(8,128)(2,1)S(1)} %collective-permute-done.rest_1_), channel_id=1, source_target_pairs={{0,4},{4,0},{1,5},{5,1},{2,6},{6,2},{3,7},{7,3},{8,12},{12,8},{9,1... | collective-permute-start | bytes 786440 | tf_op jit(solution)/shard_map/ppermute | solution.py:39
  40.7 7.0 %collective-permute-start.9 = (bf16[4,32,1024]{2,1,0:T(8,128)(2,1)S(1)}, bf16[4,32,1024]{2,1,0:T(8,128)(2,1)S(1)}, u32[]{:S(2)}, u32[]{:S(2)}) collective-permute-start(bf16[4,32,1024]{2,1,0:T(8,128)(2,1)S(1)} %collective-permute-done.1.rest_2_), channel_id=1, source_target_pairs={{0,4},{4,0},{1,5},{5,1},{2,6},{6,2},{3,7},{7,3},{8,12},{12,8},{9,1... | collective-permute-start | bytes 786440 | tf_op jit(solution)/shard_map/ppermute | solution.py:39
  43.6 4.1 %collective-permute-start.11 = (bf16[4,32,1024]{2,1,0:T(8,128)(2,1)S(1)}, bf16[4,32,1024]{2,1,0:T(8,128)(2,1)S(1)}, u32[]{:S(2)}, u32[]{:S(2)}) collective-permute-start(bf16[4,32,1024]{2,1,0:T(8,128)(2,1)S(1)} %collective-permute-done.3.rest_4_), channel_id=1, source_target_pairs={{0,4},{4,0},{1,5},{5,1},{2,6},{6,2},{3,7},{7,3},{8,12},{12,8},{9,1... | collective-permute-start | bytes 786440 | tf_op jit(solution)/shard_map/ppermute | solution.py:39
  44.6 3.7 %collective-permute-start.12 = (bf16[4,32,1024]{2,1,0:T(8,128)(2,1)S(1)}, bf16[4,32,1024]{2,1,0:T(8,128)(2,1)S(1)}, u32[]{:S(2)}, u32[]{:S(2)}) collective-permute-start(bf16[4,32,1024]{2,1,0:T(8,128)(2,1)S(1)} %collective-permute-done.4.rest_5_), channel_id=1, source_target_pairs={{0,4},{4,0},{1,5},{5,1},{2,6},{6,2},{3,7},{7,3},{8,12},{12,8},{9,1... | collective-permute-start | bytes 786440 | tf_op jit(solution)/shard_map/ppermute | solution.py:39
  47.2 1.5 %collective-permute-start.13 = (bf16[4,32,1024]{2,1,0:T(8,128)(2,1)S(1)}, bf16[4,32,1024]{2,1,0:T(8,128)(2,1)S(1)}, u32[]{:S(2)}, u32[]{:S(2)}) collective-permute-start(bf16[4,32,1024]{2,1,0:T(8,128)(2,1)S(1)} %collective-permute-done.5.rest_6_), channel_id=1, source_target_pairs={{0,4},{4,0},{1,5},{5,1},{2,6},{6,2},{3,7},{7,3},{8,12},{12,8},{9,1... | collective-permute-start | bytes 786440 | tf_op jit(solution)/shard_map/ppermute | solution.py:39
  47.2 1.9 %collective-permute-start.14 = (bf16[4,32,1024]{2,1,0:T(8,128)(2,1)S(1)}, bf16[4,32,1024]{2,1,0:T(8,128)(2,1)S(1)}, u32[]{:S(2)}, u32[]{:S(2)}) collective-permute-start(bf16[4,32,1024]{2,1,0:T(8,128)(2,1)S(1)} %collective-permute-done.6.rest_7_), channel_id=1, source_target_pairs={{0,4},{4,0},{1,5},{5,1},{2,6},{6,2},{3,7},{7,3},{8,12},{12,8},{9,1... | collective-permute-start | bytes 786440 | tf_op jit(solution)/shard_map/ppermute | solution.py:39
  54.8 9.0 %collective-permute-start.15 = (bf16[128,1024]{1,0:T(8,128)(2,1)S(1)}, bf16[128,1024]{1,0:T(8,128)(2,1)S(1)}, u32[]{:S(2)}, u32[]{:S(2)}) collective-permute-start(bf16[128,1024]{1,0:T(8,128)(2,1)S(1)} %get-tuple-element.22), channel_id=1, source_target_pairs={{0,1},{1,2},{2,3},{3,0},{4,5},{5,6},{6,7},{7,4},{8,9},{9,10},{10,1... | collective-permute-start | bytes 786440 | tf_op jit(solution)/shard_map/ppermute | solution.py:39
  56.3 14.1 %collective-permute-start.16 = (bf16[128,1024]{1,0:T(8,128)(2,1)S(1)}, bf16[128,1024]{1,0:T(8,128)(2,1)S(1)}, u32[]{:S(2)}, u32[]{:S(2)}) collective-permute-start(bf16[128,1024]{1,0:T(8,128)(2,1)S(1)} %get-tuple-element.23), channel_id=1, source_target_pairs={{0,2},{1,3},{2,0},{3,1},{4,6},{5,7},{6,4},{7,5},{8,10},{9,11},{10,... | collective-permute-start | bytes 786440 | tf_op jit(solution)/shard_map/ppermute | solution.py:39
  58.7 11.7 %collective-permute-start.17 = (bf16[128,1024]{1,0:T(8,128)(2,1)S(1)}, bf16[128,1024]{1,0:T(8,128)(2,1)S(1)}, u32[]{:S(2)}, u32[]{:S(2)}) collective-permute-start(bf16[128,1024]{1,0:T(8,128)(2,1)S(1)} %get-tuple-element.24), channel_id=1, source_target_pairs={{0,3},{1,0},{2,1},{3,2},{4,7},{5,4},{6,5},{7,6},{8,11},{9,8},{10,9... | collective-permute-start | bytes 786440 | tf_op jit(solution)/shard_map/ppermute | solution.py:39
  72.0 7.5 %collective-permute-start.18 = (bf16[32,1152]{1,0:T(8,128)(2,1)S(1)}, bf16[32,1152]{1,0:T(8,128)(2,1)S(1)}, u32[]{:S(2)}, u32[]{:S(2)}) collective-permute-start(bf16[32,1152]{1,0:T(8,128)(2,1)S(1)} %get-tuple-element.36), channel_id=1, source_target_pairs={{0,224},{32,128},{64,160},{96,192},{128,32},{160,64},{192,96},{224... | collective-permute-start | bytes 221192 | tf_op jit(solution)/shard_map/ppermute | solution.py:56
  72.7 6.8 %collective-permute-start.19 = (bf16[32,1152]{1,0:T(8,128)(2,1)S(1)}, bf16[32,1152]{1,0:T(8,128)(2,1)S(1)}, u32[]{:S(2)}, u32[]{:S(2)}) collective-permute-start(bf16[32,1152]{1,0:T(8,128)(2,1)S(1)} %get-tuple-element.36), channel_id=1, source_target_pairs={{0,96},{32,0},{64,32},{96,64},{128,224},{160,128},{192,160},{224,1... | collective-permute-start | bytes 221192 | tf_op jit(solution)/shard_map/ppermute | solution.py:56
  72.7 6.8 %collective-permute-start.20 = (bf16[32,1152]{1,0:T(8,128)(2,1)S(1)}, bf16[32,1152]{1,0:T(8,128)(2,1)S(1)}, u32[]{:S(2)}, u32[]{:S(2)}) collective-permute-start(bf16[32,1152]{1,0:T(8,128)(2,1)S(1)} %get-tuple-element.36), channel_id=1, source_target_pairs={{0,192},{32,224},{64,128},{96,160},{128,64},{160,96},{192,0},{224,... | collective-permute-start | bytes 221192 | tf_op jit(solution)/shard_map/ppermute | solution.py:56
  74.9 16.4 %all-to-all-start.1 = ((bf16[8,144,256]{2,1,0:T(8,128)(2,1)}), bf16[8,144,256]{2,1,0:T(8,128)(2,1)S(1)}, u32[]{:S(2)}, u32[]{:S(2)}) async-start(bf16[8,144,256]{2,1,0:T(8,128)(2,1)} %get-tuple-element.32), calls=%async_computation.1 | async-start | bytes 1179648 | tf_op jit(solution)/shard_map/all_to_all | solution.py:400
  79.6 8.6 %collective-permute-start.21 = (bf16[64,1152]{1,0:T(8,128)(2,1)S(1)}, bf16[64,1152]{1,0:T(8,128)(2,1)S(1)}, u32[]{:S(2)}, u32[]{:S(2)}) collective-permute-start(bf16[64,1152]{1,0:T(8,128)(2,1)S(1)} %pad_maximum_fusion.rest_0_), channel_id=1, source_target_pairs={{0,8},{8,16},{16,24},{24,0},{1,9},{9,17},{17,25},{25,1},{2,10},{10... | collective-permute-start | bytes 442376 | tf_op jit(solution)/shard_map/ppermute | solution.py:39
  80.5 9.1 %collective-permute-start.22 = (bf16[64,1152]{1,0:T(8,128)(2,1)S(1)}, bf16[64,1152]{1,0:T(8,128)(2,1)S(1)}, u32[]{:S(2)}, u32[]{:S(2)}) collective-permute-start(bf16[64,1152]{1,0:T(8,128)(2,1)S(1)} %pad_maximum_fusion.rest_0_), channel_id=1, source_target_pairs={{0,16},{8,24},{16,0},{24,8},{1,17},{9,25},{17,1},{25,9},{2,18},{10... | collective-permute-start | bytes 442376 | tf_op jit(solution)/shard_map/ppermute | solution.py:39
  83.3 7.9 %collective-permute-start.23 = (bf16[64,1152]{1,0:T(8,128)(2,1)S(1)}, bf16[64,1152]{1,0:T(8,128)(2,1)S(1)}, u32[]{:S(2)}, u32[]{:S(2)}) collective-permute-start(bf16[64,1152]{1,0:T(8,128)(2,1)S(1)} %pad_maximum_fusion.rest_0_), channel_id=1, source_target_pairs={{0,24},{8,0},{16,8},{24,16},{1,25},{9,1},{17,9},{25,17},{2,26},{10... | collective-permute-start | bytes 442376 | tf_op jit(solution)/shard_map/ppermute | solution.py:39
  85.3 6.8 %collective-permute-start.24 = (bf16[64,1152]{1,0:T(8,128)(2,1)S(1)}, bf16[64,1152]{1,0:T(8,128)(2,1)S(1)}, u32[]{:S(2)}, u32[]{:S(2)}) collective-permute-start(bf16[64,1152]{1,0:T(8,128)(2,1)S(1)} %pad_maximum_fusion.rest_0_), channel_id=1, source_target_pairs={{0,4},{4,0},{1,5},{5,1},{2,6},{6,2},{3,7},{7,3},{8,12},{12,8},{9,1... | collective-permute-start | bytes 442376 | tf_op jit(solution)/shard_map/ppermute | solution.py:39
  88.2 3.8 %collective-permute-start.25 = (bf16[64,1152]{1,0:T(8,128)(2,1)S(1)}, bf16[64,1152]{1,0:T(8,128)(2,1)S(1)}, u32[]{:S(2)}, u32[]{:S(2)}) collective-permute-start(bf16[64,1152]{1,0:T(8,128)(2,1)S(1)} %collective-permute-done.21.rest_1_), channel_id=1, source_target_pairs={{0,4},{4,0},{1,5},{5,1},{2,6},{6,2},{3,7},{7,3},{8,12},{12,8},{9,1... | collective-permute-start | bytes 442376 | tf_op jit(solution)/shard_map/ppermute | solution.py:39
  89.6 2.6 %collective-permute-start.26 = (bf16[64,1152]{1,0:T(8,128)(2,1)S(1)}, bf16[64,1152]{1,0:T(8,128)(2,1)S(1)}, u32[]{:S(2)}, u32[]{:S(2)}) collective-permute-start(bf16[64,1152]{1,0:T(8,128)(2,1)S(1)} %collective-permute-done.22.rest_2_), channel_id=1, source_target_pairs={{0,4},{4,0},{1,5},{5,1},{2,6},{6,2},{3,7},{7,3},{8,12},{12,8},{9,1... | collective-permute-start | bytes 442376 | tf_op jit(solution)/shard_map/ppermute | solution.py:39
  91.2 1.4 %collective-permute-start.27 = (bf16[64,1152]{1,0:T(8,128)(2,1)S(1)}, bf16[64,1152]{1,0:T(8,128)(2,1)S(1)}, u32[]{:S(2)}, u32[]{:S(2)}) collective-permute-start(bf16[64,1152]{1,0:T(8,128)(2,1)S(1)} %collective-permute-done.23.rest_3_), channel_id=1, source_target_pairs={{0,4},{4,0},{1,5},{5,1},{2,6},{6,2},{3,7},{7,3},{8,12},{12,8},{9,1... | collective-permute-start | bytes 442376 | tf_op jit(solution)/shard_map/ppermute | solution.py:39
  (8 other events, 6.2 us)

commit v5 on v4

--- a/solution.py
+++ b/solution.py
@@ -23,11 +23,13 @@
 HBM = pl.BlockSpec(memory_space=pltpu.HBM)
 NT = (((1,), (1,)), ((), ()))
 N_NEG = 32
+Y_ORDER = (1, 3, 2)
+QUERY_ROWS = 2
 DIGIT = 64
 
 
-def params():
-    return pltpu.CompilerParams(vmem_limit_bytes=40 * 1024 * 1024)
+def params(mib=40):
+    return pltpu.CompilerParams(vmem_limit_bytes=mib * 1024 * 1024)
 
 
 def cost(flops, size):
@@ -82,6 +84,17 @@
         copy.wait()
 
 
+def stage_kernel(x, b_in, x_out, b_out, sems):
+    copies = [
+        pltpu.make_async_copy(x, x_out, sems.at[0]),
+        pltpu.make_async_copy(b_in, b_out, sems.at[1]),
+    ]
+    for copy in copies:
+        copy.start()
+    for copy in copies:
+        copy.wait()
+
+
 def slots():
     g, y, c = at("grp"), at("y"), at("c")
     found = []
@@ -89,33 +102,24 @@
         core = c if other == 0 else 1 - c
         for far in range(N_GRP):
             group = g if far == 0 else 1 - g
-            for k in range(N_Y):
+            for k in (0,) + Y_ORDER:
                 found.append((group, lax.rem(y - k + N_Y, N_Y) * N_C + core))
     return found
 
 
-def ffn_kernel(x_any, b_any, *rest):
-    sources, small = rest[:16], rest[16:23]
-    own_ref, s1, s2, s3 = rest[23:27]
-    small_out = rest[27:34]
-    w, x_ref, b_ref, hidden, total, sems = rest[34:]
+def ffn_kernel(x_ref, b_ref, *rest):
+    sources = rest[:16]
+    own_ref, s1, s2, s3 = rest[16:20]
+    w, hidden, total, sems = rest[20:]
     m = at("mp")
     hid = hidden.shape[1]
     shard = w.shape[3] // 2
-    early = [
-        pltpu.make_async_copy(x_any, x_ref, sems.at[32]),
-        pltpu.make_async_copy(b_any, b_ref, sems.at[33]),
-    ]
-    late = []
+    copies = []
     for i, (group, slot) in enumerate(slots()):
-        early.append(
-            pltpu.make_async_copy(sources[i], w.at[group, :, slot], sems.at[i])
-        )
-    for i, (source, target) in enumerate(zip(small, small_out)):
-        late.append(pltpu.make_async_copy(source, target, sems.at[34 + i]))
-    for copy in early + late:
+        copies.append(pltpu.make_async_copy(sources[i], w.at[group, :, slot], sems.at[i]))
+    for copy in copies:
         copy.start()
-    for copy in early:
+    for copy in copies:
         copy.wait()
     depth = x_ref.shape[1]
     tile = 256
@@ -124,8 +128,6 @@
         w_in = w[:, :, :, 0:shard, cols].reshape(depth, tile)
         pre = jnp.dot(x_ref[...], w_in, preferred_element_type=F32) + b_ref[:, cols]
         hidden[:, cols] = (0.5 * pre * (1.0 + lax.erf(pre * np.float32(0.5**0.5)))).astype(BF)
-    for copy in late:
-        copy.wait()
     planes = tile // (w.shape[2] * shard)
     per_group = w.shape[1] // planes
     for t in range(total.shape[1] // tile):
@@ -151,49 +153,24 @@
     return a, b, (rest - b.astype(F32)).astype(BF)
 
 
-def norm_kernel(
-    own, r1, r2, r3, b_out, gain, bias, lens, negs, counts, poss, p_ref, send
-):
+def prep_kernel(b_out, gain, bias, lens, negs, counts, poss, vectors, live, count, lists_ref):
     m = at("mp")
-    rows, width = own.shape
-    summed = own[...] + r1[...].astype(F32) + r2[...].astype(F32) + r3[...].astype(F32)
-    summed = summed + b_out[...]
-    center = jnp.mean(summed, axis=1, keepdims=True)
-    off = summed - center
-    spread_ = jnp.mean(off * off, axis=1, keepdims=True)
-    coded = (off * lax.rsqrt(spread_ + EPS_NORM) * gain[...] + bias[...]).astype(BF)
-
-    n_pass = p_ref.shape[0]
+    n_pass, rows = live.shape
+    part = lists_ref.shape[1]
+    vectors[0:1, :] = b_out[...]
+    vectors[1:2, :] = gain[...]
+    vectors[2:3, :] = bias[...]
     n_all = lens.shape[1]
     chosen = iota((n_pass, n_all), 1) == iota((n_pass, n_all), 0) + m * n_pass
     length = jnp.sum(jnp.where(chosen, lens[...].astype(F32), 0.0), axis=1, keepdims=True)
     row = iota((n_pass, rows), 1)
     slab = iota((n_pass, rows), 0)
     begin = ((row % WIN) * WINDOW_TOKENS).astype(F32)
-    live = jnp.where((row // WIN == slab) & (begin < length), 1.0, 0.0).astype(F32)
-    count = jnp.sum(live, axis=1, keepdims=True)
-    p = (jnp.dot(live.astype(BF), coded, preferred_element_type=F32) / count).astype(BF)
-    p_ref[:, :width] = p
-    pf = p.astype(F32)
-    square = pieces(jnp.sum(pf * pf, axis=1, keepdims=True))
-    lane = iota((n_pass, 128), 1)
-    tail = jnp.zeros((n_pass, 128), F32)
-    for i, piece in enumerate(square):
-        tail = jnp.where(lane == i, piece.astype(F32), tail)
-    p_ref[:, width:] = tail.astype(BF)
-
-    pick = onehot(iota((16, rows), 1) // QLEN == iota((16, rows), 0))
-    q = (jnp.dot(pick, coded, preferred_element_type=F32) * (1.0 / QLEN)).astype(BF)
-    part = send.shape[2]
-    block = jnp.zeros((16, part), F32)
-    r16, c16 = iota((16, 16), 0), iota((16, 16), 1)
-    n_q = rows // QLEN
-    for j in range(N_MP):
-        move = onehot((r16 == c16 + j * n_q) & (c16 < n_q))
-        block = block + jnp.dot(
-            move, q[:, j * part : (j + 1) * part], preferred_element_type=F32
-        )
+    alive = jnp.where((row // WIN == slab) & (begin < length), 1.0, 0.0).astype(F32)
+    live[...] = alive.astype(BF)
+    count[...] = jnp.broadcast_to(jnp.sum(alive, axis=1, keepdims=True), count.shape)
     own_q, n_neg = negs.shape
+    n_q = own_q // N_MP
     ids = negs[...]
     diag = iota((own_q, own_q), 0) == iota((own_q, own_q), 1)
     n_used = jnp.sum(jnp.where(diag, counts[...].astype(F32), 0.0), axis=1, keepdims=True)
@@ -212,38 +189,75 @@
     r8, c8 = iota((16, own_q), 0), iota((16, own_q), 1)
     base = N_MP * n_q
     move = onehot((r8 >= base) & (r8 < base + n_q) & (c8 == m * n_q + r8 - base))
-    block = (block + jnp.dot(move, lists.astype(BF), preferred_element_type=F32)).astype(BF)
+    lists_ref[...] = jnp.dot(move, lists.astype(BF), preferred_element_type=F32)
+
+
+def norm_kernel(own, r1, r2, r3, vectors, live, count, lists, p_ref, send):
+    rows, width = own.shape
+    summed = own[...] + r1[...].astype(F32) + r2[...].astype(F32) + r3[...].astype(F32)
+    summed = summed + vectors[0:1, :]
+    center = jnp.mean(summed, axis=1, keepdims=True)
+    off = summed - center
+    spread_ = jnp.mean(off * off, axis=1, keepdims=True)
+    coded = (off * lax.rsqrt(spread_ + EPS_NORM) * vectors[1:2, :] + vectors[2:3, :]).astype(BF)
+
+    n_pass = p_ref.shape[0]
+    p = (jnp.dot(live[...], coded, preferred_element_type=F32) / count[:, 0:1]).astype(BF)
+    p_ref[:, :width] = p
+    pf = p.astype(F32)
+    square = pieces(jnp.sum(pf * pf, axis=1, keepdims=True))
+    lane = iota((n_pass, 128), 1)
+    tail = jnp.zeros((n_pass, 128), F32)
+    for i, piece in enumerate(square):
+        tail = jnp.where(lane == i, piece.astype(F32), tail)
+    p_ref[:, width:] = tail.astype(BF)
+
+    pick = onehot(iota((16, rows), 1) // QLEN == iota((16, rows), 0))
+    q = (jnp.dot(pick, coded, preferred_element_type=F32) * (1.0 / QLEN)).astype(BF)
+    part = send.shape[2]
+    block = lists[...]
+    r16, c16 = iota((16, 16), 0), iota((16, 16), 1)
+    n_q = rows // QLEN
+    for j in range(N_MP):
+        move = onehot((r16 == c16 + j * n_q) & (c16 < n_q))
+        block = block + jnp.dot(
+            move, q[:, j * part : (j + 1) * part], preferred_element_type=F32
+        )
+    block = block.astype(BF)
     for g in range(N_GRP):
         for j in range(N_MP):
             send[g * N_MP + j, :rows, :] = coded[:, j * part : (j + 1) * part]
             send[g * N_MP + j, rows:, :] = block
 
 
-def unpack_kernel(arrived, encoded, q_ref, lists):
+def unpack_kernel(arrived, encoded):
     grp = at("grp")
-    part = encoded.shape[1]
     rows = encoded.shape[0] // N_MP
     for j in range(N_MP):
         encoded[j * rows : (j + 1) * rows, :] = arrived[grp * N_MP + j, 0:rows, :]
-    blocks = arrived[0:N_MP, rows : rows + 16, :].reshape(N_MP * 16, part)
-    n_q = rows // QLEN
-    shape = (16, N_MP * 16)
-    r, c = iota(shape, 0), iota(shape, 1)
-    for j in range(N_MP + 1):
-        take = onehot((c // 16 == r // n_q) & (c % 16 == j * n_q + r % n_q))
-        got = jnp.dot(take, blocks, preferred_element_type=F32)
-        if j < N_MP:
-            q_ref[:, j * part : (j + 1) * part] = got.astype(BF)
-        else:
-            lists[...] = got
+
+
+def query_kernel(arrived, q_ref, lists):
+    part = arrived.shape[2]
+    held = arrived[0:N_MP, arrived.shape[1] - 16 :, :].reshape(N_MP * 16, part)
+    own = QUERY_ROWS
+    shape = ((N_MP + 1) * 16, N_MP * 16)
+    r, col = iota(shape, 0), iota(shape, 1)
+    chunk, row = r // 16, r % 16
+    take = onehot((col // 16 == row // own) & (col % 16 == chunk * own + row % own))
+    got = jnp.dot(take, held, preferred_element_type=F32)
+    for j in range(N_MP):
+        q_ref[:, j * part : (j + 1) * part] = got[16 * j : 16 * (j + 1)].astype(BF)
+    lists[...] = got[16 * N_MP :]
 
 
 def score_kernel(q_ref, lists_ref, *rest):
     blocks, out = rest[:-1], rest[-1]
     g, zh, y, c, m = at("grp"), at("zh"), at("y"), at("c"), at("mp")
     size = blocks[0].shape[0]
+    each = size // N_GRP
     width = q_ref.shape[1]
-    each = size // N_GRP
+    part = width // N_MP
     n_q = out.shape[1] // 2
     q = q_ref[...]
     qf = q.astype(F32)
@@ -291,7 +305,6 @@
         )
     pull = grads[:n_q] + grads[n_q : 2 * n_q] + grads[2 * n_q : 3 * n_q]
     toward = grads[3 * n_q : 4 * n_q] + grads[4 * n_q : 5 * n_q] + grads[5 * n_q :]
-    part = width // N_MP
     stats = jnp.where(iota((n_q, 128), 1) < 64, total, score_pos)
     for g in range(N_GRP):
         for mm in range(N_MP):
@@ -337,13 +350,43 @@
         in_specs=[HBM] * 2,
         out_specs=VMEM,
         scratch_shapes=[pltpu.SemaphoreType.DMA((2 * N_ZH,))],
-        compiler_params=params(),
+        compiler_params=params(60),
         name="pack",
     )(w_in, w_out.T)
     lines = [lax.all_to_all(packed, "zh", 0, 0, tiled=True)]
-    lines = lines + [shift(lines[0], "y", k) for k in (1, 2, 3)]
-    lines = lines + [cross(v, k % 2 == 0) for k, v in enumerate(lines)]
+    x, b_in = pl.pallas_call(
+        stage_kernel,
+        out_shape=[shape((rows, width), BF), shape((1, hid), F32)],
+        in_specs=[HBM] * 2,
+        out_specs=[VMEM] * 2,
+        scratch_shapes=[pltpu.SemaphoreType.DMA((2,))],
+        compiler_params=params(20),
+        name="stage",
+    )(x, b_in[None])
+    lines[0], x, b_in = lax.optimization_barrier((lines[0], x, b_in))
+    far = [cross(lines[0], True)]
+    for k in Y_ORDER:
+        lines.append(shift(lines[0], "y", k))
+    far = far + [cross(lines[i], Y_ORDER[i - 1] == 2) for i in (1, 2, 3)]
+    lines = lines + far
     lines = lines + [shift(v, "c", 1) for v in lines]
+    weights = pltpu.VMEM((N_GRP, N_ZH, N_Y * N_C, 2 * shard, hid), BF)
+    own, s1, s2, s3 = pl.pallas_call(
+        ffn_kernel,
+        out_shape=[shape((part_rows, width), F32)] + [shape((part_rows, width), BF)] * 3,
+        in_specs=[VMEM] * 2 + [ANY] * 16,
+        out_specs=[VMEM] * 4,
+        scratch_shapes=[
+            weights,
+            pltpu.VMEM((rows, hid), BF),
+            pltpu.VMEM((rows, width), F32),
+            pltpu.SemaphoreType.DMA((16,)),
+        ],
+        compiler_params=params(20),
+        cost_estimate=cost(4 * rows * width * hid, 8 << 20),
+        name="ffn",
+    )(x, b_in, *lines)
+    r2, r1, r3 = shift(s2, "mp", 2), shift(s1, "mp", 1), shift(s3, "mp", 3)
     small = [
         b_out[None],
         ln_gain[None],
@@ -353,27 +396,20 @@
         neg_count[None],
         pos_ids[None],
     ]
-    weights = pltpu.VMEM((N_GRP, N_ZH, N_Y * N_C, 2 * shard, hid), BF)
-    own, s1, s2, s3, *small = pl.pallas_call(
-        ffn_kernel,
-        out_shape=[shape((part_rows, width), F32)]
-        + [shape((part_rows, width), BF)] * 3
-        + [shape(v.shape, v.dtype) for v in small],
-        in_specs=[HBM] * 2 + [ANY] * 16 + [HBM] * 7,
-        out_specs=[VMEM] * 11,
-        scratch_shapes=[
-            weights,
-            pltpu.VMEM((rows, width), BF),
-            pltpu.VMEM((1, hid), F32),
-            pltpu.VMEM((rows, hid), BF),
-            pltpu.VMEM((rows, width), F32),
-            pltpu.SemaphoreType.DMA((41,)),
+    r1, *small = lax.optimization_barrier((r1, *small))
+    vectors, live, count, lists = pl.pallas_call(
+        prep_kernel,
+        out_shape=[
+            shape((3, width), F32),
+            shape((n_pass, part_rows), BF),
+            shape((n_pass, 128), F32),
+            shape((16, part), F32),
         ],
-        compiler_params=params(),
-        cost_estimate=cost(4 * rows * width * hid, 8 << 20),
-        name="ffn",
-    )(x, b_in[None], *lines, *small)
-    r2, r1, r3 = shift(s2, "mp", 2), shift(s1, "mp", 1), shift(s3, "mp", 3)
+        in_specs=[VMEM] * 7,
+        out_specs=[VMEM] * 4,
+        compiler_params=params(),
+        name="prep",
+    )(*small)
 
     passages, send = pl.pallas_call(
         norm_kernel,
@@ -381,12 +417,12 @@
             shape((n_pass, width + 128), BF),
             shape((peers, part_rows + 16, part), BF),
         ],
-        in_specs=[VMEM] * 11,
+        in_specs=[VMEM] * 8,
         out_specs=[VMEM] * 2,
         compiler_params=params(),
         cost_estimate=cost(2 * part_rows * width * 64, 3 << 20),
         name="norm",
-    )(own, r1, r2, r3, *small)
+    )(own, r1, r2, r3, vectors, live, count, lists)
 
     far = reroute(passages, lambda g, z: (1 - g, z - 2 if g else z + 2))
     mid = reroute(passages, lambda g, z: (g, z - 1))
@@ -396,16 +432,25 @@
         [jnp.where(refresh, passages, near), jnp.where(refresh, mid, far)], axis=0
     )
     lines = [slab] + [shift(slab, "y", k) for k in (1, 2, 3)]
-    lines = lines + [shift(v, "c", 1) for v in lines]
     arrived = lax.all_to_all(send, ("grp", "mp"), 0, 0, tiled=True)
-    encoded, q_all, lists = pl.pallas_call(
+    q_all, lists = pl.pallas_call(
+        query_kernel,
+        out_shape=[shape((16, width), BF), shape((16, part), F32)],
+        in_specs=[VMEM],
+        out_specs=[VMEM] * 2,
+        compiler_params=params(),
+        name="query",
+    )(arrived)
+    encoded = pl.pallas_call(
         unpack_kernel,
-        out_shape=[shape((rows, part), BF), shape((16, width), BF), shape((16, part), F32)],
+        out_shape=shape((rows, part), BF),
         in_specs=[VMEM],
-        out_specs=[VMEM] * 3,
+        out_specs=VMEM,
         compiler_params=params(),
         name="unpack",
     )(arrived)
+    lines[1], q_all, encoded = lax.optimization_barrier((lines[1], q_all, encoded))
+    lines = lines + [shift(v, "c", 1) for v in lines]
     shares = pl.pallas_call(
         score_kernel,
         out_shape=shape((peers, 2 * own_q, part + 128), F32),

time: 108 us -> 105 us (0.972)
  blocking collectives: 31.5 us -> 12.9 us
  starting transfers between devices: 47.9 us -> 60.1 us
  waiting for transfers between devices: 15.9 us -> 19.5 us
  local copies, waits for them, and re-layouts: 3.43 us -> 1.91 us
    all_to_all x1 -> x0, blocking collectives: 18 us -> none  [body(): lines = [lax.all_to_all(packed, 'zh', 0, 0, tiled=True)]]
    all_to_all x0 -> x1, starting transfers between devices: none -> 9.02 us  [body(): lines = [lax.all_to_all(packed, 'zh', 0, 0, tiled=True)]]
    all_to_all x0 -> x1, waiting for transfers between devices: none -> 6.84 us  [body(): lines = [lax.all_to_all(packed, 'zh', 0, 0, tiled=True)]]
    ppermute x21, starting transfers between devices: 34.2 us -> 38.3 us  [shift(): lax.ppermute(block, axis, [(i, (i + distance) % n) for i in range(n)])]
    ppermute x21, waiting for transfers between devices: 15 us -> 12.6 us  [shift(): lax.ppermute(block, axis, [(i, (i + distance) % n) for i in range(n)])]
    ppermute x4, starting transfers between devices: 6.14 us -> 4.19 us  [cross(): return lax.ppermute(block, ('grp', 'zh'), route)]
    ppermute x3, starting transfers between devices: 2.94 us -> 4.5 us  [reroute(): return lax.ppermute(block, ('grp', 'zh'), route)]
    unnamed x22 -> x18, local copies, waits for them, and re-layouts: 3.43 us -> 1.91 us
  transfers between devices with their start and end apart: 29 -> 30, of which waited for: 9 -> 8; matrix products, arithmetic and copies ran while one was open for 0% -> 0% of each run, Pallas kernels for 1% -> 1%
where the time goes in v5:
time: 105 us; the launch traced here: 104 us
  starting transfers between devices  60.1 us (57%)
  waiting for transfers between devices  19.5 us (19%)
  blocking collectives  12.9 us (12%)
  Pallas kernels  9.06 us (9%)
  local copies, waits for them, and re-layouts  1.91 us (2%)
    ppermute x21, starting transfers between devices, shift(): lax.ppermute(block, axis, [(i, (i + distance) % n) for i in range(n)])  38.3 us
    all_to_all x1, blocking collectives, body(): arrived = lax.all_to_all(shares, ('grp', 'mp'), 0, 0, tiled=True)  12.9 us
    ppermute x21, waiting for transfers between devices, shift(): lax.ppermute(block, axis, [(i, (i + distance) % n) for i in range(n)])  12.6 us
    all_to_all x1, starting transfers between devices, body(): lines = [lax.all_to_all(packed, 'zh', 0, 0, tiled=True)]  9.02 us
    all_to_all x1, waiting for transfers between devices, body(): lines = [lax.all_to_all(packed, 'zh', 0, 0, tiled=True)]  6.84 us
    ppermute x3, starting transfers between devices, reroute(): return lax.ppermute(block, ('grp', 'zh'), route)  4.5 us
    ppermute x4, starting transfers between devices, cross(): return lax.ppermute(block, ('grp', 'zh'), route)  4.19 us
    all_to_all x1, starting transfers between devices, body(): arrived = lax.all_to_all(send, ('grp', 'mp'), 0, 0, tiled=True)  4.05 us
  transfers between devices with their start and end apart: 30, of which 8 were waited for; matrix products, arithmetic and copies ran while one was open for 0% of the time, Pallas kernels for 1%

profile of v5, /device:TPU:1, one launch (start us, length us, event | category | flops | bytes accessed | tf_op | source)
XLA Modules:
  0.0 104.3 jit_solution(18043356806481943912)
XLA Ops:
  0.6 1.7 %pack.1 = bf16[4,32,1024]{2,1,0:T(8,128)(2,1)} custom-call(bf16[16,1024]{1,0:T(8,128)(2,1)} %w_in.1, bf16[16,1024]{1,0:T(8,128)(2,1)} %bitcast.20), custom_call_target="tpu_custom_call" | custom-call | tf_op jit(solution)/shard_map/pack/pallas_call | solution.py:347
  2.4 9.0 %all-to-all-start = ((bf16[4,32,1024]{2,1,0:T(8,128)(2,1)}), bf16[4,32,1024]{2,1,0:T(8,128)(2,1)S(1)}, u32[]{:S(2)}, u32[]{:S(2)}) async-start(bf16[4,32,1024]{2,1,0:T(8,128)(2,1)} %pack.1), calls=%async_computation | async-start | bytes 524288 | tf_op jit(solution)/shard_map/all_to_all | solution.py:356
  11.4 1.2 %copy-done = bf16[1,512,1024]{2,1,0:T(8,128)(2,1)S(1)} copy-done((bf16[1,512,1024]{2,1,0:T(8,128)(2,1)S(1)}, bf16[1,512,1024]{2,1,0:T(8,128)(2,1)}, u32[]{:S(2)}) %copy-start) | copy-done | bytes 1048600
  12.7 6.8 %all-to-all-done.rest_0_ = bf16[4,32,1024]{2,1,0:T(8,128)(2,1)S(1)} async-done(((bf16[4,32,1024]{2,1,0:T(8,128)(2,1)}), bf16[4,32,1024]{2,1,0:T(8,128)(2,1)S(1)}, u32[]{:S(2)}, u32[]{:S(2)}) %all-to-all-start) | async-done | bytes 262176 | tf_op jit(solution)/shard_map/all_to_all | solution.py:356
  19.6 1.3 %collective-permute-start = (bf16[4,32,1024]{2,1,0:T(8,128)(2,1)S(1)}, bf16[4,32,1024]{2,1,0:T(8,128)(2,1)S(1)}, u32[]{:S(2)}, u32[]{:S(2)}) collective-permute-start(bf16[4,32,1024]{2,1,0:T(8,128)(2,1)S(1)} %all-to-all-done.rest_0_), channel_id=1, source_target_pairs={{0,8},{8,16},{16,24},{24,0},{1,9},{9,17},{17,25},{25,1},{2,10},{10... | collective-permute-start | bytes 786440 | tf_op jit(solution)/shard_map/ppermute | solution.py:41
  20.9 1.4 %collective-permute-start.1 = (bf16[4,32,1024]{2,1,0:T(8,128)(2,1)S(1)}, bf16[4,32,1024]{2,1,0:T(8,128)(2,1)S(1)}, u32[]{:S(2)}, u32[]{:S(2)}) collective-permute-start(bf16[4,32,1024]{2,1,0:T(8,128)(2,1)S(1)} %all-to-all-done.rest_0_), channel_id=1, source_target_pairs={{0,24},{8,0},{16,8},{24,16},{1,25},{9,1},{17,9},{25,17},{2,26},{10... | collective-permute-start | bytes 786440 | tf_op jit(solution)/shard_map/ppermute | solution.py:41
  22.3 1.6 %collective-permute-start.2 = (bf16[4,32,1024]{2,1,0:T(8,128)(2,1)S(1)}, bf16[4,32,1024]{2,1,0:T(8,128)(2,1)S(1)}, u32[]{:S(2)}, u32[]{:S(2)}) collective-permute-start(bf16[4,32,1024]{2,1,0:T(8,128)(2,1)S(1)} %all-to-all-done.rest_0_), channel_id=1, source_target_pairs={{0,16},{8,24},{16,0},{24,8},{1,17},{9,25},{17,1},{25,9},{2,18},{10... | collective-permute-start | bytes 786440 | tf_op jit(solution)/shard_map/ppermute | solution.py:41
  24.6 4.4 %collective-permute-start.7 = (bf16[4,32,1024]{2,1,0:T(8,128)(2,1)S(1)}, bf16[4,32,1024]{2,1,0:T(8,128)(2,1)S(1)}, u32[]{:S(2)}, u32[]{:S(2)}) collective-permute-start(bf16[4,32,1024]{2,1,0:T(8,128)(2,1)S(1)} %all-to-all-done.rest_0_), channel_id=1, source_target_pairs={{0,4},{4,0},{1,5},{5,1},{2,6},{6,2},{3,7},{7,3},{8,12},{12,8},{9,1... | collective-permute-start | bytes 786440 | tf_op jit(solution)/shard_map/ppermute | solution.py:41
  29.1 0.8 collective-permute-start.4
  29.9 1.9 %collective-permute-start.5 = (bf16[4,32,1024]{2,1,0:T(8,128)(2,1)S(1)}, bf16[4,32,1024]{2,1,0:T(8,128)(2,1)S(1)}, u32[]{:S(2)}, u32[]{:S(2)}) collective-permute-start(bf16[4,32,1024]{2,1,0:T(8,128)(2,1)S(1)} %collective-permute-done.1.rest_2_), channel_id=1, source_target_pairs={{0,224},{224,0},{32,128},{128,32},{64,160},{160,64},{96,192},{192,... | collective-permute-start | bytes 786440 | tf_op jit(solution)/shard_map/ppermute | solution.py:49
  31.8 0.8 collective-permute-start.6
  32.6 4.8 %collective-permute-start.10 = (bf16[4,32,1024]{2,1,0:T(8,128)(2,1)S(1)}, bf16[4,32,1024]{2,1,0:T(8,128)(2,1)S(1)}, u32[]{:S(2)}, u32[]{:S(2)}) collective-permute-start(bf16[4,32,1024]{2,1,0:T(8,128)(2,1)S(1)} %collective-permute-done.2.rest_3_), channel_id=1, source_target_pairs={{0,4},{4,0},{1,5},{5,1},{2,6},{6,2},{3,7},{7,3},{8,12},{12,8},{9,1... | collective-permute-start | bytes 786440 | tf_op jit(solution)/shard_map/ppermute | solution.py:41
  37.5 4.3 %collective-permute-start.9 = (bf16[4,32,1024]{2,1,0:T(8,128)(2,1)S(1)}, bf16[4,32,1024]{2,1,0:T(8,128)(2,1)S(1)}, u32[]{:S(2)}, u32[]{:S(2)}) collective-permute-start(bf16[4,32,1024]{2,1,0:T(8,128)(2,1)S(1)} %collective-permute-done.1.rest_2_), channel_id=1, source_target_pairs={{0,4},{4,0},{1,5},{5,1},{2,6},{6,2},{3,7},{7,3},{8,12},{12,8},{9,1... | collective-permute-start | bytes 786440 | tf_op jit(solution)/shard_map/ppermute | solution.py:41
  41.8 2.8 %collective-permute-start.11 = (bf16[4,32,1024]{2,1,0:T(8,128)(2,1)S(1)}, bf16[4,32,1024]{2,1,0:T(8,128)(2,1)S(1)}, u32[]{:S(2)}, u32[]{:S(2)}) collective-permute-start(bf16[4,32,1024]{2,1,0:T(8,128)(2,1)S(1)} %collective-permute-done.3.rest_4_), channel_id=1, source_target_pairs={{0,4},{4,0},{1,5},{5,1},{2,6},{6,2},{3,7},{7,3},{8,12},{12,8},{9,1... | collective-permute-start | bytes 786440 | tf_op jit(solution)/shard_map/ppermute | solution.py:41
  46.9 3.1 %ffn.1 = (f32[128,1024]{1,0:T(8,128)S(1)}, bf16[128,1024]{1,0:T(8,128)(2,1)S(1)}, bf16[128,1024]{1,0:T(8,128)(2,1)S(1)}, bf16[128,1024]{1,0:T(8,128)(2,1)S(1)}) custom-call(bf16[512,1024]{1,0:T(8,128)(2,1)S(1)} %get-tuple-element.35.x_ref, f32[1,1024]{1,0:T(1,128)S(1)} %get-tuple-element.36.b_ref, bf16[4,32,1024]{2,1,0:T(8,128)(2,1)S(1)} %all-to-all-done.rest_0_, ...), custom_call_target="tpu_custom_call" | custom-call | flops 2147483648 | bytes 8388608 | tf_op jit(solution)/shard_map/ffn/pallas_call | solution.py:374
  50.1 1.3 %collective-permute-start.15 = (bf16[128,1024]{1,0:T(8,128)(2,1)S(1)}, bf16[128,1024]{1,0:T(8,128)(2,1)S(1)}, u32[]{:S(2)}, u32[]{:S(2)}) collective-permute-start(bf16[128,1024]{1,0:T(8,128)(2,1)S(1)} %get-tuple-element.39), channel_id=1, source_target_pairs={{0,1},{1,2},{2,3},{3,0},{4,5},{5,6},{6,7},{7,4},{8,9},{9,10},{10,1... | collective-permute-start | bytes 786440 | tf_op jit(solution)/shard_map/ppermute | solution.py:41
  51.3 2.5 %collective-permute-start.16 = (bf16[128,1024]{1,0:T(8,128)(2,1)S(1)}, bf16[128,1024]{1,0:T(8,128)(2,1)S(1)}, u32[]{:S(2)}, u32[]{:S(2)}) collective-permute-start(bf16[128,1024]{1,0:T(8,128)(2,1)S(1)} %get-tuple-element.41), channel_id=1, source_target_pairs={{0,2},{1,3},{2,0},{3,1},{4,6},{5,7},{6,4},{7,5},{8,10},{9,11},{10,... | collective-permute-start | bytes 786440 | tf_op jit(solution)/shard_map/ppermute | solution.py:41
  53.8 1.1 %collective-permute-start.17 = (bf16[128,1024]{1,0:T(8,128)(2,1)S(1)}, bf16[128,1024]{1,0:T(8,128)(2,1)S(1)}, u32[]{:S(2)}, u32[]{:S(2)}) collective-permute-start(bf16[128,1024]{1,0:T(8,128)(2,1)S(1)} %get-tuple-element.42), channel_id=1, source_target_pairs={{0,3},{1,0},{2,1},{3,2},{4,7},{5,4},{6,5},{7,6},{8,11},{9,8},{10,9... | collective-permute-start | bytes 786440 | tf_op jit(solution)/shard_map/ppermute | solution.py:41
  54.9 3.9 %collective-permute-done.15.r1 = bf16[128,1024]{1,0:T(8,128)(2,1)S(1)} collective-permute-done((bf16[128,1024]{1,0:T(8,128)(2,1)S(1)}, bf16[128,1024]{1,0:T(8,128)(2,1)S(1)}, u32[]{:S(2)}, u32[]{:S(2)}) %collective-permute-start.15) | collective-permute-done | bytes 262176 | tf_op jit(solution)/shard_map/ppermute | solution.py:41
  59.8 5.6 %collective-permute-done.16.r2 = bf16[128,1024]{1,0:T(8,128)(2,1)S(1)} collective-permute-done((bf16[128,1024]{1,0:T(8,128)(2,1)S(1)}, bf16[128,1024]{1,0:T(8,128)(2,1)S(1)}, u32[]{:S(2)}, u32[]{:S(2)}) %collective-permute-start.16) | collective-permute-done | bytes 262176 | tf_op jit(solution)/shard_map/ppermute | solution.py:41
  65.5 1.5 %norm.1 = (bf16[32,1152]{1,0:T(8,128)(2,1)S(1)}, bf16[8,144,256]{2,1,0:T(8,128)(2,1)}) custom-call(f32[128,1024]{1,0:T(8,128)S(1)} %get-tuple-element.38.own, bf16[128,1024]{1,0:T(8,128)(2,1)S(1)} %collective-permute-done.15.r1, bf16[128,1024]{1,0:T(8,128)(2,1)S(1)} %collective-permute-done.16.r2, bf16[128,1024]{1,0:T(8,128)(2,1)S(1)} %collective-permute-done.17.r3, ...), custom_call_target="tpu_custom_call" | custom-call | flops 16777216 | bytes 3145728 | tf_op jit(solution)/shard_map/norm/pallas_call | solution.py:414
  67.7 3.7 %collective-permute-start.20 = (bf16[32,1152]{1,0:T(8,128)(2,1)S(1)}, bf16[32,1152]{1,0:T(8,128)(2,1)S(1)}, u32[]{:S(2)}, u32[]{:S(2)}) collective-permute-start(bf16[32,1152]{1,0:T(8,128)(2,1)S(1)} %get-tuple-element.54), channel_id=1, source_target_pairs={{0,192},{32,224},{64,128},{96,160},{128,64},{160,96},{192,0},{224,... | collective-permute-start | bytes 221192 | tf_op jit(solution)/shard_map/ppermute | solution.py:58
  71.4 4.0 %all-to-all-start.1 = ((bf16[8,144,256]{2,1,0:T(8,128)(2,1)}), bf16[8,144,256]{2,1,0:T(8,128)(2,1)S(1)}, u32[]{:S(2)}, u32[]{:S(2)}) async-start(bf16[8,144,256]{2,1,0:T(8,128)(2,1)} %get-tuple-element.55), calls=%async_computation.1 | async-start | bytes 1179648 | tf_op jit(solution)/shard_map/all_to_all | solution.py:435
  75.6 3.9 %collective-permute-start.22 = (bf16[64,1152]{1,0:T(8,128)(2,1)S(1)}, bf16[64,1152]{1,0:T(8,128)(2,1)S(1)}, u32[]{:S(2)}, u32[]{:S(2)}) collective-permute-start(bf16[64,1152]{1,0:T(8,128)(2,1)S(1)} %pad_maximum_fusion.rest_0_), channel_id=1, source_target_pairs={{0,16},{8,24},{16,0},{24,8},{1,17},{9,25},{17,1},{25,9},{2,18},{10... | collective-permute-start | bytes 442376 | tf_op jit(solution)/shard_map/ppermute | solution.py:41
  79.5 1.5 %collective-permute-start.21 = (bf16[64,1152]{1,0:T(8,128)(2,1)S(1)}, bf16[64,1152]{1,0:T(8,128)(2,1)S(1)}, u32[]{:S(2)}, u32[]{:S(2)}) collective-permute-start(bf16[64,1152]{1,0:T(8,128)(2,1)S(1)} %pad_maximum_fusion.rest_0_), channel_id=1, source_target_pairs={{0,8},{8,16},{16,24},{24,0},{1,9},{9,17},{17,25},{25,1},{2,10},{10... | collective-permute-start | bytes 442376 | tf_op jit(solution)/shard_map/ppermute | solution.py:41
  81.0 2.8 %collective-permute-start.24 = (bf16[64,1152]{1,0:T(8,128)(2,1)S(1)}, bf16[64,1152]{1,0:T(8,128)(2,1)S(1)}, u32[]{:S(2)}, u32[]{:S(2)}) collective-permute-start(bf16[64,1152]{1,0:T(8,128)(2,1)S(1)} %pad_maximum_fusion.rest_0_), channel_id=1, source_target_pairs={{0,4},{4,0},{1,5},{5,1},{2,6},{6,2},{3,7},{7,3},{8,12},{12,8},{9,1... | collective-permute-start | bytes 442376 | tf_op jit(solution)/shard_map/ppermute | solution.py:41
  83.8 2.5 %collective-permute-start.26 = (bf16[64,1152]{1,0:T(8,128)(2,1)S(1)}, bf16[64,1152]{1,0:T(8,128)(2,1)S(1)}, u32[]{:S(2)}, u32[]{:S(2)}) collective-permute-start(bf16[64,1152]{1,0:T(8,128)(2,1)S(1)} %collective-permute-done.22.rest_2_), channel_id=1, source_target_pairs={{0,4},{4,0},{1,5},{5,1},{2,6},{6,2},{3,7},{7,3},{8,12},{12,8},{9,1... | collective-permute-start | bytes 442376 | tf_op jit(solution)/shard_map/ppermute | solution.py:41
  86.2 1.3 %collective-permute-start.27 = (bf16[64,1152]{1,0:T(8,128)(2,1)S(1)}, bf16[64,1152]{1,0:T(8,128)(2,1)S(1)}, u32[]{:S(2)}, u32[]{:S(2)}) collective-permute-start(bf16[64,1152]{1,0:T(8,128)(2,1)S(1)} %collective-permute-done.23.rest_3_), channel_id=1, source_target_pairs={{0,4},{4,0},{1,5},{5,1},{2,6},{6,2},{3,7},{7,3},{8,12},{12,8},{9,1... | collective-permute-start | bytes 442376 | tf_op jit(solution)/shard_map/ppermute | solution.py:41
  88.5 1.3 %collective-permute-done.25.rest_5_ = bf16[64,1152]{1,0:T(8,128)(2,1)S(1)} collective-permute-done((bf16[64,1152]{1,0:T(8,128)(2,1)S(1)}, bf16[64,1152]{1,0:T(8,128)(2,1)S(1)}, u32[]{:S(2)}, u32[]{:S(2)}) %collective-permute-start.25) | collective-permute-done | bytes 147488 | tf_op jit(solution)/shard_map/ppermute | solution.py:41
  89.8 0.8 score.1
  90.6 12.9 %all_to_all.15.arrived = f32[8,16,384]{2,1,0:T(8,128)S(1)} all-to-all(f32[8,16,384]{2,1,0:T(8,128)S(1)} %score.1), channel_id=1, replica_groups=mesh['grp'=2,'zh'=4,'y'=4,'c'=2,'mp'=4] {'grp','mp'}, dimensions={0} | all-to-all | bytes 393216 | tf_op jit(solution)/shard_map/all_to_all | solution.py:463
  103.5 0.8 final.1
  (59 shorter events, 5.9 us)
Async XLA Ops:
  2.4 17.2 %all-to-all-start = ((bf16[4,32,1024]{2,1,0:T(8,128)(2,1)}), bf16[4,32,1024]{2,1,0:T(8,128)(2,1)S(1)}, u32[]{:S(2)}, u32[]{:S(2)}) async-start(bf16[4,32,1024]{2,1,0:T(8,128)(2,1)} %pack.1), calls=%async_computation | async-start | bytes 524288 | tf_op jit(solution)/shard_map/all_to_all | solution.py:356
  19.6 9.5 %collective-permute-start = (bf16[4,32,1024]{2,1,0:T(8,128)(2,1)S(1)}, bf16[4,32,1024]{2,1,0:T(8,128)(2,1)S(1)}, u32[]{:S(2)}, u32[]{:S(2)}) collective-permute-start(bf16[4,32,1024]{2,1,0:T(8,128)(2,1)S(1)} %all-to-all-done.rest_0_), channel_id=1, source_target_pairs={{0,8},{8,16},{16,24},{24,0},{1,9},{9,17},{17,25},{25,1},{2,10},{10... | collective-permute-start | bytes 786440 | tf_op jit(solution)/shard_map/ppermute | solution.py:41
  20.9 9.0 %collective-permute-start.1 = (bf16[4,32,1024]{2,1,0:T(8,128)(2,1)S(1)}, bf16[4,32,1024]{2,1,0:T(8,128)(2,1)S(1)}, u32[]{:S(2)}, u32[]{:S(2)}) collective-permute-start(bf16[4,32,1024]{2,1,0:T(8,128)(2,1)S(1)} %all-to-all-done.rest_0_), channel_id=1, source_target_pairs={{0,24},{8,0},{16,8},{24,16},{1,25},{9,1},{17,9},{25,17},{2,26},{10... | collective-permute-start | bytes 786440 | tf_op jit(solution)/shard_map/ppermute | solution.py:41
  22.3 9.5 %collective-permute-start.2 = (bf16[4,32,1024]{2,1,0:T(8,128)(2,1)S(1)}, bf16[4,32,1024]{2,1,0:T(8,128)(2,1)S(1)}, u32[]{:S(2)}, u32[]{:S(2)}) collective-permute-start(bf16[4,32,1024]{2,1,0:T(8,128)(2,1)S(1)} %all-to-all-done.rest_0_), channel_id=1, source_target_pairs={{0,16},{8,24},{16,0},{24,8},{1,17},{9,25},{17,1},{25,9},{2,18},{10... | collective-permute-start | bytes 786440 | tf_op jit(solution)/shard_map/ppermute | solution.py:41
  23.9 8.6 %collective-permute-start.3 = (bf16[4,32,1024]{2,1,0:T(8,128)(2,1)S(1)}, bf16[4,32,1024]{2,1,0:T(8,128)(2,1)S(1)}, u32[]{:S(2)}, u32[]{:S(2)}) collective-permute-start(bf16[4,32,1024]{2,1,0:T(8,128)(2,1)S(1)} %all-to-all-done.rest_0_), channel_id=1, source_target_pairs={{0,128},{128,0},{32,160},{160,32},{64,192},{192,64},{96,224},{224,... | collective-permute-start | bytes 786440 | tf_op jit(solution)/shard_map/ppermute | solution.py:49
  24.6 12.7 %collective-permute-start.7 = (bf16[4,32,1024]{2,1,0:T(8,128)(2,1)S(1)}, bf16[4,32,1024]{2,1,0:T(8,128)(2,1)S(1)}, u32[]{:S(2)}, u32[]{:S(2)}) collective-permute-start(bf16[4,32,1024]{2,1,0:T(8,128)(2,1)S(1)} %all-to-all-done.rest_0_), channel_id=1, source_target_pairs={{0,4},{4,0},{1,5},{5,1},{2,6},{6,2},{3,7},{7,3},{8,12},{12,8},{9,1... | collective-permute-start | bytes 786440 | tf_op jit(solution)/shard_map/ppermute | solution.py:41
  29.1 8.4 %collective-permute-start.4 = (bf16[4,32,1024]{2,1,0:T(8,128)(2,1)S(1)}, bf16[4,32,1024]{2,1,0:T(8,128)(2,1)S(1)}, u32[]{:S(2)}, u32[]{:S(2)}) collective-permute-start(bf16[4,32,1024]{2,1,0:T(8,128)(2,1)S(1)} %collective-permute-done.rest_1_), channel_id=1, source_target_pairs={{0,224},{224,0},{32,128},{128,32},{64,160},{160,64},{96,192},{192,... | collective-permute-start | bytes 786440 | tf_op jit(solution)/shard_map/ppermute | solution.py:49
  29.9 12.0 %collective-permute-start.5 = (bf16[4,32,1024]{2,1,0:T(8,128)(2,1)S(1)}, bf16[4,32,1024]{2,1,0:T(8,128)(2,1)S(1)}, u32[]{:S(2)}, u32[]{:S(2)}) collective-permute-start(bf16[4,32,1024]{2,1,0:T(8,128)(2,1)S(1)} %collective-permute-done.1.rest_2_), channel_id=1, source_target_pairs={{0,224},{224,0},{32,128},{128,32},{64,160},{160,64},{96,192},{192,... | collective-permute-start | bytes 786440 | tf_op jit(solution)/shard_map/ppermute | solution.py:49
  31.8 12.8 %collective-permute-start.6 = (bf16[4,32,1024]{2,1,0:T(8,128)(2,1)S(1)}, bf16[4,32,1024]{2,1,0:T(8,128)(2,1)S(1)}, u32[]{:S(2)}, u32[]{:S(2)}) collective-permute-start(bf16[4,32,1024]{2,1,0:T(8,128)(2,1)S(1)} %collective-permute-done.2.rest_3_), channel_id=1, source_target_pairs={{0,128},{128,0},{32,160},{160,32},{64,192},{192,64},{96,224},{224,... | collective-permute-start | bytes 786440 | tf_op jit(solution)/shard_map/ppermute | solution.py:49
  32.6 12.1 %collective-permute-start.10 = (bf16[4,32,1024]{2,1,0:T(8,128)(2,1)S(1)}, bf16[4,32,1024]{2,1,0:T(8,128)(2,1)S(1)}, u32[]{:S(2)}, u32[]{:S(2)}) collective-permute-start(bf16[4,32,1024]{2,1,0:T(8,128)(2,1)S(1)} %collective-permute-done.2.rest_3_), channel_id=1, source_target_pairs={{0,4},{4,0},{1,5},{5,1},{2,6},{6,2},{3,7},{7,3},{8,12},{12,8},{9,1... | collective-permute-start | bytes 786440 | tf_op jit(solution)/shard_map/ppermute | solution.py:41
  37.4 7.8 %collective-permute-start.8 = (bf16[4,32,1024]{2,1,0:T(8,128)(2,1)S(1)}, bf16[4,32,1024]{2,1,0:T(8,128)(2,1)S(1)}, u32[]{:S(2)}, u32[]{:S(2)}) collective-permute-start(bf16[4,32,1024]{2,1,0:T(8,128)(2,1)S(1)} %collective-permute-done.rest_1_), channel_id=1, source_target_pairs={{0,4},{4,0},{1,5},{5,1},{2,6},{6,2},{3,7},{7,3},{8,12},{12,8},{9,1... | collective-permute-start | bytes 786440 | tf_op jit(solution)/shard_map/ppermute | solution.py:41
  37.5 7.8 %collective-permute-start.9 = (bf16[4,32,1024]{2,1,0:T(8,128)(2,1)S(1)}, bf16[4,32,1024]{2,1,0:T(8,128)(2,1)S(1)}, u32[]{:S(2)}, u32[]{:S(2)}) collective-permute-start(bf16[4,32,1024]{2,1,0:T(8,128)(2,1)S(1)} %collective-permute-done.1.rest_2_), channel_id=1, source_target_pairs={{0,4},{4,0},{1,5},{5,1},{2,6},{6,2},{3,7},{7,3},{8,12},{12,8},{9,1... | collective-permute-start | bytes 786440 | tf_op jit(solution)/shard_map/ppermute | solution.py:41
  41.8 4.0 %collective-permute-start.11 = (bf16[4,32,1024]{2,1,0:T(8,128)(2,1)S(1)}, bf16[4,32,1024]{2,1,0:T(8,128)(2,1)S(1)}, u32[]{:S(2)}, u32[]{:S(2)}) collective-permute-start(bf16[4,32,1024]{2,1,0:T(8,128)(2,1)S(1)} %collective-permute-done.3.rest_4_), channel_id=1, source_target_pairs={{0,4},{4,0},{1,5},{5,1},{2,6},{6,2},{3,7},{7,3},{8,12},{12,8},{9,1... | collective-permute-start | bytes 786440 | tf_op jit(solution)/shard_map/ppermute | solution.py:41
  44.6 1.5 %collective-permute-start.12 = (bf16[4,32,1024]{2,1,0:T(8,128)(2,1)S(1)}, bf16[4,32,1024]{2,1,0:T(8,128)(2,1)S(1)}, u32[]{:S(2)}, u32[]{:S(2)}) collective-permute-start(bf16[4,32,1024]{2,1,0:T(8,128)(2,1)S(1)} %collective-permute-done.4.rest_5_), channel_id=1, source_target_pairs={{0,4},{4,0},{1,5},{5,1},{2,6},{6,2},{3,7},{7,3},{8,12},{12,8},{9,1... | collective-permute-start | bytes 786440 | tf_op jit(solution)/shard_map/ppermute | solution.py:41
  44.6 1.9 %collective-permute-start.13 = (bf16[4,32,1024]{2,1,0:T(8,128)(2,1)S(1)}, bf16[4,32,1024]{2,1,0:T(8,128)(2,1)S(1)}, u32[]{:S(2)}, u32[]{:S(2)}) collective-permute-start(bf16[4,32,1024]{2,1,0:T(8,128)(2,1)S(1)} %collective-permute-done.5.rest_6_), channel_id=1, source_target_pairs={{0,4},{4,0},{1,5},{5,1},{2,6},{6,2},{3,7},{7,3},{8,12},{12,8},{9,1... | collective-permute-start | bytes 786440 | tf_op jit(solution)/shard_map/ppermute | solution.py:41
  45.2 1.8 %collective-permute-start.14 = (bf16[4,32,1024]{2,1,0:T(8,128)(2,1)S(1)}, bf16[4,32,1024]{2,1,0:T(8,128)(2,1)S(1)}, u32[]{:S(2)}, u32[]{:S(2)}) collective-permute-start(bf16[4,32,1024]{2,1,0:T(8,128)(2,1)S(1)} %collective-permute-done.6.rest_7_), channel_id=1, source_target_pairs={{0,4},{4,0},{1,5},{5,1},{2,6},{6,2},{3,7},{7,3},{8,12},{12,8},{9,1... | collective-permute-start | bytes 786440 | tf_op jit(solution)/shard_map/ppermute | solution.py:41
  46.9 12.0 %copy-start.5 = (s32[8,32]{1,0:T(8,128)S(1)}, s32[8,32]{1,0:T(8,128)}, u32[]{:S(2)}) copy-start(s32[8,32]{1,0:T(8,128)} %negs) | copy-start | bytes 3076
  46.9 12.0 %copy-start.8 = (s32[8]{0:T(128)S(1)}, s32[8]{0:T(128)}, u32[]{:S(2)}) copy-start(s32[8]{0:T(128)} %param.21) | copy-start | bytes 100
  50.1 8.8 %collective-permute-start.15 = (bf16[128,1024]{1,0:T(8,128)(2,1)S(1)}, bf16[128,1024]{1,0:T(8,128)(2,1)S(1)}, u32[]{:S(2)}, u32[]{:S(2)}) collective-permute-start(bf16[128,1024]{1,0:T(8,128)(2,1)S(1)} %get-tuple-element.39), channel_id=1, source_target_pairs={{0,1},{1,2},{2,3},{3,0},{4,5},{5,6},{6,7},{7,4},{8,9},{9,10},{10,1... | collective-permute-start | bytes 786440 | tf_op jit(solution)/shard_map/ppermute | solution.py:41
  51.3 14.1 %collective-permute-start.16 = (bf16[128,1024]{1,0:T(8,128)(2,1)S(1)}, bf16[128,1024]{1,0:T(8,128)(2,1)S(1)}, u32[]{:S(2)}, u32[]{:S(2)}) collective-permute-start(bf16[128,1024]{1,0:T(8,128)(2,1)S(1)} %get-tuple-element.41), channel_id=1, source_target_pairs={{0,2},{1,3},{2,0},{3,1},{4,6},{5,7},{6,4},{7,5},{8,10},{9,11},{10,... | collective-permute-start | bytes 786440 | tf_op jit(solution)/shard_map/ppermute | solution.py:41
  53.8 11.7 %collective-permute-start.17 = (bf16[128,1024]{1,0:T(8,128)(2,1)S(1)}, bf16[128,1024]{1,0:T(8,128)(2,1)S(1)}, u32[]{:S(2)}, u32[]{:S(2)}) collective-permute-start(bf16[128,1024]{1,0:T(8,128)(2,1)S(1)} %get-tuple-element.42), channel_id=1, source_target_pairs={{0,3},{1,0},{2,1},{3,2},{4,7},{5,4},{6,5},{7,6},{8,11},{9,8},{10,9... | collective-permute-start | bytes 786440 | tf_op jit(solution)/shard_map/ppermute | solution.py:41
  66.9 8.6 %collective-permute-start.18 = (bf16[32,1152]{1,0:T(8,128)(2,1)S(1)}, bf16[32,1152]{1,0:T(8,128)(2,1)S(1)}, u32[]{:S(2)}, u32[]{:S(2)}) collective-permute-start(bf16[32,1152]{1,0:T(8,128)(2,1)S(1)} %get-tuple-element.54), channel_id=1, source_target_pairs={{0,224},{32,128},{64,160},{96,192},{128,32},{160,64},{192,96},{224... | collective-permute-start | bytes 221192 | tf_op jit(solution)/shard_map/ppermute | solution.py:58
  67.7 7.8 %collective-permute-start.19 = (bf16[32,1152]{1,0:T(8,128)(2,1)S(1)}, bf16[32,1152]{1,0:T(8,128)(2,1)S(1)}, u32[]{:S(2)}, u32[]{:S(2)}) collective-permute-start(bf16[32,1152]{1,0:T(8,128)(2,1)S(1)} %get-tuple-element.54), channel_id=1, source_target_pairs={{0,96},{32,0},{64,32},{96,64},{128,224},{160,128},{192,160},{224,1... | collective-permute-start | bytes 221192 | tf_op jit(solution)/shard_map/ppermute | solution.py:58
  67.7 7.8 %collective-permute-start.20 = (bf16[32,1152]{1,0:T(8,128)(2,1)S(1)}, bf16[32,1152]{1,0:T(8,128)(2,1)S(1)}, u32[]{:S(2)}, u32[]{:S(2)}) collective-permute-start(bf16[32,1152]{1,0:T(8,128)(2,1)S(1)} %get-tuple-element.54), channel_id=1, source_target_pairs={{0,192},{32,224},{64,128},{96,160},{128,64},{160,96},{192,0},{224,... | collective-permute-start | bytes 221192 | tf_op jit(solution)/shard_map/ppermute | solution.py:58
  71.4 16.1 %all-to-all-start.1 = ((bf16[8,144,256]{2,1,0:T(8,128)(2,1)}), bf16[8,144,256]{2,1,0:T(8,128)(2,1)S(1)}, u32[]{:S(2)}, u32[]{:S(2)}) async-start(bf16[8,144,256]{2,1,0:T(8,128)(2,1)} %get-tuple-element.55), calls=%async_computation.1 | async-start | bytes 1179648 | tf_op jit(solution)/shard_map/all_to_all | solution.py:435
  75.6 8.2 %collective-permute-start.22 = (bf16[64,1152]{1,0:T(8,128)(2,1)S(1)}, bf16[64,1152]{1,0:T(8,128)(2,1)S(1)}, u32[]{:S(2)}, u32[]{:S(2)}) collective-permute-start(bf16[64,1152]{1,0:T(8,128)(2,1)S(1)} %pad_maximum_fusion.rest_0_), channel_id=1, source_target_pairs={{0,16},{8,24},{16,0},{24,8},{1,17},{9,25},{17,1},{25,9},{2,18},{10... | collective-permute-start | bytes 442376 | tf_op jit(solution)/shard_map/ppermute | solution.py:41
  79.5 6.7 %collective-permute-start.23 = (bf16[64,1152]{1,0:T(8,128)(2,1)S(1)}, bf16[64,1152]{1,0:T(8,128)(2,1)S(1)}, u32[]{:S(2)}, u32[]{:S(2)}) collective-permute-start(bf16[64,1152]{1,0:T(8,128)(2,1)S(1)} %pad_maximum_fusion.rest_0_), channel_id=1, source_target_pairs={{0,24},{8,0},{16,8},{24,16},{1,25},{9,1},{17,9},{25,17},{2,26},{10... | collective-permute-start | bytes 442376 | tf_op jit(solution)/shard_map/ppermute | solution.py:41
  79.5 8.8 %collective-permute-start.21 = (bf16[64,1152]{1,0:T(8,128)(2,1)S(1)}, bf16[64,1152]{1,0:T(8,128)(2,1)S(1)}, u32[]{:S(2)}, u32[]{:S(2)}) collective-permute-start(bf16[64,1152]{1,0:T(8,128)(2,1)S(1)} %pad_maximum_fusion.rest_0_), channel_id=1, source_target_pairs={{0,8},{8,16},{16,24},{24,0},{1,9},{9,17},{17,25},{25,1},{2,10},{10... | collective-permute-start | bytes 442376 | tf_op jit(solution)/shard_map/ppermute | solution.py:41
  81.0 7.5 %collective-permute-start.24 = (bf16[64,1152]{1,0:T(8,128)(2,1)S(1)}, bf16[64,1152]{1,0:T(8,128)(2,1)S(1)}, u32[]{:S(2)}, u32[]{:S(2)}) collective-permute-start(bf16[64,1152]{1,0:T(8,128)(2,1)S(1)} %pad_maximum_fusion.rest_0_), channel_id=1, source_target_pairs={{0,4},{4,0},{1,5},{5,1},{2,6},{6,2},{3,7},{7,3},{8,12},{12,8},{9,1... | collective-permute-start | bytes 442376 | tf_op jit(solution)/shard_map/ppermute | solution.py:41
  83.8 4.7 %collective-permute-start.26 = (bf16[64,1152]{1,0:T(8,128)(2,1)S(1)}, bf16[64,1152]{1,0:T(8,128)(2,1)S(1)}, u32[]{:S(2)}, u32[]{:S(2)}) collective-permute-start(bf16[64,1152]{1,0:T(8,128)(2,1)S(1)} %collective-permute-done.22.rest_2_), channel_id=1, source_target_pairs={{0,4},{4,0},{1,5},{5,1},{2,6},{6,2},{3,7},{7,3},{8,12},{12,8},{9,1... | collective-permute-start | bytes 442376 | tf_op jit(solution)/shard_map/ppermute | solution.py:41
  86.2 2.3 %collective-permute-start.27 = (bf16[64,1152]{1,0:T(8,128)(2,1)S(1)}, bf16[64,1152]{1,0:T(8,128)(2,1)S(1)}, u32[]{:S(2)}, u32[]{:S(2)}) collective-permute-start(bf16[64,1152]{1,0:T(8,128)(2,1)S(1)} %collective-permute-done.23.rest_3_), channel_id=1, source_target_pairs={{0,4},{4,0},{1,5},{5,1},{2,6},{6,2},{3,7},{7,3},{8,12},{12,8},{9,1... | collective-permute-start | bytes 442376 | tf_op jit(solution)/shard_map/ppermute | solution.py:41
  88.4 1.5 %collective-permute-start.25 = (bf16[64,1152]{1,0:T(8,128)(2,1)S(1)}, bf16[64,1152]{1,0:T(8,128)(2,1)S(1)}, u32[]{:S(2)}, u32[]{:S(2)}) collective-permute-start(bf16[64,1152]{1,0:T(8,128)(2,1)S(1)} %collective-permute-done.21.rest_1_), channel_id=1, source_target_pairs={{0,4},{4,0},{1,5},{5,1},{2,6},{6,2},{3,7},{7,3},{8,12},{12,8},{9,1... | collective-permute-start | bytes 442376 | tf_op jit(solution)/shard_map/ppermute | solution.py:41
  (7 other events, 25.0 us)

commit v6 on v5

--- a/solution.py
+++ b/solution.py
@@ -70,14 +70,18 @@
     return jnp.where(hit, 1.0, 0.0).astype(BF)
 
 
-def pack_kernel(w_in, w_out_t, packed, sems):
+def pack_kernel(w_in, w_out_t, packed, held, sems):
     shard = w_in.shape[0]
-    copies = []
-    for z in range(packed.shape[0]):
-        copies.append(pltpu.make_async_copy(w_in, packed.at[z, 0:shard], sems.at[2 * z]))
-        copies.append(
-            pltpu.make_async_copy(w_out_t, packed.at[z, shard : 2 * shard], sems.at[2 * z + 1])
-        )
+    n = packed.shape[0]
+    copies = [
+        pltpu.make_async_copy(w_in, held.at[0:shard], sems.at[n]),
+        pltpu.make_async_copy(w_out_t, held.at[shard : 2 * shard], sems.at[n + 1]),
+    ]
+    for copy in copies:
+        copy.start()
+    for copy in copies:
+        copy.wait()
+    copies = [pltpu.make_async_copy(held, packed.at[z], sems.at[z]) for z in range(n)]
     for copy in copies:
         copy.start()
     for copy in copies:
@@ -186,13 +190,12 @@
     lists = jnp.where(lane == 2 * n_neg, n_used, lists)
     lists = jnp.where(lane == 2 * n_neg + 1, (pos // DIGIT).astype(F32), lists)
     lists = jnp.where(lane == 2 * n_neg + 2, (pos % DIGIT).astype(F32), lists)
-    r8, c8 = iota((16, own_q), 0), iota((16, own_q), 1)
-    base = N_MP * n_q
-    move = onehot((r8 >= base) & (r8 < base + n_q) & (c8 == m * n_q + r8 - base))
-    lists_ref[...] = jnp.dot(move, lists.astype(BF), preferred_element_type=F32)
-
-
-def norm_kernel(own, r1, r2, r3, vectors, live, count, lists, p_ref, send):
+    r8, c8 = iota((n_pass, own_q), 0), iota((n_pass, own_q), 1)
+    move = onehot((r8 < n_q) & (c8 == m * n_q + r8))
+    lists_ref[...] = jnp.dot(move, lists.astype(BF), preferred_element_type=F32).astype(BF)
+
+
+def norm_kernel(own, r1, r2, r3, vectors, live, count, lists, p_ref, coded_ref):
     rows, width = own.shape
     summed = own[...] + r1[...].astype(F32) + r2[...].astype(F32) + r3[...].astype(F32)
     summed = summed + vectors[0:1, :]
@@ -203,38 +206,37 @@
 
     n_pass = p_ref.shape[0]
     p = (jnp.dot(live[...], coded, preferred_element_type=F32) / count[:, 0:1]).astype(BF)
-    p_ref[:, :width] = p
+    n_pass = p_ref.shape[0]
     pf = p.astype(F32)
     square = pieces(jnp.sum(pf * pf, axis=1, keepdims=True))
     lane = iota((n_pass, 128), 1)
     tail = jnp.zeros((n_pass, 128), F32)
     for i, piece in enumerate(square):
         tail = jnp.where(lane == i, piece.astype(F32), tail)
-    p_ref[:, width:] = tail.astype(BF)
-
-    pick = onehot(iota((16, rows), 1) // QLEN == iota((16, rows), 0))
+    n_pass = p_ref.shape[0]
+    pick = onehot(iota((n_pass, rows), 1) // QLEN == iota((n_pass, rows), 0))
     q = (jnp.dot(pick, coded, preferred_element_type=F32) * (1.0 / QLEN)).astype(BF)
-    part = send.shape[2]
-    block = lists[...]
-    r16, c16 = iota((16, 16), 0), iota((16, 16), 1)
+    refresh = at("grp") == 1
+    p_ref[:, :width] = jnp.where(refresh, p, q)
+    p_ref[:, width:] = jnp.where(refresh, tail.astype(BF), lists[...])
+    coded_ref[...] = coded
+
+
+def send_kernel(coded, mine, came, send):
+    rows, width = coded.shape
+    part = width // N_MP
     n_q = rows // QLEN
+    rider = jnp.where(at("grp") == 1, came[0:16, :], mine[0:16, :])
+    parts = [rider[:, j * part : (j + 1) * part] for j in range(N_MP)]
+    lists = jnp.concatenate([rider[:, width:], rider[:, width:]], axis=1)
+    stacked = jnp.concatenate(parts + [lists], axis=0)
+    shape = (16, 16 * (N_MP + 1))
+    to, come = iota(shape, 0), iota(shape, 1)
+    move = onehot((to == come // 16 * n_q + come % 16) & (come % 16 < n_q))
+    block = jnp.dot(move, stacked, preferred_element_type=F32).astype(BF)
     for j in range(N_MP):
-        move = onehot((r16 == c16 + j * n_q) & (c16 < n_q))
-        block = block + jnp.dot(
-            move, q[:, j * part : (j + 1) * part], preferred_element_type=F32
-        )
-    block = block.astype(BF)
-    for g in range(N_GRP):
-        for j in range(N_MP):
-            send[g * N_MP + j, :rows, :] = coded[:, j * part : (j + 1) * part]
-            send[g * N_MP + j, rows:, :] = block
-
-
-def unpack_kernel(arrived, encoded):
-    grp = at("grp")
-    rows = encoded.shape[0] // N_MP
-    for j in range(N_MP):
-        encoded[j * rows : (j + 1) * rows, :] = arrived[grp * N_MP + j, 0:rows, :]
+        send[j, :rows, :] = coded[:, j * part : (j + 1) * part]
+        send[j, rows:, :] = block
 
 
 def query_kernel(arrived, q_ref, lists):
@@ -249,6 +251,12 @@
     for j in range(N_MP):
         q_ref[:, j * part : (j + 1) * part] = got[16 * j : 16 * (j + 1)].astype(BF)
     lists[...] = got[16 * N_MP :]
+
+
+def unpack_kernel(arrived, encoded):
+    rows = encoded.shape[0] // N_MP
+    for j in range(N_MP):
+        encoded[j * rows : (j + 1) * rows, :] = arrived[j, 0:rows, :]
 
 
 def score_kernel(q_ref, lists_ref, *rest):
@@ -284,7 +292,9 @@
     lane = iota((1, n_p), 1)
     per_core = size * N_Y
     core = lax.rem(c + lane // per_core, N_C)
-    line = lax.rem(y - lax.rem(lane, per_core) // size + N_Y, N_Y)
+    turn = lax.rem(lane, per_core) // size
+    turn = jnp.where(turn < 2, turn, 5 - turn)
+    line = lax.rem(y - turn + N_Y, N_Y)
     piece = lax.rem(lane, size) // each
     slab = lax.rem(zh + g * piece + (1 - g) * (N_ZH - 1) * (1 + piece), N_ZH)
     number = ((slab * N_Y + line) * N_C + core) * (each * N_MP) + m * each + lax.rem(lane, each)
@@ -349,7 +359,10 @@
         out_shape=shape((N_ZH, 2 * shard, hid), BF),
         in_specs=[HBM] * 2,
         out_specs=VMEM,
-        scratch_shapes=[pltpu.SemaphoreType.DMA((2 * N_ZH,))],
+        scratch_shapes=[
+            pltpu.VMEM((2 * shard, hid), BF),
+            pltpu.SemaphoreType.DMA((N_ZH + 2,)),
+        ],
         compiler_params=params(60),
         name="pack",
     )(w_in, w_out.T)
@@ -386,7 +399,7 @@
         cost_estimate=cost(4 * rows * width * hid, 8 << 20),
         name="ffn",
     )(x, b_in, *lines)
-    r2, r1, r3 = shift(s2, "mp", 2), shift(s1, "mp", 1), shift(s3, "mp", 3)
+    r1, r3, r2 = shift(s1, "mp", 1), shift(s3, "mp", 3), shift(s2, "mp", 2)
     small = [
         b_out[None],
         ln_gain[None],
@@ -403,7 +416,7 @@
             shape((3, width), F32),
             shape((n_pass, part_rows), BF),
             shape((n_pass, 128), F32),
-            shape((16, part), F32),
+            shape((n_pass, 128), BF),
         ],
         in_specs=[VMEM] * 7,
         out_specs=[VMEM] * 4,
@@ -411,28 +424,36 @@
         name="prep",
     )(*small)
 
-    passages, send = pl.pallas_call(
+    passages, coded = pl.pallas_call(
         norm_kernel,
         out_shape=[
             shape((n_pass, width + 128), BF),
-            shape((peers, part_rows + 16, part), BF),
+            shape((part_rows, width), BF),
         ],
         in_specs=[VMEM] * 8,
         out_specs=[VMEM] * 2,
         compiler_params=params(),
         cost_estimate=cost(2 * part_rows * width * 64, 3 << 20),
         name="norm",
-    )(own, r1, r2, r3, vectors, live, count, lists)
-
+    )(own, r1, r3, r2, vectors, live, count, lists)
+
+    near = reroute(passages, lambda g, z: (1 - g, z + 1 if g else z))
+    mid = reroute(passages, lambda g, z: (g, z - 1))
     far = reroute(passages, lambda g, z: (1 - g, z - 2 if g else z + 2))
-    mid = reroute(passages, lambda g, z: (g, z - 1))
-    near = reroute(passages, lambda g, z: (1 - g, z + 1 if g else z - 1))
     refresh = at("grp") == 1
     slab = jnp.concatenate(
         [jnp.where(refresh, passages, near), jnp.where(refresh, mid, far)], axis=0
     )
-    lines = [slab] + [shift(slab, "y", k) for k in (1, 2, 3)]
-    arrived = lax.all_to_all(send, ("grp", "mp"), 0, 0, tiled=True)
+    lines = [slab] + [shift(slab, "y", k) for k in Y_ORDER]
+    send = pl.pallas_call(
+        send_kernel,
+        out_shape=shape((N_MP, part_rows + 16, part), BF),
+        in_specs=[VMEM] * 3,
+        out_specs=VMEM,
+        compiler_params=params(),
+        name="send",
+    )(coded, passages, near)
+    arrived = lax.all_to_all(send, "mp", 0, 0, tiled=True)
     q_all, lists = pl.pallas_call(
         query_kernel,
         out_shape=[shape((16, width), BF), shape((16, part), F32)],
@@ -449,7 +470,8 @@
         compiler_params=params(),
         name="unpack",
     )(arrived)
-    lines[1], q_all, encoded = lax.optimization_barrier((lines[1], q_all, encoded))
+    lines[3], q_all = lax.optimization_barrier((lines[3], q_all))
+    lines[2], encoded = lax.optimization_barrier((lines[2], encoded))
     lines = lines + [shift(v, "c", 1) for v in lines]
     shares = pl.pallas_call(
         score_kernel,

time: 105 us -> 102 us (0.971)
  blocking collectives: 12.9 us -> 10.2 us
    all_to_all x1, blocking collectives: 12.9 us -> 10.2 us  [body(): arrived = lax.all_to_all(shares, ('grp', 'mp'), 0, 0, tiled=True)]
  transfers between devices with their start and end apart: 30 -> 30, of which waited for: 8 -> 10; matrix products, arithmetic and copies ran while one was open for 0% -> 0% of each run, Pallas kernels for 1% -> 1%
where the time goes in v6:
time: 102 us
  starting transfers between devices  59.3 us (58%)
  waiting for transfers between devices  20.1 us (20%)
  blocking collectives  10.2 us (10%)
  Pallas kernels  9.14 us (9%)
  local copies, waits for them, and re-layouts  1.91 us (2%)
    ppermute x21, starting transfers between devices, shift(): lax.ppermute(block, axis, [(i, (i + distance) % n) for i in range(n)])  38 us
    ppermute x21, waiting for transfers between devices, shift(): lax.ppermute(block, axis, [(i, (i + distance) % n) for i in range(n)])  13.2 us
    all_to_all x1, blocking collectives, body(): arrived = lax.all_to_all(shares, ('grp', 'mp'), 0, 0, tiled=True)  10.2 us
    all_to_all x1, starting transfers between devices, body(): lines = [lax.all_to_all(packed, 'zh', 0, 0, tiled=True)]  9.02 us
    all_to_all x1, waiting for transfers between devices, body(): lines = [lax.all_to_all(packed, 'zh', 0, 0, tiled=True)]  6.84 us
    ppermute x3, starting transfers between devices, reroute(): return lax.ppermute(block, ('grp', 'zh'), route)  4.67 us
    ppermute x4, starting transfers between devices, cross(): return lax.ppermute(block, ('grp', 'zh'), route)  4.19 us
    all_to_all x1, starting transfers between devices, body(): arrived = lax.all_to_all(send, 'mp', 0, 0, tiled=True)  3.45 us
  transfers between devices with their start and end apart: 30, of which 10 were waited for; matrix products, arithmetic and copies ran while one was open for 0% of the time, Pallas kernels for 1%

profile of v6, /device:TPU:1, one launch (start us, length us, event | category | flops | bytes accessed | tf_op | source)
XLA Modules:
  0.0 101.6 jit_solution(4275959976958544468)
XLA Ops:
  0.6 1.8 %pack.1 = bf16[4,32,1024]{2,1,0:T(8,128)(2,1)} custom-call(bf16[16,1024]{1,0:T(8,128)(2,1)} %w_in.1, bf16[16,1024]{1,0:T(8,128)(2,1)} %bitcast.20), custom_call_target="tpu_custom_call" | custom-call | tf_op jit(solution)/shard_map/pack/pallas_call | solution.py:357
  2.5 9.0 %all-to-all-start = ((bf16[4,32,1024]{2,1,0:T(8,128)(2,1)}), bf16[4,32,1024]{2,1,0:T(8,128)(2,1)S(1)}, u32[]{:S(2)}, u32[]{:S(2)}) async-start(bf16[4,32,1024]{2,1,0:T(8,128)(2,1)} %pack.1), calls=%async_computation | async-start | bytes 524288 | tf_op jit(solution)/shard_map/all_to_all | solution.py:369
  11.5 1.2 %copy-done = bf16[1,512,1024]{2,1,0:T(8,128)(2,1)S(1)} copy-done((bf16[1,512,1024]{2,1,0:T(8,128)(2,1)S(1)}, bf16[1,512,1024]{2,1,0:T(8,128)(2,1)}, u32[]{:S(2)}) %copy-start) | copy-done | bytes 1048600
  12.8 6.8 %all-to-all-done.rest_0_ = bf16[4,32,1024]{2,1,0:T(8,128)(2,1)S(1)} async-done(((bf16[4,32,1024]{2,1,0:T(8,128)(2,1)}), bf16[4,32,1024]{2,1,0:T(8,128)(2,1)S(1)}, u32[]{:S(2)}, u32[]{:S(2)}) %all-to-all-start) | async-done | bytes 262176 | tf_op jit(solution)/shard_map/all_to_all | solution.py:369
  19.7 1.3 %collective-permute-start = (bf16[4,32,1024]{2,1,0:T(8,128)(2,1)S(1)}, bf16[4,32,1024]{2,1,0:T(8,128)(2,1)S(1)}, u32[]{:S(2)}, u32[]{:S(2)}) collective-permute-start(bf16[4,32,1024]{2,1,0:T(8,128)(2,1)S(1)} %all-to-all-done.rest_0_), channel_id=1, source_target_pairs={{0,8},{8,16},{16,24},{24,0},{1,9},{9,17},{17,25},{25,1},{2,10},{10... | collective-permute-start | bytes 786440 | tf_op jit(solution)/shard_map/ppermute | solution.py:41
  21.0 1.4 %collective-permute-start.1 = (bf16[4,32,1024]{2,1,0:T(8,128)(2,1)S(1)}, bf16[4,32,1024]{2,1,0:T(8,128)(2,1)S(1)}, u32[]{:S(2)}, u32[]{:S(2)}) collective-permute-start(bf16[4,32,1024]{2,1,0:T(8,128)(2,1)S(1)} %all-to-all-done.rest_0_), channel_id=1, source_target_pairs={{0,24},{8,0},{16,8},{24,16},{1,25},{9,1},{17,9},{25,17},{2,26},{10... | collective-permute-start | bytes 786440 | tf_op jit(solution)/shard_map/ppermute | solution.py:41
  22.4 1.6 %collective-permute-start.2 = (bf16[4,32,1024]{2,1,0:T(8,128)(2,1)S(1)}, bf16[4,32,1024]{2,1,0:T(8,128)(2,1)S(1)}, u32[]{:S(2)}, u32[]{:S(2)}) collective-permute-start(bf16[4,32,1024]{2,1,0:T(8,128)(2,1)S(1)} %all-to-all-done.rest_0_), channel_id=1, source_target_pairs={{0,16},{8,24},{16,0},{24,8},{1,17},{9,25},{17,1},{25,9},{2,18},{10... | collective-permute-start | bytes 786440 | tf_op jit(solution)/shard_map/ppermute | solution.py:41
  24.8 4.4 %collective-permute-start.7 = (bf16[4,32,1024]{2,1,0:T(8,128)(2,1)S(1)}, bf16[4,32,1024]{2,1,0:T(8,128)(2,1)S(1)}, u32[]{:S(2)}, u32[]{:S(2)}) collective-permute-start(bf16[4,32,1024]{2,1,0:T(8,128)(2,1)S(1)} %all-to-all-done.rest_0_), channel_id=1, source_target_pairs={{0,4},{4,0},{1,5},{5,1},{2,6},{6,2},{3,7},{7,3},{8,12},{12,8},{9,1... | collective-permute-start | bytes 786440 | tf_op jit(solution)/shard_map/ppermute | solution.py:41
  29.2 0.8 collective-permute-start.4
  30.0 1.9 %collective-permute-start.5 = (bf16[4,32,1024]{2,1,0:T(8,128)(2,1)S(1)}, bf16[4,32,1024]{2,1,0:T(8,128)(2,1)S(1)}, u32[]{:S(2)}, u32[]{:S(2)}) collective-permute-start(bf16[4,32,1024]{2,1,0:T(8,128)(2,1)S(1)} %collective-permute-done.1.rest_2_), channel_id=1, source_target_pairs={{0,224},{224,0},{32,128},{128,32},{64,160},{160,64},{96,192},{192,... | collective-permute-start | bytes 786440 | tf_op jit(solution)/shard_map/ppermute | solution.py:49
  31.9 0.8 collective-permute-start.6
  32.7 4.8 %collective-permute-start.10 = (bf16[4,32,1024]{2,1,0:T(8,128)(2,1)S(1)}, bf16[4,32,1024]{2,1,0:T(8,128)(2,1)S(1)}, u32[]{:S(2)}, u32[]{:S(2)}) collective-permute-start(bf16[4,32,1024]{2,1,0:T(8,128)(2,1)S(1)} %collective-permute-done.2.rest_3_), channel_id=1, source_target_pairs={{0,4},{4,0},{1,5},{5,1},{2,6},{6,2},{3,7},{7,3},{8,12},{12,8},{9,1... | collective-permute-start | bytes 786440 | tf_op jit(solution)/shard_map/ppermute | solution.py:41
  37.6 4.3 %collective-permute-start.9 = (bf16[4,32,1024]{2,1,0:T(8,128)(2,1)S(1)}, bf16[4,32,1024]{2,1,0:T(8,128)(2,1)S(1)}, u32[]{:S(2)}, u32[]{:S(2)}) collective-permute-start(bf16[4,32,1024]{2,1,0:T(8,128)(2,1)S(1)} %collective-permute-done.1.rest_2_), channel_id=1, source_target_pairs={{0,4},{4,0},{1,5},{5,1},{2,6},{6,2},{3,7},{7,3},{8,12},{12,8},{9,1... | collective-permute-start | bytes 786440 | tf_op jit(solution)/shard_map/ppermute | solution.py:41
  41.9 2.8 %collective-permute-start.11 = (bf16[4,32,1024]{2,1,0:T(8,128)(2,1)S(1)}, bf16[4,32,1024]{2,1,0:T(8,128)(2,1)S(1)}, u32[]{:S(2)}, u32[]{:S(2)}) collective-permute-start(bf16[4,32,1024]{2,1,0:T(8,128)(2,1)S(1)} %collective-permute-done.3.rest_4_), channel_id=1, source_target_pairs={{0,4},{4,0},{1,5},{5,1},{2,6},{6,2},{3,7},{7,3},{8,12},{12,8},{9,1... | collective-permute-start | bytes 786440 | tf_op jit(solution)/shard_map/ppermute | solution.py:41
  47.0 3.1 %ffn.1 = (f32[128,1024]{1,0:T(8,128)S(1)}, bf16[128,1024]{1,0:T(8,128)(2,1)S(1)}, bf16[128,1024]{1,0:T(8,128)(2,1)S(1)}, bf16[128,1024]{1,0:T(8,128)(2,1)S(1)}) custom-call(bf16[512,1024]{1,0:T(8,128)(2,1)S(1)} %get-tuple-element.36.x_ref, f32[1,1024]{1,0:T(1,128)S(1)} %get-tuple-element.37.b_ref, bf16[4,32,1024]{2,1,0:T(8,128)(2,1)S(1)} %all-to-all-done.rest_0_, ...), custom_call_target="tpu_custom_call" | custom-call | flops 2147483648 | bytes 8388608 | tf_op jit(solution)/shard_map/ffn/pallas_call | solution.py:387
  50.2 1.3 %collective-permute-start.15 = (bf16[128,1024]{1,0:T(8,128)(2,1)S(1)}, bf16[128,1024]{1,0:T(8,128)(2,1)S(1)}, u32[]{:S(2)}, u32[]{:S(2)}) collective-permute-start(bf16[128,1024]{1,0:T(8,128)(2,1)S(1)} %get-tuple-element.40), channel_id=1, source_target_pairs={{0,1},{1,2},{2,3},{3,0},{4,5},{5,6},{6,7},{7,4},{8,9},{9,10},{10,1... | collective-permute-start | bytes 786440 | tf_op jit(solution)/shard_map/ppermute | solution.py:41
  51.5 1.5 %collective-permute-start.16 = (bf16[128,1024]{1,0:T(8,128)(2,1)S(1)}, bf16[128,1024]{1,0:T(8,128)(2,1)S(1)}, u32[]{:S(2)}, u32[]{:S(2)}) collective-permute-start(bf16[128,1024]{1,0:T(8,128)(2,1)S(1)} %get-tuple-element.42), channel_id=1, source_target_pairs={{0,3},{1,0},{2,1},{3,2},{4,7},{5,4},{6,5},{7,6},{8,11},{9,8},{10,9... | collective-permute-start | bytes 786440 | tf_op jit(solution)/shard_map/ppermute | solution.py:41
  53.0 1.5 %collective-permute-start.17 = (bf16[128,1024]{1,0:T(8,128)(2,1)S(1)}, bf16[128,1024]{1,0:T(8,128)(2,1)S(1)}, u32[]{:S(2)}, u32[]{:S(2)}) collective-permute-start(bf16[128,1024]{1,0:T(8,128)(2,1)S(1)} %get-tuple-element.43), channel_id=1, source_target_pairs={{0,2},{1,3},{2,0},{3,1},{4,6},{5,7},{6,4},{7,5},{8,10},{9,11},{10,... | collective-permute-start | bytes 786440 | tf_op jit(solution)/shard_map/ppermute | solution.py:41
  54.5 4.5 %collective-permute-done.15.r1 = bf16[128,1024]{1,0:T(8,128)(2,1)S(1)} collective-permute-done((bf16[128,1024]{1,0:T(8,128)(2,1)S(1)}, bf16[128,1024]{1,0:T(8,128)(2,1)S(1)}, u32[]{:S(2)}, u32[]{:S(2)}) %collective-permute-start.15) | collective-permute-done | bytes 262176 | tf_op jit(solution)/shard_map/ppermute | solution.py:41
  59.9 5.6 %collective-permute-done.17.r3 = bf16[128,1024]{1,0:T(8,128)(2,1)S(1)} collective-permute-done((bf16[128,1024]{1,0:T(8,128)(2,1)S(1)}, bf16[128,1024]{1,0:T(8,128)(2,1)S(1)}, u32[]{:S(2)}, u32[]{:S(2)}) %collective-permute-start.17) | collective-permute-done | bytes 262176 | tf_op jit(solution)/shard_map/ppermute | solution.py:41
  66.2 1.9 %collective-permute-start.19 = (bf16[32,1152]{1,0:T(8,128)(2,1)S(1)}, bf16[32,1152]{1,0:T(8,128)(2,1)S(1)}, u32[]{:S(2)}, u32[]{:S(2)}) collective-permute-start(bf16[32,1152]{1,0:T(8,128)(2,1)S(1)} %get-tuple-element.55.mine), channel_id=1, source_target_pairs={{0,96},{32,0},{64,32},{96,64},{128,224},{160,128},{192,160},{224,1... | collective-permute-start | bytes 221192 | tf_op jit(solution)/shard_map/ppermute | solution.py:58
  68.2 2.7 %collective-permute-start.20 = (bf16[32,1152]{1,0:T(8,128)(2,1)S(1)}, bf16[32,1152]{1,0:T(8,128)(2,1)S(1)}, u32[]{:S(2)}, u32[]{:S(2)}) collective-permute-start(bf16[32,1152]{1,0:T(8,128)(2,1)S(1)} %get-tuple-element.55.mine), channel_id=1, source_target_pairs={{0,192},{32,224},{64,128},{96,160},{128,64},{160,96},{192,0},{224,... | collective-permute-start | bytes 221192 | tf_op jit(solution)/shard_map/ppermute | solution.py:58
  70.8 0.9 send.1
  71.7 3.5 %all-to-all-start.1 = ((bf16[4,144,256]{2,1,0:T(8,128)(2,1)}), bf16[4,144,256]{2,1,0:T(8,128)(2,1)S(1)}, u32[]{:S(2)}, u32[]{:S(2)}) async-start(bf16[4,144,256]{2,1,0:T(8,128)(2,1)} %send.1), calls=%async_computation.1 | async-start | bytes 589824 | tf_op jit(solution)/shard_map/all_to_all | solution.py:456
  75.8 3.9 %collective-permute-start.22 = (bf16[64,1152]{1,0:T(8,128)(2,1)S(1)}, bf16[64,1152]{1,0:T(8,128)(2,1)S(1)}, u32[]{:S(2)}, u32[]{:S(2)}) collective-permute-start(bf16[64,1152]{1,0:T(8,128)(2,1)S(1)} %pad_maximum_fusion.rest_0_), channel_id=1, source_target_pairs={{0,16},{8,24},{16,0},{24,8},{1,17},{9,25},{17,1},{25,9},{2,18},{10... | collective-permute-start | bytes 442376 | tf_op jit(solution)/shard_map/ppermute | solution.py:41
  79.7 1.5 %collective-permute-start.21 = (bf16[64,1152]{1,0:T(8,128)(2,1)S(1)}, bf16[64,1152]{1,0:T(8,128)(2,1)S(1)}, u32[]{:S(2)}, u32[]{:S(2)}) collective-permute-start(bf16[64,1152]{1,0:T(8,128)(2,1)S(1)} %pad_maximum_fusion.rest_0_), channel_id=1, source_target_pairs={{0,24},{8,0},{16,8},{24,16},{1,25},{9,1},{17,9},{25,17},{2,26},{10... | collective-permute-start | bytes 442376 | tf_op jit(solution)/shard_map/ppermute | solution.py:41
  81.2 3.4 %collective-permute-start.24 = (bf16[64,1152]{1,0:T(8,128)(2,1)S(1)}, bf16[64,1152]{1,0:T(8,128)(2,1)S(1)}, u32[]{:S(2)}, u32[]{:S(2)}) collective-permute-start(bf16[64,1152]{1,0:T(8,128)(2,1)S(1)} %pad_maximum_fusion.rest_0_), channel_id=1, source_target_pairs={{0,4},{4,0},{1,5},{5,1},{2,6},{6,2},{3,7},{7,3},{8,12},{12,8},{9,1... | collective-permute-start | bytes 442376 | tf_op jit(solution)/shard_map/ppermute | solution.py:41
  84.7 1.3 %collective-permute-start.25 = (bf16[64,1152]{1,0:T(8,128)(2,1)S(1)}, bf16[64,1152]{1,0:T(8,128)(2,1)S(1)}, u32[]{:S(2)}, u32[]{:S(2)}) collective-permute-start(bf16[64,1152]{1,0:T(8,128)(2,1)S(1)} %collective-permute-done.23.rest_1_), channel_id=1, source_target_pairs={{0,4},{4,0},{1,5},{5,1},{2,6},{6,2},{3,7},{7,3},{8,12},{12,8},{9,1... | collective-permute-start | bytes 442376 | tf_op jit(solution)/shard_map/ppermute | solution.py:41
  86.1 1.6 %collective-permute-start.27 = (bf16[64,1152]{1,0:T(8,128)(2,1)S(1)}, bf16[64,1152]{1,0:T(8,128)(2,1)S(1)}, u32[]{:S(2)}, u32[]{:S(2)}) collective-permute-start(bf16[64,1152]{1,0:T(8,128)(2,1)S(1)} %collective-permute-done.22.rest_3_), channel_id=1, source_target_pairs={{0,4},{4,0},{1,5},{5,1},{2,6},{6,2},{3,7},{7,3},{8,12},{12,8},{9,1... | collective-permute-start | bytes 442376 | tf_op jit(solution)/shard_map/ppermute | solution.py:41
  88.7 1.1 %collective-permute-done.26.rest_6_ = bf16[64,1152]{1,0:T(8,128)(2,1)S(1)} collective-permute-done((bf16[64,1152]{1,0:T(8,128)(2,1)S(1)}, bf16[64,1152]{1,0:T(8,128)(2,1)S(1)}, u32[]{:S(2)}, u32[]{:S(2)}) %collective-permute-start.26) | collective-permute-done | bytes 147488 | tf_op jit(solution)/shard_map/ppermute | solution.py:41
  89.8 0.8 score.1
  90.6 10.2 %all_to_all.15.arrived = f32[8,16,384]{2,1,0:T(8,128)S(1)} all-to-all(f32[8,16,384]{2,1,0:T(8,128)S(1)} %score.1), channel_id=1, replica_groups=mesh['grp'=2,'zh'=4,'y'=4,'c'=2,'mp'=4] {'grp','mp'}, dimensions={0} | all-to-all | bytes 393216 | tf_op jit(solution)/shard_map/all_to_all | solution.py:485
  (60 shorter events, 7.3 us)
Async XLA Ops:
  2.5 17.2 %all-to-all-start = ((bf16[4,32,1024]{2,1,0:T(8,128)(2,1)}), bf16[4,32,1024]{2,1,0:T(8,128)(2,1)S(1)}, u32[]{:S(2)}, u32[]{:S(2)}) async-start(bf16[4,32,1024]{2,1,0:T(8,128)(2,1)} %pack.1), calls=%async_computation | async-start | bytes 524288 | tf_op jit(solution)/shard_map/all_to_all | solution.py:369
  19.7 9.5 %collective-permute-start = (bf16[4,32,1024]{2,1,0:T(8,128)(2,1)S(1)}, bf16[4,32,1024]{2,1,0:T(8,128)(2,1)S(1)}, u32[]{:S(2)}, u32[]{:S(2)}) collective-permute-start(bf16[4,32,1024]{2,1,0:T(8,128)(2,1)S(1)} %all-to-all-done.rest_0_), channel_id=1, source_target_pairs={{0,8},{8,16},{16,24},{24,0},{1,9},{9,17},{17,25},{25,1},{2,10},{10... | collective-permute-start | bytes 786440 | tf_op jit(solution)/shard_map/ppermute | solution.py:41
  21.0 9.0 %collective-permute-start.1 = (bf16[4,32,1024]{2,1,0:T(8,128)(2,1)S(1)}, bf16[4,32,1024]{2,1,0:T(8,128)(2,1)S(1)}, u32[]{:S(2)}, u32[]{:S(2)}) collective-permute-start(bf16[4,32,1024]{2,1,0:T(8,128)(2,1)S(1)} %all-to-all-done.rest_0_), channel_id=1, source_target_pairs={{0,24},{8,0},{16,8},{24,16},{1,25},{9,1},{17,9},{25,17},{2,26},{10... | collective-permute-start | bytes 786440 | tf_op jit(solution)/shard_map/ppermute | solution.py:41
  22.4 9.5 %collective-permute-start.2 = (bf16[4,32,1024]{2,1,0:T(8,128)(2,1)S(1)}, bf16[4,32,1024]{2,1,0:T(8,128)(2,1)S(1)}, u32[]{:S(2)}, u32[]{:S(2)}) collective-permute-start(bf16[4,32,1024]{2,1,0:T(8,128)(2,1)S(1)} %all-to-all-done.rest_0_), channel_id=1, source_target_pairs={{0,16},{8,24},{16,0},{24,8},{1,17},{9,25},{17,1},{25,9},{2,18},{10... | collective-permute-start | bytes 786440 | tf_op jit(solution)/shard_map/ppermute | solution.py:41
  24.1 8.6 %collective-permute-start.3 = (bf16[4,32,1024]{2,1,0:T(8,128)(2,1)S(1)}, bf16[4,32,1024]{2,1,0:T(8,128)(2,1)S(1)}, u32[]{:S(2)}, u32[]{:S(2)}) collective-permute-start(bf16[4,32,1024]{2,1,0:T(8,128)(2,1)S(1)} %all-to-all-done.rest_0_), channel_id=1, source_target_pairs={{0,128},{128,0},{32,160},{160,32},{64,192},{192,64},{96,224},{224,... | collective-permute-start | bytes 786440 | tf_op jit(solution)/shard_map/ppermute | solution.py:49
  24.8 12.7 %collective-permute-start.7 = (bf16[4,32,1024]{2,1,0:T(8,128)(2,1)S(1)}, bf16[4,32,1024]{2,1,0:T(8,128)(2,1)S(1)}, u32[]{:S(2)}, u32[]{:S(2)}) collective-permute-start(bf16[4,32,1024]{2,1,0:T(8,128)(2,1)S(1)} %all-to-all-done.rest_0_), channel_id=1, source_target_pairs={{0,4},{4,0},{1,5},{5,1},{2,6},{6,2},{3,7},{7,3},{8,12},{12,8},{9,1... | collective-permute-start | bytes 786440 | tf_op jit(solution)/shard_map/ppermute | solution.py:41
  29.2 8.4 %collective-permute-start.4 = (bf16[4,32,1024]{2,1,0:T(8,128)(2,1)S(1)}, bf16[4,32,1024]{2,1,0:T(8,128)(2,1)S(1)}, u32[]{:S(2)}, u32[]{:S(2)}) collective-permute-start(bf16[4,32,1024]{2,1,0:T(8,128)(2,1)S(1)} %collective-permute-done.rest_1_), channel_id=1, source_target_pairs={{0,224},{224,0},{32,128},{128,32},{64,160},{160,64},{96,192},{192,... | collective-permute-start | bytes 786440 | tf_op jit(solution)/shard_map/ppermute | solution.py:49
  30.0 12.0 %collective-permute-start.5 = (bf16[4,32,1024]{2,1,0:T(8,128)(2,1)S(1)}, bf16[4,32,1024]{2,1,0:T(8,128)(2,1)S(1)}, u32[]{:S(2)}, u32[]{:S(2)}) collective-permute-start(bf16[4,32,1024]{2,1,0:T(8,128)(2,1)S(1)} %collective-permute-done.1.rest_2_), channel_id=1, source_target_pairs={{0,224},{224,0},{32,128},{128,32},{64,160},{160,64},{96,192},{192,... | collective-permute-start | bytes 786440 | tf_op jit(solution)/shard_map/ppermute | solution.py:49
  31.9 12.8 %collective-permute-start.6 = (bf16[4,32,1024]{2,1,0:T(8,128)(2,1)S(1)}, bf16[4,32,1024]{2,1,0:T(8,128)(2,1)S(1)}, u32[]{:S(2)}, u32[]{:S(2)}) collective-permute-start(bf16[4,32,1024]{2,1,0:T(8,128)(2,1)S(1)} %collective-permute-done.2.rest_3_), channel_id=1, source_target_pairs={{0,128},{128,0},{32,160},{160,32},{64,192},{192,64},{96,224},{224,... | collective-permute-start | bytes 786440 | tf_op jit(solution)/shard_map/ppermute | solution.py:49
  32.7 12.1 %collective-permute-start.10 = (bf16[4,32,1024]{2,1,0:T(8,128)(2,1)S(1)}, bf16[4,32,1024]{2,1,0:T(8,128)(2,1)S(1)}, u32[]{:S(2)}, u32[]{:S(2)}) collective-permute-start(bf16[4,32,1024]{2,1,0:T(8,128)(2,1)S(1)} %collective-permute-done.2.rest_3_), channel_id=1, source_target_pairs={{0,4},{4,0},{1,5},{5,1},{2,6},{6,2},{3,7},{7,3},{8,12},{12,8},{9,1... | collective-permute-start | bytes 786440 | tf_op jit(solution)/shard_map/ppermute | solution.py:41
  37.5 7.8 %collective-permute-start.8 = (bf16[4,32,1024]{2,1,0:T(8,128)(2,1)S(1)}, bf16[4,32,1024]{2,1,0:T(8,128)(2,1)S(1)}, u32[]{:S(2)}, u32[]{:S(2)}) collective-permute-start(bf16[4,32,1024]{2,1,0:T(8,128)(2,1)S(1)} %collective-permute-done.rest_1_), channel_id=1, source_target_pairs={{0,4},{4,0},{1,5},{5,1},{2,6},{6,2},{3,7},{7,3},{8,12},{12,8},{9,1... | collective-permute-start | bytes 786440 | tf_op jit(solution)/shard_map/ppermute | solution.py:41
  37.6 7.8 %collective-permute-start.9 = (bf16[4,32,1024]{2,1,0:T(8,128)(2,1)S(1)}, bf16[4,32,1024]{2,1,0:T(8,128)(2,1)S(1)}, u32[]{:S(2)}, u32[]{:S(2)}) collective-permute-start(bf16[4,32,1024]{2,1,0:T(8,128)(2,1)S(1)} %collective-permute-done.1.rest_2_), channel_id=1, source_target_pairs={{0,4},{4,0},{1,5},{5,1},{2,6},{6,2},{3,7},{7,3},{8,12},{12,8},{9,1... | collective-permute-start | bytes 786440 | tf_op jit(solution)/shard_map/ppermute | solution.py:41
  41.9 4.0 %collective-permute-start.11 = (bf16[4,32,1024]{2,1,0:T(8,128)(2,1)S(1)}, bf16[4,32,1024]{2,1,0:T(8,128)(2,1)S(1)}, u32[]{:S(2)}, u32[]{:S(2)}) collective-permute-start(bf16[4,32,1024]{2,1,0:T(8,128)(2,1)S(1)} %collective-permute-done.3.rest_4_), channel_id=1, source_target_pairs={{0,4},{4,0},{1,5},{5,1},{2,6},{6,2},{3,7},{7,3},{8,12},{12,8},{9,1... | collective-permute-start | bytes 786440 | tf_op jit(solution)/shard_map/ppermute | solution.py:41
  44.8 1.5 %collective-permute-start.12 = (bf16[4,32,1024]{2,1,0:T(8,128)(2,1)S(1)}, bf16[4,32,1024]{2,1,0:T(8,128)(2,1)S(1)}, u32[]{:S(2)}, u32[]{:S(2)}) collective-permute-start(bf16[4,32,1024]{2,1,0:T(8,128)(2,1)S(1)} %collective-permute-done.4.rest_5_), channel_id=1, source_target_pairs={{0,4},{4,0},{1,5},{5,1},{2,6},{6,2},{3,7},{7,3},{8,12},{12,8},{9,1... | collective-permute-start | bytes 786440 | tf_op jit(solution)/shard_map/ppermute | solution.py:41
  44.8 1.9 %collective-permute-start.13 = (bf16[4,32,1024]{2,1,0:T(8,128)(2,1)S(1)}, bf16[4,32,1024]{2,1,0:T(8,128)(2,1)S(1)}, u32[]{:S(2)}, u32[]{:S(2)}) collective-permute-start(bf16[4,32,1024]{2,1,0:T(8,128)(2,1)S(1)} %collective-permute-done.5.rest_6_), channel_id=1, source_target_pairs={{0,4},{4,0},{1,5},{5,1},{2,6},{6,2},{3,7},{7,3},{8,12},{12,8},{9,1... | collective-permute-start | bytes 786440 | tf_op jit(solution)/shard_map/ppermute | solution.py:41
  45.3 1.8 %collective-permute-start.14 = (bf16[4,32,1024]{2,1,0:T(8,128)(2,1)S(1)}, bf16[4,32,1024]{2,1,0:T(8,128)(2,1)S(1)}, u32[]{:S(2)}, u32[]{:S(2)}) collective-permute-start(bf16[4,32,1024]{2,1,0:T(8,128)(2,1)S(1)} %collective-permute-done.6.rest_7_), channel_id=1, source_target_pairs={{0,4},{4,0},{1,5},{5,1},{2,6},{6,2},{3,7},{7,3},{8,12},{12,8},{9,1... | collective-permute-start | bytes 786440 | tf_op jit(solution)/shard_map/ppermute | solution.py:41
  47.0 12.0 %copy-start.5 = (s32[8,32]{1,0:T(8,128)S(1)}, s32[8,32]{1,0:T(8,128)}, u32[]{:S(2)}) copy-start(s32[8,32]{1,0:T(8,128)} %negs) | copy-start | bytes 3076
  47.0 12.0 %copy-start.8 = (s32[8]{0:T(128)S(1)}, s32[8]{0:T(128)}, u32[]{:S(2)}) copy-start(s32[8]{0:T(128)} %param.21) | copy-start | bytes 100
  50.2 8.8 %collective-permute-start.15 = (bf16[128,1024]{1,0:T(8,128)(2,1)S(1)}, bf16[128,1024]{1,0:T(8,128)(2,1)S(1)}, u32[]{:S(2)}, u32[]{:S(2)}) collective-permute-start(bf16[128,1024]{1,0:T(8,128)(2,1)S(1)} %get-tuple-element.40), channel_id=1, source_target_pairs={{0,1},{1,2},{2,3},{3,0},{4,5},{5,6},{6,7},{7,4},{8,9},{9,10},{10,1... | collective-permute-start | bytes 786440 | tf_op jit(solution)/shard_map/ppermute | solution.py:41
  51.5 8.5 %collective-permute-start.16 = (bf16[128,1024]{1,0:T(8,128)(2,1)S(1)}, bf16[128,1024]{1,0:T(8,128)(2,1)S(1)}, u32[]{:S(2)}, u32[]{:S(2)}) collective-permute-start(bf16[128,1024]{1,0:T(8,128)(2,1)S(1)} %get-tuple-element.42), channel_id=1, source_target_pairs={{0,3},{1,0},{2,1},{3,2},{4,7},{5,4},{6,5},{7,6},{8,11},{9,8},{10,9... | collective-permute-start | bytes 786440 | tf_op jit(solution)/shard_map/ppermute | solution.py:41
  53.0 12.6 %collective-permute-start.17 = (bf16[128,1024]{1,0:T(8,128)(2,1)S(1)}, bf16[128,1024]{1,0:T(8,128)(2,1)S(1)}, u32[]{:S(2)}, u32[]{:S(2)}) collective-permute-start(bf16[128,1024]{1,0:T(8,128)(2,1)S(1)} %get-tuple-element.43), channel_id=1, source_target_pairs={{0,2},{1,3},{2,0},{3,1},{4,6},{5,7},{6,4},{7,5},{8,10},{9,11},{10,... | collective-permute-start | bytes 786440 | tf_op jit(solution)/shard_map/ppermute | solution.py:41
  66.1 4.7 %collective-permute-start.18 = (bf16[32,1152]{1,0:T(8,128)(2,1)S(1)}, bf16[32,1152]{1,0:T(8,128)(2,1)S(1)}, u32[]{:S(2)}, u32[]{:S(2)}) collective-permute-start(bf16[32,1152]{1,0:T(8,128)(2,1)S(1)} %get-tuple-element.55.mine), channel_id=1, source_target_pairs={{0,128},{32,160},{64,192},{96,224},{128,32},{160,64},{192,96},{224... | collective-permute-start | bytes 221192 | tf_op jit(solution)/shard_map/ppermute | solution.py:58
  66.2 8.9 %collective-permute-start.19 = (bf16[32,1152]{1,0:T(8,128)(2,1)S(1)}, bf16[32,1152]{1,0:T(8,128)(2,1)S(1)}, u32[]{:S(2)}, u32[]{:S(2)}) collective-permute-start(bf16[32,1152]{1,0:T(8,128)(2,1)S(1)} %get-tuple-element.55.mine), channel_id=1, source_target_pairs={{0,96},{32,0},{64,32},{96,64},{128,224},{160,128},{192,160},{224,1... | collective-permute-start | bytes 221192 | tf_op jit(solution)/shard_map/ppermute | solution.py:58
  68.2 7.1 %collective-permute-start.20 = (bf16[32,1152]{1,0:T(8,128)(2,1)S(1)}, bf16[32,1152]{1,0:T(8,128)(2,1)S(1)}, u32[]{:S(2)}, u32[]{:S(2)}) collective-permute-start(bf16[32,1152]{1,0:T(8,128)(2,1)S(1)} %get-tuple-element.55.mine), channel_id=1, source_target_pairs={{0,192},{32,224},{64,128},{96,160},{128,64},{160,96},{192,0},{224,... | collective-permute-start | bytes 221192 | tf_op jit(solution)/shard_map/ppermute | solution.py:58
  71.7 14.3 %all-to-all-start.1 = ((bf16[4,144,256]{2,1,0:T(8,128)(2,1)}), bf16[4,144,256]{2,1,0:T(8,128)(2,1)S(1)}, u32[]{:S(2)}, u32[]{:S(2)}) async-start(bf16[4,144,256]{2,1,0:T(8,128)(2,1)} %send.1), calls=%async_computation.1 | async-start | bytes 589824 | tf_op jit(solution)/shard_map/all_to_all | solution.py:456
  75.3 9.4 %collective-permute-start.23 = (bf16[64,1152]{1,0:T(8,128)(2,1)S(1)}, bf16[64,1152]{1,0:T(8,128)(2,1)S(1)}, u32[]{:S(2)}, u32[]{:S(2)}) collective-permute-start(bf16[64,1152]{1,0:T(8,128)(2,1)S(1)} %pad_maximum_fusion.rest_0_), channel_id=1, source_target_pairs={{0,8},{8,16},{16,24},{24,0},{1,9},{9,17},{17,25},{25,1},{2,10},{10... | collective-permute-start | bytes 442376 | tf_op jit(solution)/shard_map/ppermute | solution.py:41
  75.8 10.3 %collective-permute-start.22 = (bf16[64,1152]{1,0:T(8,128)(2,1)S(1)}, bf16[64,1152]{1,0:T(8,128)(2,1)S(1)}, u32[]{:S(2)}, u32[]{:S(2)}) collective-permute-start(bf16[64,1152]{1,0:T(8,128)(2,1)S(1)} %pad_maximum_fusion.rest_0_), channel_id=1, source_target_pairs={{0,16},{8,24},{16,0},{24,8},{1,17},{9,25},{17,1},{25,9},{2,18},{10... | collective-permute-start | bytes 442376 | tf_op jit(solution)/shard_map/ppermute | solution.py:41
  79.7 8.7 %collective-permute-start.21 = (bf16[64,1152]{1,0:T(8,128)(2,1)S(1)}, bf16[64,1152]{1,0:T(8,128)(2,1)S(1)}, u32[]{:S(2)}, u32[]{:S(2)}) collective-permute-start(bf16[64,1152]{1,0:T(8,128)(2,1)S(1)} %pad_maximum_fusion.rest_0_), channel_id=1, source_target_pairs={{0,24},{8,0},{16,8},{24,16},{1,25},{9,1},{17,9},{25,17},{2,26},{10... | collective-permute-start | bytes 442376 | tf_op jit(solution)/shard_map/ppermute | solution.py:41
  81.2 7.2 %collective-permute-start.24 = (bf16[64,1152]{1,0:T(8,128)(2,1)S(1)}, bf16[64,1152]{1,0:T(8,128)(2,1)S(1)}, u32[]{:S(2)}, u32[]{:S(2)}) collective-permute-start(bf16[64,1152]{1,0:T(8,128)(2,1)S(1)} %pad_maximum_fusion.rest_0_), channel_id=1, source_target_pairs={{0,4},{4,0},{1,5},{5,1},{2,6},{6,2},{3,7},{7,3},{8,12},{12,8},{9,1... | collective-permute-start | bytes 442376 | tf_op jit(solution)/shard_map/ppermute | solution.py:41
  84.7 3.8 %collective-permute-start.25 = (bf16[64,1152]{1,0:T(8,128)(2,1)S(1)}, bf16[64,1152]{1,0:T(8,128)(2,1)S(1)}, u32[]{:S(2)}, u32[]{:S(2)}) collective-permute-start(bf16[64,1152]{1,0:T(8,128)(2,1)S(1)} %collective-permute-done.23.rest_1_), channel_id=1, source_target_pairs={{0,4},{4,0},{1,5},{5,1},{2,6},{6,2},{3,7},{7,3},{8,12},{12,8},{9,1... | collective-permute-start | bytes 442376 | tf_op jit(solution)/shard_map/ppermute | solution.py:41
  86.1 2.6 %collective-permute-start.27 = (bf16[64,1152]{1,0:T(8,128)(2,1)S(1)}, bf16[64,1152]{1,0:T(8,128)(2,1)S(1)}, u32[]{:S(2)}, u32[]{:S(2)}) collective-permute-start(bf16[64,1152]{1,0:T(8,128)(2,1)S(1)} %collective-permute-done.22.rest_3_), channel_id=1, source_target_pairs={{0,4},{4,0},{1,5},{5,1},{2,6},{6,2},{3,7},{7,3},{8,12},{12,8},{9,1... | collective-permute-start | bytes 442376 | tf_op jit(solution)/shard_map/ppermute | solution.py:41
  88.4 1.4 %collective-permute-start.26 = (bf16[64,1152]{1,0:T(8,128)(2,1)S(1)}, bf16[64,1152]{1,0:T(8,128)(2,1)S(1)}, u32[]{:S(2)}, u32[]{:S(2)}) collective-permute-start(bf16[64,1152]{1,0:T(8,128)(2,1)S(1)} %collective-permute-done.21.rest_2_), channel_id=1, source_target_pairs={{0,4},{4,0},{1,5},{5,1},{2,6},{6,2},{3,7},{7,3},{8,12},{12,8},{9,1... | collective-permute-start | bytes 442376 | tf_op jit(solution)/shard_map/ppermute | solution.py:41
  (7 other events, 25.0 us)

commit v7 on v6

--- a/solution.py
+++ b/solution.py
@@ -195,7 +195,7 @@
     lists_ref[...] = jnp.dot(move, lists.astype(BF), preferred_element_type=F32).astype(BF)
 
 
-def norm_kernel(own, r1, r2, r3, vectors, live, count, lists, p_ref, coded_ref):
+def norm_kernel(own, r1, r2, r3, vectors, live, count, lists, p_ref, blocks):
     rows, width = own.shape
     summed = own[...] + r1[...].astype(F32) + r2[...].astype(F32) + r3[...].astype(F32)
     summed = summed + vectors[0:1, :]
@@ -219,12 +219,16 @@
     refresh = at("grp") == 1
     p_ref[:, :width] = jnp.where(refresh, p, q)
     p_ref[:, width:] = jnp.where(refresh, tail.astype(BF), lists[...])
-    coded_ref[...] = coded
-
-
-def send_kernel(coded, mine, came, send):
-    rows, width = coded.shape
     part = width // N_MP
+    for j in range(N_MP):
+        blocks[j, :rows, :] = coded[:, j * part : (j + 1) * part]
+        blocks[j, rows:, :] = jnp.zeros((16, part), BF)
+
+
+def send_kernel(blocks, mine, came, send, held, sems):
+    part = held.shape[1]
+    rows = send.shape[1] - 16
+    width = part * N_MP
     n_q = rows // QLEN
     rider = jnp.where(at("grp") == 1, came[0:16, :], mine[0:16, :])
     parts = [rider[:, j * part : (j + 1) * part] for j in range(N_MP)]
@@ -233,10 +237,14 @@
     shape = (16, 16 * (N_MP + 1))
     to, come = iota(shape, 0), iota(shape, 1)
     move = onehot((to == come // 16 * n_q + come % 16) & (come % 16 < n_q))
-    block = jnp.dot(move, stacked, preferred_element_type=F32).astype(BF)
-    for j in range(N_MP):
-        send[j, :rows, :] = coded[:, j * part : (j + 1) * part]
-        send[j, rows:, :] = block
+    held[...] = jnp.dot(move, stacked, preferred_element_type=F32).astype(BF)
+    copies = [
+        pltpu.make_async_copy(held, send.at[j, rows : rows + 16], sems.at[j]) for j in range(N_MP)
+    ]
+    for copy in copies:
+        copy.start()
+    for copy in copies:
+        copy.wait()
 
 
 def query_kernel(arrived, q_ref, lists):
@@ -424,11 +432,11 @@
         name="prep",
     )(*small)
 
-    passages, coded = pl.pallas_call(
+    passages, blocks = pl.pallas_call(
         norm_kernel,
         out_shape=[
             shape((n_pass, width + 128), BF),
-            shape((part_rows, width), BF),
+            shape((N_MP, part_rows + 16, part), BF),
         ],
         in_specs=[VMEM] * 8,
         out_specs=[VMEM] * 2,
@@ -447,12 +455,14 @@
     lines = [slab] + [shift(slab, "y", k) for k in Y_ORDER]
     send = pl.pallas_call(
         send_kernel,
-        out_shape=shape((N_MP, part_rows + 16, part), BF),
-        in_specs=[VMEM] * 3,
-        out_specs=VMEM,
+        out_shape=shape(blocks.shape, BF),
+        in_specs=[ANY, VMEM, VMEM],
+        out_specs=ANY,
+        scratch_shapes=[pltpu.VMEM((16, part), BF), pltpu.SemaphoreType.DMA((N_MP,))],
+        input_output_aliases={0: 0},
         compiler_params=params(),
         name="send",
-    )(coded, passages, near)
+    )(blocks, passages, near)
     arrived = lax.all_to_all(send, "mp", 0, 0, tiled=True)
     q_all, lists = pl.pallas_call(
         query_kernel,

time: 102 us -> 102 us (level)
  no operation moved by 1% of the time
where the time goes in v7:
time: 102 us
  starting transfers between devices  59.2 us (58%)
  waiting for transfers between devices  20.3 us (20%)
  blocking collectives  10.2 us (10%)
  Pallas kernels  9.56 us (9%)
  local copies, waits for them, and re-layouts  1.91 us (2%)
    ppermute x21, starting transfers between devices, shift(): lax.ppermute(block, axis, [(i, (i + distance) % n) for i in range(n)])  38 us
    ppermute x21, waiting for transfers between devices, shift(): lax.ppermute(block, axis, [(i, (i + distance) % n) for i in range(n)])  13.2 us
    all_to_all x1, blocking collectives, body(): arrived = lax.all_to_all(shares, ('grp', 'mp'), 0, 0, tiled=True)  10.2 us
    all_to_all x1, starting transfers between devices, body(): lines = [lax.all_to_all(packed, 'zh', 0, 0, tiled=True)]  9.02 us
    all_to_all x1, waiting for transfers between devices, body(): lines = [lax.all_to_all(packed, 'zh', 0, 0, tiled=True)]  6.84 us
    ppermute x3, starting transfers between devices, reroute(): return lax.ppermute(block, ('grp', 'zh'), route)  4.52 us
    ppermute x4, starting transfers between devices, cross(): return lax.ppermute(block, ('grp', 'zh'), route)  4.19 us
    all_to_all x1, starting transfers between devices, body(): arrived = lax.all_to_all(send, 'mp', 0, 0, tiled=True)  3.46 us
  transfers between devices with their start and end apart: 30, of which 10 were waited for; matrix products, arithmetic and copies ran while one was open for 0% of the time, Pallas kernels for 1%

profile of v7, /device:TPU:1, one launch (start us, length us, event | category | flops | bytes accessed | tf_op | source)
XLA Modules:
  0.0 101.9 jit_solution(6370458989804846292)
XLA Ops:
  0.6 1.8 %pack.1 = bf16[4,32,1024]{2,1,0:T(8,128)(2,1)} custom-call(bf16[16,1024]{1,0:T(8,128)(2,1)} %w_in.1, bf16[16,1024]{1,0:T(8,128)(2,1)} %bitcast.20), custom_call_target="tpu_custom_call" | custom-call | tf_op jit(solution)/shard_map/pack/pallas_call | solution.py:365
  2.5 9.0 %all-to-all-start = ((bf16[4,32,1024]{2,1,0:T(8,128)(2,1)}), bf16[4,32,1024]{2,1,0:T(8,128)(2,1)S(1)}, u32[]{:S(2)}, u32[]{:S(2)}) async-start(bf16[4,32,1024]{2,1,0:T(8,128)(2,1)} %pack.1), calls=%async_computation | async-start | bytes 524288 | tf_op jit(solution)/shard_map/all_to_all | solution.py:377
  11.5 1.2 %copy-done = bf16[1,512,1024]{2,1,0:T(8,128)(2,1)S(1)} copy-done((bf16[1,512,1024]{2,1,0:T(8,128)(2,1)S(1)}, bf16[1,512,1024]{2,1,0:T(8,128)(2,1)}, u32[]{:S(2)}) %copy-start) | copy-done | bytes 1048600
  12.8 6.8 %all-to-all-done.rest_0_ = bf16[4,32,1024]{2,1,0:T(8,128)(2,1)S(1)} async-done(((bf16[4,32,1024]{2,1,0:T(8,128)(2,1)}), bf16[4,32,1024]{2,1,0:T(8,128)(2,1)S(1)}, u32[]{:S(2)}, u32[]{:S(2)}) %all-to-all-start) | async-done | bytes 262176 | tf_op jit(solution)/shard_map/all_to_all | solution.py:377
  19.7 1.3 %collective-permute-start = (bf16[4,32,1024]{2,1,0:T(8,128)(2,1)S(1)}, bf16[4,32,1024]{2,1,0:T(8,128)(2,1)S(1)}, u32[]{:S(2)}, u32[]{:S(2)}) collective-permute-start(bf16[4,32,1024]{2,1,0:T(8,128)(2,1)S(1)} %all-to-all-done.rest_0_), channel_id=1, source_target_pairs={{0,8},{8,16},{16,24},{24,0},{1,9},{9,17},{17,25},{25,1},{2,10},{10... | collective-permute-start | bytes 786440 | tf_op jit(solution)/shard_map/ppermute | solution.py:41
  21.0 1.4 %collective-permute-start.1 = (bf16[4,32,1024]{2,1,0:T(8,128)(2,1)S(1)}, bf16[4,32,1024]{2,1,0:T(8,128)(2,1)S(1)}, u32[]{:S(2)}, u32[]{:S(2)}) collective-permute-start(bf16[4,32,1024]{2,1,0:T(8,128)(2,1)S(1)} %all-to-all-done.rest_0_), channel_id=1, source_target_pairs={{0,24},{8,0},{16,8},{24,16},{1,25},{9,1},{17,9},{25,17},{2,26},{10... | collective-permute-start | bytes 786440 | tf_op jit(solution)/shard_map/ppermute | solution.py:41
  22.4 1.6 %collective-permute-start.2 = (bf16[4,32,1024]{2,1,0:T(8,128)(2,1)S(1)}, bf16[4,32,1024]{2,1,0:T(8,128)(2,1)S(1)}, u32[]{:S(2)}, u32[]{:S(2)}) collective-permute-start(bf16[4,32,1024]{2,1,0:T(8,128)(2,1)S(1)} %all-to-all-done.rest_0_), channel_id=1, source_target_pairs={{0,16},{8,24},{16,0},{24,8},{1,17},{9,25},{17,1},{25,9},{2,18},{10... | collective-permute-start | bytes 786440 | tf_op jit(solution)/shard_map/ppermute | solution.py:41
  24.8 4.4 %collective-permute-start.7 = (bf16[4,32,1024]{2,1,0:T(8,128)(2,1)S(1)}, bf16[4,32,1024]{2,1,0:T(8,128)(2,1)S(1)}, u32[]{:S(2)}, u32[]{:S(2)}) collective-permute-start(bf16[4,32,1024]{2,1,0:T(8,128)(2,1)S(1)} %all-to-all-done.rest_0_), channel_id=1, source_target_pairs={{0,4},{4,0},{1,5},{5,1},{2,6},{6,2},{3,7},{7,3},{8,12},{12,8},{9,1... | collective-permute-start | bytes 786440 | tf_op jit(solution)/shard_map/ppermute | solution.py:41
  30.0 1.9 %collective-permute-start.5 = (bf16[4,32,1024]{2,1,0:T(8,128)(2,1)S(1)}, bf16[4,32,1024]{2,1,0:T(8,128)(2,1)S(1)}, u32[]{:S(2)}, u32[]{:S(2)}) collective-permute-start(bf16[4,32,1024]{2,1,0:T(8,128)(2,1)S(1)} %collective-permute-done.1.rest_2_), channel_id=1, source_target_pairs={{0,224},{224,0},{32,128},{128,32},{64,160},{160,64},{96,192},{192,... | collective-permute-start | bytes 786440 | tf_op jit(solution)/shard_map/ppermute | solution.py:49
  31.9 0.8 collective-permute-start.6
  32.7 4.8 %collective-permute-start.10 = (bf16[4,32,1024]{2,1,0:T(8,128)(2,1)S(1)}, bf16[4,32,1024]{2,1,0:T(8,128)(2,1)S(1)}, u32[]{:S(2)}, u32[]{:S(2)}) collective-permute-start(bf16[4,32,1024]{2,1,0:T(8,128)(2,1)S(1)} %collective-permute-done.2.rest_3_), channel_id=1, source_target_pairs={{0,4},{4,0},{1,5},{5,1},{2,6},{6,2},{3,7},{7,3},{8,12},{12,8},{9,1... | collective-permute-start | bytes 786440 | tf_op jit(solution)/shard_map/ppermute | solution.py:41
  37.6 4.3 %collective-permute-start.9 = (bf16[4,32,1024]{2,1,0:T(8,128)(2,1)S(1)}, bf16[4,32,1024]{2,1,0:T(8,128)(2,1)S(1)}, u32[]{:S(2)}, u32[]{:S(2)}) collective-permute-start(bf16[4,32,1024]{2,1,0:T(8,128)(2,1)S(1)} %collective-permute-done.1.rest_2_), channel_id=1, source_target_pairs={{0,4},{4,0},{1,5},{5,1},{2,6},{6,2},{3,7},{7,3},{8,12},{12,8},{9,1... | collective-permute-start | bytes 786440 | tf_op jit(solution)/shard_map/ppermute | solution.py:41
  41.9 2.8 %collective-permute-start.11 = (bf16[4,32,1024]{2,1,0:T(8,128)(2,1)S(1)}, bf16[4,32,1024]{2,1,0:T(8,128)(2,1)S(1)}, u32[]{:S(2)}, u32[]{:S(2)}) collective-permute-start(bf16[4,32,1024]{2,1,0:T(8,128)(2,1)S(1)} %collective-permute-done.3.rest_4_), channel_id=1, source_target_pairs={{0,4},{4,0},{1,5},{5,1},{2,6},{6,2},{3,7},{7,3},{8,12},{12,8},{9,1... | collective-permute-start | bytes 786440 | tf_op jit(solution)/shard_map/ppermute | solution.py:41
  47.0 3.1 %ffn.1 = (f32[128,1024]{1,0:T(8,128)S(1)}, bf16[128,1024]{1,0:T(8,128)(2,1)S(1)}, bf16[128,1024]{1,0:T(8,128)(2,1)S(1)}, bf16[128,1024]{1,0:T(8,128)(2,1)S(1)}) custom-call(bf16[512,1024]{1,0:T(8,128)(2,1)S(1)} %get-tuple-element.36.x_ref, f32[1,1024]{1,0:T(1,128)S(1)} %get-tuple-element.37.b_ref, bf16[4,32,1024]{2,1,0:T(8,128)(2,1)S(1)} %all-to-all-done.rest_0_, ...), custom_call_target="tpu_custom_call" | custom-call | flops 2147483648 | bytes 8388608 | tf_op jit(solution)/shard_map/ffn/pallas_call | solution.py:395
  50.2 1.3 %collective-permute-start.15 = (bf16[128,1024]{1,0:T(8,128)(2,1)S(1)}, bf16[128,1024]{1,0:T(8,128)(2,1)S(1)}, u32[]{:S(2)}, u32[]{:S(2)}) collective-permute-start(bf16[128,1024]{1,0:T(8,128)(2,1)S(1)} %get-tuple-element.40), channel_id=1, source_target_pairs={{0,1},{1,2},{2,3},{3,0},{4,5},{5,6},{6,7},{7,4},{8,9},{9,10},{10,1... | collective-permute-start | bytes 786440 | tf_op jit(solution)/shard_map/ppermute | solution.py:41
  51.5 1.5 %collective-permute-start.16 = (bf16[128,1024]{1,0:T(8,128)(2,1)S(1)}, bf16[128,1024]{1,0:T(8,128)(2,1)S(1)}, u32[]{:S(2)}, u32[]{:S(2)}) collective-permute-start(bf16[128,1024]{1,0:T(8,128)(2,1)S(1)} %get-tuple-element.42), channel_id=1, source_target_pairs={{0,3},{1,0},{2,1},{3,2},{4,7},{5,4},{6,5},{7,6},{8,11},{9,8},{10,9... | collective-permute-start | bytes 786440 | tf_op jit(solution)/shard_map/ppermute | solution.py:41
  53.0 1.5 %collective-permute-start.17 = (bf16[128,1024]{1,0:T(8,128)(2,1)S(1)}, bf16[128,1024]{1,0:T(8,128)(2,1)S(1)}, u32[]{:S(2)}, u32[]{:S(2)}) collective-permute-start(bf16[128,1024]{1,0:T(8,128)(2,1)S(1)} %get-tuple-element.43), channel_id=1, source_target_pairs={{0,2},{1,3},{2,0},{3,1},{4,6},{5,7},{6,4},{7,5},{8,10},{9,11},{10,... | collective-permute-start | bytes 786440 | tf_op jit(solution)/shard_map/ppermute | solution.py:41
  54.5 4.5 %collective-permute-done.15.r1 = bf16[128,1024]{1,0:T(8,128)(2,1)S(1)} collective-permute-done((bf16[128,1024]{1,0:T(8,128)(2,1)S(1)}, bf16[128,1024]{1,0:T(8,128)(2,1)S(1)}, u32[]{:S(2)}, u32[]{:S(2)}) %collective-permute-start.15) | collective-permute-done | bytes 262176 | tf_op jit(solution)/shard_map/ppermute | solution.py:41
  59.9 5.6 %collective-permute-done.17.r3 = bf16[128,1024]{1,0:T(8,128)(2,1)S(1)} collective-permute-done((bf16[128,1024]{1,0:T(8,128)(2,1)S(1)}, bf16[128,1024]{1,0:T(8,128)(2,1)S(1)}, u32[]{:S(2)}, u32[]{:S(2)}) %collective-permute-start.17) | collective-permute-done | bytes 262176 | tf_op jit(solution)/shard_map/ppermute | solution.py:41
  65.6 1.0 %norm.1 = (bf16[32,1152]{1,0:T(8,128)(2,1)S(1)}, bf16[4,144,256]{2,1,0:T(8,128)(2,1)}) custom-call(f32[128,1024]{1,0:T(8,128)S(1)} %get-tuple-element.39.own, bf16[128,1024]{1,0:T(8,128)(2,1)S(1)} %collective-permute-done.15.r1, bf16[128,1024]{1,0:T(8,128)(2,1)S(1)} %collective-permute-done.16.r2, bf16[128,1024]{1,0:T(8,128)(2,1)S(1)} %collective-permute-done.17.r3, ...), custom_call_target="tpu_custom_call" | custom-call | flops 16777216 | bytes 3145728 | tf_op jit(solution)/shard_map/norm/pallas_call | solution.py:435
  66.6 1.9 %collective-permute-start.19 = (bf16[32,1152]{1,0:T(8,128)(2,1)S(1)}, bf16[32,1152]{1,0:T(8,128)(2,1)S(1)}, u32[]{:S(2)}, u32[]{:S(2)}) collective-permute-start(bf16[32,1152]{1,0:T(8,128)(2,1)S(1)} %get-tuple-element.55.mine), channel_id=1, source_target_pairs={{0,96},{32,0},{64,32},{96,64},{128,224},{160,128},{192,160},{224,1... | collective-permute-start | bytes 221192 | tf_op jit(solution)/shard_map/ppermute | solution.py:58
  68.6 2.6 %collective-permute-start.20 = (bf16[32,1152]{1,0:T(8,128)(2,1)S(1)}, bf16[32,1152]{1,0:T(8,128)(2,1)S(1)}, u32[]{:S(2)}, u32[]{:S(2)}) collective-permute-start(bf16[32,1152]{1,0:T(8,128)(2,1)S(1)} %get-tuple-element.55.mine), channel_id=1, source_target_pairs={{0,192},{32,224},{64,128},{96,160},{128,64},{160,96},{192,0},{224,... | collective-permute-start | bytes 221192 | tf_op jit(solution)/shard_map/ppermute | solution.py:58
  71.1 0.8 send.1
  71.9 3.5 %all-to-all-start.1 = ((bf16[4,144,256]{2,1,0:T(8,128)(2,1)}), bf16[4,144,256]{2,1,0:T(8,128)(2,1)S(1)}, u32[]{:S(2)}, u32[]{:S(2)}) async-start(bf16[4,144,256]{2,1,0:T(8,128)(2,1)} %send.1), calls=%async_computation.1 | async-start | bytes 589824 | tf_op jit(solution)/shard_map/all_to_all | solution.py:466
  76.2 3.9 %collective-permute-start.22 = (bf16[64,1152]{1,0:T(8,128)(2,1)S(1)}, bf16[64,1152]{1,0:T(8,128)(2,1)S(1)}, u32[]{:S(2)}, u32[]{:S(2)}) collective-permute-start(bf16[64,1152]{1,0:T(8,128)(2,1)S(1)} %pad_maximum_fusion.rest_0_), channel_id=1, source_target_pairs={{0,16},{8,24},{16,0},{24,8},{1,17},{9,25},{17,1},{25,9},{2,18},{10... | collective-permute-start | bytes 442376 | tf_op jit(solution)/shard_map/ppermute | solution.py:41
  80.1 1.5 %collective-permute-start.21 = (bf16[64,1152]{1,0:T(8,128)(2,1)S(1)}, bf16[64,1152]{1,0:T(8,128)(2,1)S(1)}, u32[]{:S(2)}, u32[]{:S(2)}) collective-permute-start(bf16[64,1152]{1,0:T(8,128)(2,1)S(1)} %pad_maximum_fusion.rest_0_), channel_id=1, source_target_pairs={{0,24},{8,0},{16,8},{24,16},{1,25},{9,1},{17,9},{25,17},{2,26},{10... | collective-permute-start | bytes 442376 | tf_op jit(solution)/shard_map/ppermute | solution.py:41
  81.6 3.4 %collective-permute-start.24 = (bf16[64,1152]{1,0:T(8,128)(2,1)S(1)}, bf16[64,1152]{1,0:T(8,128)(2,1)S(1)}, u32[]{:S(2)}, u32[]{:S(2)}) collective-permute-start(bf16[64,1152]{1,0:T(8,128)(2,1)S(1)} %pad_maximum_fusion.rest_0_), channel_id=1, source_target_pairs={{0,4},{4,0},{1,5},{5,1},{2,6},{6,2},{3,7},{7,3},{8,12},{12,8},{9,1... | collective-permute-start | bytes 442376 | tf_op jit(solution)/shard_map/ppermute | solution.py:41
  85.0 1.2 %collective-permute-start.25 = (bf16[64,1152]{1,0:T(8,128)(2,1)S(1)}, bf16[64,1152]{1,0:T(8,128)(2,1)S(1)}, u32[]{:S(2)}, u32[]{:S(2)}) collective-permute-start(bf16[64,1152]{1,0:T(8,128)(2,1)S(1)} %collective-permute-done.23.rest_1_), channel_id=1, source_target_pairs={{0,4},{4,0},{1,5},{5,1},{2,6},{6,2},{3,7},{7,3},{8,12},{12,8},{9,1... | collective-permute-start | bytes 442376 | tf_op jit(solution)/shard_map/ppermute | solution.py:41
  86.4 1.7 %collective-permute-start.27 = (bf16[64,1152]{1,0:T(8,128)(2,1)S(1)}, bf16[64,1152]{1,0:T(8,128)(2,1)S(1)}, u32[]{:S(2)}, u32[]{:S(2)}) collective-permute-start(bf16[64,1152]{1,0:T(8,128)(2,1)S(1)} %collective-permute-done.22.rest_3_), channel_id=1, source_target_pairs={{0,4},{4,0},{1,5},{5,1},{2,6},{6,2},{3,7},{7,3},{8,12},{12,8},{9,1... | collective-permute-start | bytes 442376 | tf_op jit(solution)/shard_map/ppermute | solution.py:41
  89.1 1.1 %collective-permute-done.26.rest_6_ = bf16[64,1152]{1,0:T(8,128)(2,1)S(1)} collective-permute-done((bf16[64,1152]{1,0:T(8,128)(2,1)S(1)}, bf16[64,1152]{1,0:T(8,128)(2,1)S(1)}, u32[]{:S(2)}, u32[]{:S(2)}) %collective-permute-start.26) | collective-permute-done | bytes 147488 | tf_op jit(solution)/shard_map/ppermute | solution.py:41
  90.2 0.8 score.1
  91.0 10.2 %all_to_all.15.arrived = f32[8,16,384]{2,1,0:T(8,128)S(1)} all-to-all(f32[8,16,384]{2,1,0:T(8,128)S(1)} %score.1), channel_id=1, replica_groups=mesh['grp'=2,'zh'=4,'y'=4,'c'=2,'mp'=4] {'grp','mp'}, dimensions={0} | all-to-all | bytes 393216 | tf_op jit(solution)/shard_map/all_to_all | solution.py:495
  (60 shorter events, 7.6 us)
Async XLA Ops:
  2.5 17.2 %all-to-all-start = ((bf16[4,32,1024]{2,1,0:T(8,128)(2,1)}), bf16[4,32,1024]{2,1,0:T(8,128)(2,1)S(1)}, u32[]{:S(2)}, u32[]{:S(2)}) async-start(bf16[4,32,1024]{2,1,0:T(8,128)(2,1)} %pack.1), calls=%async_computation | async-start | bytes 524288 | tf_op jit(solution)/shard_map/all_to_all | solution.py:377
  19.7 9.5 %collective-permute-start = (bf16[4,32,1024]{2,1,0:T(8,128)(2,1)S(1)}, bf16[4,32,1024]{2,1,0:T(8,128)(2,1)S(1)}, u32[]{:S(2)}, u32[]{:S(2)}) collective-permute-start(bf16[4,32,1024]{2,1,0:T(8,128)(2,1)S(1)} %all-to-all-done.rest_0_), channel_id=1, source_target_pairs={{0,8},{8,16},{16,24},{24,0},{1,9},{9,17},{17,25},{25,1},{2,10},{10... | collective-permute-start | bytes 786440 | tf_op jit(solution)/shard_map/ppermute | solution.py:41
  21.0 9.0 %collective-permute-start.1 = (bf16[4,32,1024]{2,1,0:T(8,128)(2,1)S(1)}, bf16[4,32,1024]{2,1,0:T(8,128)(2,1)S(1)}, u32[]{:S(2)}, u32[]{:S(2)}) collective-permute-start(bf16[4,32,1024]{2,1,0:T(8,128)(2,1)S(1)} %all-to-all-done.rest_0_), channel_id=1, source_target_pairs={{0,24},{8,0},{16,8},{24,16},{1,25},{9,1},{17,9},{25,17},{2,26},{10... | collective-permute-start | bytes 786440 | tf_op jit(solution)/shard_map/ppermute | solution.py:41
  22.4 9.5 %collective-permute-start.2 = (bf16[4,32,1024]{2,1,0:T(8,128)(2,1)S(1)}, bf16[4,32,1024]{2,1,0:T(8,128)(2,1)S(1)}, u32[]{:S(2)}, u32[]{:S(2)}) collective-permute-start(bf16[4,32,1024]{2,1,0:T(8,128)(2,1)S(1)} %all-to-all-done.rest_0_), channel_id=1, source_target_pairs={{0,16},{8,24},{16,0},{24,8},{1,17},{9,25},{17,1},{25,9},{2,18},{10... | collective-permute-start | bytes 786440 | tf_op jit(solution)/shard_map/ppermute | solution.py:41
  24.1 8.6 %collective-permute-start.3 = (bf16[4,32,1024]{2,1,0:T(8,128)(2,1)S(1)}, bf16[4,32,1024]{2,1,0:T(8,128)(2,1)S(1)}, u32[]{:S(2)}, u32[]{:S(2)}) collective-permute-start(bf16[4,32,1024]{2,1,0:T(8,128)(2,1)S(1)} %all-to-all-done.rest_0_), channel_id=1, source_target_pairs={{0,128},{128,0},{32,160},{160,32},{64,192},{192,64},{96,224},{224,... | collective-permute-start | bytes 786440 | tf_op jit(solution)/shard_map/ppermute | solution.py:49
  24.8 12.7 %collective-permute-start.7 = (bf16[4,32,1024]{2,1,0:T(8,128)(2,1)S(1)}, bf16[4,32,1024]{2,1,0:T(8,128)(2,1)S(1)}, u32[]{:S(2)}, u32[]{:S(2)}) collective-permute-start(bf16[4,32,1024]{2,1,0:T(8,128)(2,1)S(1)} %all-to-all-done.rest_0_), channel_id=1, source_target_pairs={{0,4},{4,0},{1,5},{5,1},{2,6},{6,2},{3,7},{7,3},{8,12},{12,8},{9,1... | collective-permute-start | bytes 786440 | tf_op jit(solution)/shard_map/ppermute | solution.py:41
  29.2 8.4 %collective-permute-start.4 = (bf16[4,32,1024]{2,1,0:T(8,128)(2,1)S(1)}, bf16[4,32,1024]{2,1,0:T(8,128)(2,1)S(1)}, u32[]{:S(2)}, u32[]{:S(2)}) collective-permute-start(bf16[4,32,1024]{2,1,0:T(8,128)(2,1)S(1)} %collective-permute-done.rest_1_), channel_id=1, source_target_pairs={{0,224},{224,0},{32,128},{128,32},{64,160},{160,64},{96,192},{192,... | collective-permute-start | bytes 786440 | tf_op jit(solution)/shard_map/ppermute | solution.py:49
  30.0 12.0 %collective-permute-start.5 = (bf16[4,32,1024]{2,1,0:T(8,128)(2,1)S(1)}, bf16[4,32,1024]{2,1,0:T(8,128)(2,1)S(1)}, u32[]{:S(2)}, u32[]{:S(2)}) collective-permute-start(bf16[4,32,1024]{2,1,0:T(8,128)(2,1)S(1)} %collective-permute-done.1.rest_2_), channel_id=1, source_target_pairs={{0,224},{224,0},{32,128},{128,32},{64,160},{160,64},{96,192},{192,... | collective-permute-start | bytes 786440 | tf_op jit(solution)/shard_map/ppermute | solution.py:49
  31.9 12.8 %collective-permute-start.6 = (bf16[4,32,1024]{2,1,0:T(8,128)(2,1)S(1)}, bf16[4,32,1024]{2,1,0:T(8,128)(2,1)S(1)}, u32[]{:S(2)}, u32[]{:S(2)}) collective-permute-start(bf16[4,32,1024]{2,1,0:T(8,128)(2,1)S(1)} %collective-permute-done.2.rest_3_), channel_id=1, source_target_pairs={{0,128},{128,0},{32,160},{160,32},{64,192},{192,64},{96,224},{224,... | collective-permute-start | bytes 786440 | tf_op jit(solution)/shard_map/ppermute | solution.py:49
  32.7 12.1 %collective-permute-start.10 = (bf16[4,32,1024]{2,1,0:T(8,128)(2,1)S(1)}, bf16[4,32,1024]{2,1,0:T(8,128)(2,1)S(1)}, u32[]{:S(2)}, u32[]{:S(2)}) collective-permute-start(bf16[4,32,1024]{2,1,0:T(8,128)(2,1)S(1)} %collective-permute-done.2.rest_3_), channel_id=1, source_target_pairs={{0,4},{4,0},{1,5},{5,1},{2,6},{6,2},{3,7},{7,3},{8,12},{12,8},{9,1... | collective-permute-start | bytes 786440 | tf_op jit(solution)/shard_map/ppermute | solution.py:41
  37.5 7.8 %collective-permute-start.8 = (bf16[4,32,1024]{2,1,0:T(8,128)(2,1)S(1)}, bf16[4,32,1024]{2,1,0:T(8,128)(2,1)S(1)}, u32[]{:S(2)}, u32[]{:S(2)}) collective-permute-start(bf16[4,32,1024]{2,1,0:T(8,128)(2,1)S(1)} %collective-permute-done.rest_1_), channel_id=1, source_target_pairs={{0,4},{4,0},{1,5},{5,1},{2,6},{6,2},{3,7},{7,3},{8,12},{12,8},{9,1... | collective-permute-start | bytes 786440 | tf_op jit(solution)/shard_map/ppermute | solution.py:41
  37.6 7.8 %collective-permute-start.9 = (bf16[4,32,1024]{2,1,0:T(8,128)(2,1)S(1)}, bf16[4,32,1024]{2,1,0:T(8,128)(2,1)S(1)}, u32[]{:S(2)}, u32[]{:S(2)}) collective-permute-start(bf16[4,32,1024]{2,1,0:T(8,128)(2,1)S(1)} %collective-permute-done.1.rest_2_), channel_id=1, source_target_pairs={{0,4},{4,0},{1,5},{5,1},{2,6},{6,2},{3,7},{7,3},{8,12},{12,8},{9,1... | collective-permute-start | bytes 786440 | tf_op jit(solution)/shard_map/ppermute | solution.py:41
  41.9 4.0 %collective-permute-start.11 = (bf16[4,32,1024]{2,1,0:T(8,128)(2,1)S(1)}, bf16[4,32,1024]{2,1,0:T(8,128)(2,1)S(1)}, u32[]{:S(2)}, u32[]{:S(2)}) collective-permute-start(bf16[4,32,1024]{2,1,0:T(8,128)(2,1)S(1)} %collective-permute-done.3.rest_4_), channel_id=1, source_target_pairs={{0,4},{4,0},{1,5},{5,1},{2,6},{6,2},{3,7},{7,3},{8,12},{12,8},{9,1... | collective-permute-start | bytes 786440 | tf_op jit(solution)/shard_map/ppermute | solution.py:41
  44.8 1.5 %collective-permute-start.12 = (bf16[4,32,1024]{2,1,0:T(8,128)(2,1)S(1)}, bf16[4,32,1024]{2,1,0:T(8,128)(2,1)S(1)}, u32[]{:S(2)}, u32[]{:S(2)}) collective-permute-start(bf16[4,32,1024]{2,1,0:T(8,128)(2,1)S(1)} %collective-permute-done.4.rest_5_), channel_id=1, source_target_pairs={{0,4},{4,0},{1,5},{5,1},{2,6},{6,2},{3,7},{7,3},{8,12},{12,8},{9,1... | collective-permute-start | bytes 786440 | tf_op jit(solution)/shard_map/ppermute | solution.py:41
  44.8 1.9 %collective-permute-start.13 = (bf16[4,32,1024]{2,1,0:T(8,128)(2,1)S(1)}, bf16[4,32,1024]{2,1,0:T(8,128)(2,1)S(1)}, u32[]{:S(2)}, u32[]{:S(2)}) collective-permute-start(bf16[4,32,1024]{2,1,0:T(8,128)(2,1)S(1)} %collective-permute-done.5.rest_6_), channel_id=1, source_target_pairs={{0,4},{4,0},{1,5},{5,1},{2,6},{6,2},{3,7},{7,3},{8,12},{12,8},{9,1... | collective-permute-start | bytes 786440 | tf_op jit(solution)/shard_map/ppermute | solution.py:41
  45.3 1.8 %collective-permute-start.14 = (bf16[4,32,1024]{2,1,0:T(8,128)(2,1)S(1)}, bf16[4,32,1024]{2,1,0:T(8,128)(2,1)S(1)}, u32[]{:S(2)}, u32[]{:S(2)}) collective-permute-start(bf16[4,32,1024]{2,1,0:T(8,128)(2,1)S(1)} %collective-permute-done.6.rest_7_), channel_id=1, source_target_pairs={{0,4},{4,0},{1,5},{5,1},{2,6},{6,2},{3,7},{7,3},{8,12},{12,8},{9,1... | collective-permute-start | bytes 786440 | tf_op jit(solution)/shard_map/ppermute | solution.py:41
  47.0 12.0 %copy-start.5 = (s32[8,32]{1,0:T(8,128)S(1)}, s32[8,32]{1,0:T(8,128)}, u32[]{:S(2)}) copy-start(s32[8,32]{1,0:T(8,128)} %negs) | copy-start | bytes 3076
  47.0 12.0 %copy-start.8 = (s32[8]{0:T(128)S(1)}, s32[8]{0:T(128)}, u32[]{:S(2)}) copy-start(s32[8]{0:T(128)} %param.21) | copy-start | bytes 100
  50.2 8.8 %collective-permute-start.15 = (bf16[128,1024]{1,0:T(8,128)(2,1)S(1)}, bf16[128,1024]{1,0:T(8,128)(2,1)S(1)}, u32[]{:S(2)}, u32[]{:S(2)}) collective-permute-start(bf16[128,1024]{1,0:T(8,128)(2,1)S(1)} %get-tuple-element.40), channel_id=1, source_target_pairs={{0,1},{1,2},{2,3},{3,0},{4,5},{5,6},{6,7},{7,4},{8,9},{9,10},{10,1... | collective-permute-start | bytes 786440 | tf_op jit(solution)/shard_map/ppermute | solution.py:41
  51.5 8.5 %collective-permute-start.16 = (bf16[128,1024]{1,0:T(8,128)(2,1)S(1)}, bf16[128,1024]{1,0:T(8,128)(2,1)S(1)}, u32[]{:S(2)}, u32[]{:S(2)}) collective-permute-start(bf16[128,1024]{1,0:T(8,128)(2,1)S(1)} %get-tuple-element.42), channel_id=1, source_target_pairs={{0,3},{1,0},{2,1},{3,2},{4,7},{5,4},{6,5},{7,6},{8,11},{9,8},{10,9... | collective-permute-start | bytes 786440 | tf_op jit(solution)/shard_map/ppermute | solution.py:41
  53.0 12.6 %collective-permute-start.17 = (bf16[128,1024]{1,0:T(8,128)(2,1)S(1)}, bf16[128,1024]{1,0:T(8,128)(2,1)S(1)}, u32[]{:S(2)}, u32[]{:S(2)}) collective-permute-start(bf16[128,1024]{1,0:T(8,128)(2,1)S(1)} %get-tuple-element.43), channel_id=1, source_target_pairs={{0,2},{1,3},{2,0},{3,1},{4,6},{5,7},{6,4},{7,5},{8,10},{9,11},{10,... | collective-permute-start | bytes 786440 | tf_op jit(solution)/shard_map/ppermute | solution.py:41
  66.6 4.5 %collective-permute-start.18 = (bf16[32,1152]{1,0:T(8,128)(2,1)S(1)}, bf16[32,1152]{1,0:T(8,128)(2,1)S(1)}, u32[]{:S(2)}, u32[]{:S(2)}) collective-permute-start(bf16[32,1152]{1,0:T(8,128)(2,1)S(1)} %get-tuple-element.55.mine), channel_id=1, source_target_pairs={{0,128},{32,160},{64,192},{96,224},{128,32},{160,64},{192,96},{224... | collective-permute-start | bytes 221192 | tf_op jit(solution)/shard_map/ppermute | solution.py:58
  66.6 8.8 %collective-permute-start.19 = (bf16[32,1152]{1,0:T(8,128)(2,1)S(1)}, bf16[32,1152]{1,0:T(8,128)(2,1)S(1)}, u32[]{:S(2)}, u32[]{:S(2)}) collective-permute-start(bf16[32,1152]{1,0:T(8,128)(2,1)S(1)} %get-tuple-element.55.mine), channel_id=1, source_target_pairs={{0,96},{32,0},{64,32},{96,64},{128,224},{160,128},{192,160},{224,1... | collective-permute-start | bytes 221192 | tf_op jit(solution)/shard_map/ppermute | solution.py:58
  68.6 7.1 %collective-permute-start.20 = (bf16[32,1152]{1,0:T(8,128)(2,1)S(1)}, bf16[32,1152]{1,0:T(8,128)(2,1)S(1)}, u32[]{:S(2)}, u32[]{:S(2)}) collective-permute-start(bf16[32,1152]{1,0:T(8,128)(2,1)S(1)} %get-tuple-element.55.mine), channel_id=1, source_target_pairs={{0,192},{32,224},{64,128},{96,160},{128,64},{160,96},{192,0},{224,... | collective-permute-start | bytes 221192 | tf_op jit(solution)/shard_map/ppermute | solution.py:58
  71.9 14.3 %all-to-all-start.1 = ((bf16[4,144,256]{2,1,0:T(8,128)(2,1)}), bf16[4,144,256]{2,1,0:T(8,128)(2,1)S(1)}, u32[]{:S(2)}, u32[]{:S(2)}) async-start(bf16[4,144,256]{2,1,0:T(8,128)(2,1)} %send.1), calls=%async_computation.1 | async-start | bytes 589824 | tf_op jit(solution)/shard_map/all_to_all | solution.py:466
  75.7 9.3 %collective-permute-start.23 = (bf16[64,1152]{1,0:T(8,128)(2,1)S(1)}, bf16[64,1152]{1,0:T(8,128)(2,1)S(1)}, u32[]{:S(2)}, u32[]{:S(2)}) collective-permute-start(bf16[64,1152]{1,0:T(8,128)(2,1)S(1)} %pad_maximum_fusion.rest_0_), channel_id=1, source_target_pairs={{0,8},{8,16},{16,24},{24,0},{1,9},{9,17},{17,25},{25,1},{2,10},{10... | collective-permute-start | bytes 442376 | tf_op jit(solution)/shard_map/ppermute | solution.py:41
  76.2 10.2 %collective-permute-start.22 = (bf16[64,1152]{1,0:T(8,128)(2,1)S(1)}, bf16[64,1152]{1,0:T(8,128)(2,1)S(1)}, u32[]{:S(2)}, u32[]{:S(2)}) collective-permute-start(bf16[64,1152]{1,0:T(8,128)(2,1)S(1)} %pad_maximum_fusion.rest_0_), channel_id=1, source_target_pairs={{0,16},{8,24},{16,0},{24,8},{1,17},{9,25},{17,1},{25,9},{2,18},{10... | collective-permute-start | bytes 442376 | tf_op jit(solution)/shard_map/ppermute | solution.py:41
  80.1 8.7 %collective-permute-start.21 = (bf16[64,1152]{1,0:T(8,128)(2,1)S(1)}, bf16[64,1152]{1,0:T(8,128)(2,1)S(1)}, u32[]{:S(2)}, u32[]{:S(2)}) collective-permute-start(bf16[64,1152]{1,0:T(8,128)(2,1)S(1)} %pad_maximum_fusion.rest_0_), channel_id=1, source_target_pairs={{0,24},{8,0},{16,8},{24,16},{1,25},{9,1},{17,9},{25,17},{2,26},{10... | collective-permute-start | bytes 442376 | tf_op jit(solution)/shard_map/ppermute | solution.py:41
  81.6 7.2 %collective-permute-start.24 = (bf16[64,1152]{1,0:T(8,128)(2,1)S(1)}, bf16[64,1152]{1,0:T(8,128)(2,1)S(1)}, u32[]{:S(2)}, u32[]{:S(2)}) collective-permute-start(bf16[64,1152]{1,0:T(8,128)(2,1)S(1)} %pad_maximum_fusion.rest_0_), channel_id=1, source_target_pairs={{0,4},{4,0},{1,5},{5,1},{2,6},{6,2},{3,7},{7,3},{8,12},{12,8},{9,1... | collective-permute-start | bytes 442376 | tf_op jit(solution)/shard_map/ppermute | solution.py:41
  85.0 3.8 %collective-permute-start.25 = (bf16[64,1152]{1,0:T(8,128)(2,1)S(1)}, bf16[64,1152]{1,0:T(8,128)(2,1)S(1)}, u32[]{:S(2)}, u32[]{:S(2)}) collective-permute-start(bf16[64,1152]{1,0:T(8,128)(2,1)S(1)} %collective-permute-done.23.rest_1_), channel_id=1, source_target_pairs={{0,4},{4,0},{1,5},{5,1},{2,6},{6,2},{3,7},{7,3},{8,12},{12,8},{9,1... | collective-permute-start | bytes 442376 | tf_op jit(solution)/shard_map/ppermute | solution.py:41
  86.4 2.7 %collective-permute-start.27 = (bf16[64,1152]{1,0:T(8,128)(2,1)S(1)}, bf16[64,1152]{1,0:T(8,128)(2,1)S(1)}, u32[]{:S(2)}, u32[]{:S(2)}) collective-permute-start(bf16[64,1152]{1,0:T(8,128)(2,1)S(1)} %collective-permute-done.22.rest_3_), channel_id=1, source_target_pairs={{0,4},{4,0},{1,5},{5,1},{2,6},{6,2},{3,7},{7,3},{8,12},{12,8},{9,1... | collective-permute-start | bytes 442376 | tf_op jit(solution)/shard_map/ppermute | solution.py:41
  88.8 1.4 %collective-permute-start.26 = (bf16[64,1152]{1,0:T(8,128)(2,1)S(1)}, bf16[64,1152]{1,0:T(8,128)(2,1)S(1)}, u32[]{:S(2)}, u32[]{:S(2)}) collective-permute-start(bf16[64,1152]{1,0:T(8,128)(2,1)S(1)} %collective-permute-done.21.rest_2_), channel_id=1, source_target_pairs={{0,4},{4,0},{1,5},{5,1},{2,6},{6,2},{3,7},{7,3},{8,12},{12,8},{9,1... | collective-permute-start | bytes 442376 | tf_op jit(solution)/shard_map/ppermute | solution.py:41
  (7 other events, 25.0 us)
